TPU v7x, 32 devices: a whole 2x2x4 slice. The times are simulated.
32 devices in a mesh: ctx: 8 (over y, x, core), tp: 4 (over z).
Axes of the slice: x: 2, y: 2, z: 4, core: 2. Of those that a mesh axis runs over, the one named last changes fastest.
Arguments:
- tokens_in: bfloat16 [4096, 2560], P('ctx'), may hold values from -1.5 to 1.5
- w_qa: bfloat16 [2560, 768], replicated, may hold values from -0.125 to 0.125
- w_kva: bfloat16 [2560, 288], replicated, may hold values from -0.125 to 0.125
- w_qb: bfloat16 [768, 3840], P(None, 'tp'), may hold values from -0.4375 to 0.4375
- w_kvb: bfloat16 [256, 5120], P(None, 'tp'), may hold values from -0.375 to 0.375
- w_out: bfloat16 [2560, 2560], P(None, 'tp'), may hold values from -1 to 1
- w_gate: bfloat16 [2560, 6400], P(None, 'tp'), may hold values from -0.125 to 0.125
- w_up: bfloat16 [2560, 6400], P(None, 'tp'), may hold values from -0.125 to 0.125
- w_down: bfloat16 [2560, 6400], P(None, 'tp'), may hold values from -0.15625 to 0.15625
- gain_in: float32 [2560], replicated, may hold values from 0.5 to 1.5
- gain_q: float32 [768], replicated, may hold values from 0.5 to 1.5
- gain_kv: float32 [256], replicated, may hold values from 0.5 to 1.5
- gain_mid: float32 [2560], replicated, may hold values from 0.5 to 1.5
- cotangent: bfloat16 [4096, 2560], P('ctx'), may hold values from -6 to 6
- block_map: int32 [8, 2], replicated, may hold values from 0 to 15, as said below
- doc_lengths: int32 [4], replicated, may hold values from 1 to 3072, as said below
Outputs:
- out: bfloat16 [4096, 2560], P('ctx')
- grad_in: float32 [4096, 2560], P('ctx')
- grad_w_qa: float32 [2560, 768], P('ctx')
- grad_w_kva: float32 [2560, 288], P('ctx')
- grad_w_qb: float32 [768, 3840], P('ctx', 'tp')
- grad_w_kvb: float32 [256, 5120], P('ctx', 'tp')
- grad_w_out: float32 [2560, 2560], P('ctx', 'tp')
- grad_w_gate: float32 [2560, 6400], P('ctx', 'tp')
- grad_w_up: float32 [2560, 6400], P('ctx', 'tp')
- grad_w_down: float32 [2560, 6400], P('ctx', 'tp')
- grad_gain_in: float32 [2560], P('ctx')
- grad_gain_q: float32 [768], P('ctx')
- grad_gain_kv: float32 [256], P('ctx')
- grad_gain_mid: float32 [2560], P('ctx')
Inputs may be any that keep to these rules, and one draw needn't show every extreme that they name: `block_map`: row c lists the two blocks of 256 context places whose tokens ctx index c holds, first the one in column 0, then the one in column 1. Column 0 holds each block of the first half of the context once, column 1 each block of the second half once. `doc_lengths`: the lengths sum to 4096. The first or the last sequence has 3072 tokens.
All inputs are finite; a program needn't handle non-finite values.
Results may differ from a plain program's by a relative error of at most 0.025.
Values may be sent and summed in bfloat16 or wider, within the bound.
A program may use at most 320 MiB of HBM per device.

v0:
```python
import math

import jax
import jax.numpy as jnp
from jax import lax
from jax.sharding import PartitionSpec as P

KVR = 256
NOPE = 64
ROPE = 32
VDIM = 64


EPSILON = 1e-05
ROPE_BASE = 10000.0
MASKED = -1e30
RESIDUAL_SCALE = 1.4 / math.sqrt(62.0)
HIGH = lax.Precision.HIGHEST


def dot_plain(left_op, right_op):
    return jnp.dot(left_op, right_op, preferred_element_type=jnp.float32)


def dot_rows(left_op, right_op):
    return lax.dot_general(
        left_op, right_op, (((0,), (0,)), ((), ())), preferred_element_type=jnp.float32
    )


def dot_cols(left_op, right_op):
    return lax.dot_general(
        left_op, right_op, (((1,), (1,)), ((), ())), preferred_element_type=jnp.float32
    )


def exact_rows(left_op, right_op):
    return lax.dot_general(
        left_op,
        right_op,
        (((0,), (0,)), ((), ())),
        precision=HIGH,
        preferred_element_type=jnp.float32,
    )


def exact_cols(left_op, right_op):
    return lax.dot_general(
        left_op,
        right_op,
        (((1,), (1,)), ((), ())),
        precision=HIGH,
        preferred_element_type=jnp.float32,
    )


def rms_scale(values):
    return lax.rsqrt(jnp.mean(values * values, axis=-1, keepdims=True) + EPSILON)


def rms_back(incoming, values, inv_rms, gain_vec):
    weighted = incoming * gain_vec
    d_values = inv_rms * weighted - values * inv_rms**3 * jnp.mean(
        weighted * values, axis=-1, keepdims=True
    )
    return (d_values, jnp.sum(incoming * values * inv_rms, axis=0))


def token_places(block_map, doc_lengths, per_device, devices):
    all_rows = per_device * devices
    half_block = per_device // 2
    token_rows = jnp.arange(all_rows, dtype=jnp.int32)
    device_of = token_rows // per_device
    within = token_rows % per_device
    wanted = device_of * 2 + within // half_block
    select = wanted[:, None] == jnp.arange(2 * devices, dtype=jnp.int32)[None, :]
    blocks = jnp.sum(jnp.where(select, block_map.reshape(-1)[None, :], 0), axis=1)
    places = blocks * half_block + within % half_block
    ends = jnp.cumsum(doc_lengths)
    segment = jnp.sum((places[:, None] >= ends[None, :]).astype(jnp.int32), axis=1)
    starts = ends - doc_lengths
    picked = segment[:, None] == jnp.arange(doc_lengths.shape[0], dtype=jnp.int32)[None, :]
    begins = jnp.sum(jnp.where(picked, starts[None, :], 0), axis=1)
    return (places, segment, places - begins)


def tables(inside):
    half_width = ROPE // 2
    frequency = ROPE_BASE ** (-2.0 * jnp.arange(half_width, dtype=jnp.float32) / ROPE)
    angles = inside.astype(jnp.float32)[:, None] * frequency[None, :]
    cosine_table = jnp.concatenate([jnp.cos(angles), jnp.cos(angles)], axis=1)
    sine_table = jnp.concatenate([jnp.sin(angles), jnp.sin(angles)], axis=1)
    return (cosine_table, sine_table)


def rotate(values, cosine_table, sine_table):
    half_width = values.shape[-1] // 2
    turned = jnp.concatenate([-values[..., half_width:], values[..., :half_width]], axis=-1)
    return values * cosine_table + turned * sine_table


def rotate_back(incoming, cosine_table, sine_table):
    half_width = incoming.shape[-1] // 2
    shifted = incoming * sine_table
    turned = jnp.concatenate([shifted[..., half_width:], -shifted[..., :half_width]], axis=-1)
    return incoming * cosine_table + turned


def on_device(
    tokens_in,
    w_qa,
    w_kva,
    w_qb,
    w_kvb,
    w_out,
    w_gate,
    w_up,
    w_down,
    gain_in,
    gain_q,
    gain_kv,
    gain_mid,
    cotangent,
    block_map,
    doc_lengths,
):
    local_rows = tokens_in.shape[0]
    devices = lax.axis_size("ctx")
    ctx_index = lax.axis_index("ctx")
    places, segment, inside = token_places(block_map, doc_lengths, local_rows, devices)
    own_first = ctx_index * local_rows
    query_place = lax.dynamic_slice_in_dim(places, own_first, local_rows, 0)
    query_segment = lax.dynamic_slice_in_dim(segment, own_first, local_rows, 0)
    cosine_table, sine_table = tables(lax.dynamic_slice_in_dim(inside, own_first, local_rows, 0))
    cosine_heads = cosine_table[:, None, :]
    sine_heads = sine_table[:, None, :]
    score_scale = (NOPE + ROPE) ** (-0.5)
    head_count = w_qb.shape[1] // (NOPE + ROPE)
    w_kvb_exact = w_kvb.astype(jnp.float32)
    tokens_f = tokens_in.astype(jnp.float32)
    scale_in = rms_scale(tokens_f)
    normed_in = (tokens_f * scale_in * gain_in).astype(jnp.bfloat16)
    q_latent_pre = dot_plain(normed_in, w_qa)
    scale_q = rms_scale(q_latent_pre)
    q_latent = (q_latent_pre * scale_q * gain_q).astype(jnp.bfloat16)
    query_full = dot_plain(q_latent, w_qb).reshape(local_rows, head_count, NOPE + ROPE)
    queries = jnp.concatenate(
        [query_full[..., :NOPE], rotate(query_full[..., NOPE:], cosine_heads, sine_heads)], axis=-1
    ).astype(jnp.bfloat16)
    query_nope = queries[..., :NOPE]
    query_rope = queries[..., NOPE:]
    kv_input = dot_plain(normed_in, w_kva)
    latent_raw = kv_input[:, :KVR]
    scale_kv = rms_scale(latent_raw)
    latent = (latent_raw * scale_kv * gain_kv).astype(jnp.bfloat16)
    key_rope = rotate(kv_input[:, KVR:], cosine_table, sine_table).astype(jnp.bfloat16)

    def expand(latent_rows):
        return (
            dot_plain(latent_rows, w_kvb)
            .astype(jnp.bfloat16)
            .reshape(latent_rows.shape[0], head_count, NOPE + VDIM)
        )

    def scores_of(kv_rows, rope_rows):
        piece_rows = kv_rows.shape[0]
        allowed = (segment[None, :] == query_segment[:, None]) & (
            places[None, :] <= query_place[:, None]
        )
        raw_scores = jnp.einsum(
            "qhd,khd->hqk", query_nope, kv_rows[..., :NOPE], preferred_element_type=jnp.float32
        )
        raw_scores = raw_scores + jnp.einsum(
            "qhd,kd->hqk", query_rope, rope_rows, preferred_element_type=jnp.float32
        )
        return (raw_scores * score_scale, allowed[None])

    pieces = (
        lax.all_gather(latent, "ctx", axis=0, tiled=True),
        lax.all_gather(key_rope, "ctx", axis=0, tiled=True),
    )
    run_top = jnp.full((head_count, local_rows), MASKED, jnp.float32)
    scores, allowed = scores_of(expand(pieces[0]), pieces[1])
    scores = jnp.where(allowed, scores, MASKED)
    new_top = jnp.maximum(run_top, jnp.max(scores, axis=-1))
    terms = jnp.where(allowed, jnp.exp(scores - new_top[..., None]), 0.0)
    run_total = jnp.sum(terms, axis=-1)
    log_total = new_top + jnp.log(run_total)
    pieces = (
        lax.all_gather(latent, "ctx", axis=0, tiled=True),
        lax.all_gather(key_rope, "ctx", axis=0, tiled=True),
    )
    kv_rows = expand(pieces[0])
    scores, allowed = scores_of(kv_rows, pieces[1])
    weights = jnp.where(allowed, jnp.exp(scores - log_total[..., None]), 0.0).astype(jnp.bfloat16)
    attn_f = jnp.einsum(
        "hqk,khd->qhd", weights, kv_rows[..., NOPE:], preferred_element_type=jnp.float32
    )
    heads_out = attn_f.astype(jnp.bfloat16).reshape(local_rows, head_count * VDIM)
    attention = lax.psum(dot_cols(heads_out, w_out).astype(jnp.bfloat16), "tp").astype(jnp.float32)
    middle = tokens_f + RESIDUAL_SCALE * attention
    scale_mid = rms_scale(middle)
    normed_mid = (middle * scale_mid * gain_mid).astype(jnp.bfloat16)
    gate_val = dot_plain(normed_mid, w_gate)
    up_val = dot_plain(normed_mid, w_up)
    sig_gate = jax.nn.sigmoid(gate_val)
    silu_gate = gate_val * sig_gate
    activation = (silu_gate * up_val).astype(jnp.bfloat16)
    feed_out = lax.psum(dot_cols(activation, w_down).astype(jnp.bfloat16), "tp").astype(jnp.float32)
    out = (middle + RESIDUAL_SCALE * feed_out).astype(jnp.bfloat16)
    cotangent_f = cotangent.astype(jnp.float32)
    d_feed = (RESIDUAL_SCALE * cotangent_f).astype(jnp.bfloat16)
    gw_down = dot_rows(d_feed, activation)
    d_activation = dot_plain(d_feed, w_down)
    d_gate = (d_activation * up_val * sig_gate * (1.0 + gate_val * (1.0 - sig_gate))).astype(
        jnp.bfloat16
    )
    d_up = (d_activation * silu_gate).astype(jnp.bfloat16)
    gw_gate = dot_rows(normed_mid, d_gate)
    gw_up = dot_rows(normed_mid, d_up)
    d_normed_mid = lax.psum(
        (dot_cols(d_gate, w_gate) + dot_cols(d_up, w_up)).astype(jnp.bfloat16), "tp"
    ).astype(jnp.float32)
    d_middle_norm, d_gain_mid = rms_back(d_normed_mid, middle, scale_mid, gain_mid)
    d_middle = cotangent_f + d_middle_norm
    d_attention = (RESIDUAL_SCALE * d_middle).astype(jnp.bfloat16)
    gw_out = dot_rows(d_attention, heads_out)
    d_heads = (
        dot_plain(d_attention, w_out).astype(jnp.bfloat16).reshape(local_rows, head_count, VDIM)
    )
    delta = jnp.sum(d_heads.astype(jnp.float32) * attn_f, axis=-1).T
    pieces = (
        lax.all_gather(latent, "ctx", axis=0, tiled=True),
        lax.all_gather(key_rope, "ctx", axis=0, tiled=True),
    )
    kv_rows = expand(pieces[0])
    rope_rows = pieces[1]
    piece_rows = kv_rows.shape[0]
    scores, allowed = scores_of(kv_rows, rope_rows)
    probabilities = jnp.where(allowed, jnp.exp(scores - log_total[..., None]), 0.0)
    d_probs = jnp.einsum(
        "qhd,khd->hqk", d_heads, kv_rows[..., NOPE:], preferred_element_type=jnp.float32
    )
    d_scores = (probabilities * (d_probs - delta[..., None])).astype(jnp.bfloat16)
    weights = probabilities.astype(jnp.bfloat16)
    d_nope = jnp.einsum(
        "hqk,khd->qhd", d_scores, kv_rows[..., :NOPE], preferred_element_type=jnp.float32
    )
    d_rope = jnp.einsum("hqk,kd->qhd", d_scores, rope_rows, preferred_element_type=jnp.float32)
    d_keys = score_scale * jnp.einsum(
        "hqk,qhd->khd", d_scores, query_nope, preferred_element_type=jnp.float32
    )
    d_values = jnp.einsum("hqk,qhd->khd", weights, d_heads, preferred_element_type=jnp.float32)
    d_key_rope = score_scale * jnp.einsum(
        "hqk,qhd->kd", d_scores, query_rope, preferred_element_type=jnp.float32
    )
    kv_piece = jnp.concatenate([d_keys, d_values], axis=-1).reshape(
        piece_rows, head_count * (NOPE + VDIM)
    )
    d_query = score_scale * jnp.concatenate([d_nope, d_rope], axis=-1)
    latent_piece = exact_cols(kv_piece, w_kvb_exact)
    kvb_grad = exact_rows(pieces[0].astype(jnp.float32), kv_piece)
    folded = (d_query, latent_piece, d_key_rope, kvb_grad)
    d_query = folded[0]
    gw_kvb = folded[3]
    d_latent_part, rope_own = (
        lax.psum_scatter(
            folded[1].astype(jnp.bfloat16), "ctx", scatter_dimension=0, tiled=True
        ).astype(jnp.float32),
        lax.psum_scatter(
            folded[2].astype(jnp.bfloat16), "ctx", scatter_dimension=0, tiled=True
        ).astype(jnp.float32),
    )
    d_query_pre = jnp.concatenate(
        [d_query[..., :NOPE], rotate_back(d_query[..., NOPE:], cosine_heads, sine_heads)], axis=-1
    )
    d_query_pre = d_query_pre.reshape(local_rows, head_count * (NOPE + ROPE)).astype(jnp.bfloat16)
    gw_qb = dot_rows(q_latent, d_query_pre)
    d_q_latent, d_latent, d_rope_sum = (
        lax.psum(dot_cols(d_query_pre, w_qb).astype(jnp.bfloat16), "tp").astype(jnp.float32),
        lax.psum(d_latent_part.astype(jnp.bfloat16), "tp").astype(jnp.float32),
        lax.psum(rope_own.astype(jnp.bfloat16), "tp").astype(jnp.float32),
    )
    d_q_pre, d_gain_q = rms_back(d_q_latent, q_latent_pre, scale_q, gain_q)
    d_q_low = d_q_pre.astype(jnp.bfloat16)
    d_latent_raw, d_gain_kv = rms_back(d_latent, latent_raw, scale_kv, gain_kv)
    d_kv_input = jnp.concatenate(
        [d_latent_raw, rotate_back(d_rope_sum, cosine_table, sine_table)], axis=-1
    ).astype(jnp.bfloat16)
    gw_qa = dot_rows(normed_in, d_q_low)
    gw_kva = dot_rows(normed_in, d_kv_input)
    d_normed_in = dot_cols(d_q_low, w_qa) + dot_cols(d_kv_input, w_kva)
    d_tokens_norm, d_gain_in = rms_back(d_normed_in, tokens_f, scale_in, gain_in)
    grad_in = d_middle + d_tokens_norm
    summed = (
        lax.psum_scatter(gw_qa.astype(jnp.bfloat16), "ctx", scatter_dimension=0, tiled=True).astype(
            jnp.float32
        ),
        lax.psum_scatter(
            gw_kva.astype(jnp.bfloat16), "ctx", scatter_dimension=0, tiled=True
        ).astype(jnp.float32),
        lax.psum_scatter(gw_qb.astype(jnp.bfloat16), "ctx", scatter_dimension=0, tiled=True).astype(
            jnp.float32
        ),
        lax.psum_scatter(
            gw_kvb.astype(jnp.bfloat16), "ctx", scatter_dimension=0, tiled=True
        ).astype(jnp.float32),
        lax.psum_scatter(
            gw_out.astype(jnp.bfloat16), "ctx", scatter_dimension=0, tiled=True
        ).astype(jnp.float32),
        lax.psum_scatter(
            gw_gate.astype(jnp.bfloat16), "ctx", scatter_dimension=0, tiled=True
        ).astype(jnp.float32),
        lax.psum_scatter(gw_up.astype(jnp.bfloat16), "ctx", scatter_dimension=0, tiled=True).astype(
            jnp.float32
        ),
        lax.psum_scatter(
            gw_down.astype(jnp.bfloat16), "ctx", scatter_dimension=0, tiled=True
        ).astype(jnp.float32),
        lax.psum_scatter(
            d_gain_in.astype(jnp.bfloat16), "ctx", scatter_dimension=0, tiled=True
        ).astype(jnp.float32),
        lax.psum_scatter(
            d_gain_q.astype(jnp.bfloat16), "ctx", scatter_dimension=0, tiled=True
        ).astype(jnp.float32),
        lax.psum_scatter(
            d_gain_kv.astype(jnp.bfloat16), "ctx", scatter_dimension=0, tiled=True
        ).astype(jnp.float32),
        lax.psum_scatter(
            d_gain_mid.astype(jnp.bfloat16), "ctx", scatter_dimension=0, tiled=True
        ).astype(jnp.float32),
    )
    return (out, grad_in) + tuple(summed)


def solution(mesh):
    return jax.shard_map(
        on_device,
        mesh=mesh,
        in_specs=(
            P("ctx", None),
            P(),
            P(),
            P(None, "tp"),
            P(None, "tp"),
            P(None, "tp"),
            P(None, "tp"),
            P(None, "tp"),
            P(None, "tp"),
            P(),
            P(),
            P(),
            P(),
            P("ctx", None),
            P(),
            P(),
        ),
        out_specs=(
            P("ctx", None),
            P("ctx", None),
            P("ctx", None),
            P("ctx", None),
            P("ctx", "tp"),
            P("ctx", "tp"),
            P("ctx", "tp"),
            P("ctx", "tp"),
            P("ctx", "tp"),
            P("ctx", "tp"),
            P("ctx"),
            P("ctx"),
            P("ctx"),
            P("ctx"),
        ),
        check_vma=False,
    )
```

profile of v0, /device:TPU:0, one launch (start us, length us, event | category | flops | bytes accessed | tf_op | source)
XLA Modules:
  0.0 1350.5 jit_solution(5521593870138854980)
XLA Ops:
  18.7 10.8 all_gather.5
  55.4 31.6 %fusion.23 = f32[10,512,4096]{2,1,0:T(8,128)} fusion(bf16[4096,10,128]{0,2,1:T(8,128)(2,1)} %bitcast.84, f32[512,10,96]{0,2,1:T(8,128)} %bitcast.92), kind=kOutput, calls=%fused_computation.53 | convolution fusion | flops 2684354560 | bytes 89784320 | tf_op jit(solution)/shard_map/qhd,khd->hqk/dot_general | solution.py:170
  87.1 56.6 %select_reduce_fusion.1 = (f32[10,512]{1,0:T(8,128)}, f32[10,512,4096]{2,1,0:T(8,128)}) fusion(pred[512,4096]{1,0:T(8,128)(4,1)} %compare_and_fusion, f32[10,512,4096]{2,1,0:T(8,128)} %fusion.23, bf16[512,10,32]{0,2,1:T(8,128)(2,1)} %fusion.49, bf16[4096,32]{0,1:T(8,128)(2,1)S(1)} %all_gather.5), kind=kOutput, calls=%fused_computation.5 | convolution fusion | flops 1426058240 | bytes 170479616 | tf_op jit(solution)/shard_map/qhd,kd->hqk/dot_general | solution.py:173
  144.4 35.5 %select_reduce_fusion = f32[10,512]{1,0:T(8,128)S(1)} fusion(f32[10,512,4096]{2,1,0:T(8,128)} %get-tuple-element.60, f32[10,512]{1,0:T(8,128)S(1)} %broadcast_maximum_fusion, pred[512,4096]{1,0:T(8,128)(4,1)} %compare_and_fusion), kind=kLoop, calls=%fused_computation.4 | loop fusion | flops 83880960 | bytes 86024192 | tf_op jit(solution)/shard_map/reduce_sum | solution.py:187
  179.9 32.2 %fusion.100 = (bf16[512,10,64]{0,2,1:T(8,128)(2,1)}, f32[512,10,64]{0,2,1:T(8,128)}) fusion(f32[10,512,4096]{2,1,0:T(8,128)} %get-tuple-element.60, f32[10,512]{1,0:T(8,128)S(1)} %log_add_fusion, pred[512,4096]{1,0:T(8,128)(4,1)} %compare_and_fusion, bf16[4096,10,128]{0,2,1:T(8,128)(2,1)} %bitcast.85), kind=kOutput, calls=%fused_computation.194 | convolution fusion | flops 2747596800 | bytes 93212672 | tf_op jit(solution)/shard_map/hqk,khd->qhd/dot_general | solution.py:196
  217.0 104.2 %all-reduce.10.cloned.1.call-done = bf16[512,2560]{1,0:T(8,128)(2,1)} async-done(((bf16[512,2560]{1,0:T(8,128)(2,1)}), bf16[512,2560]{1,0:T(8,128)(2,1)}) %all-reduce.10.cloned.1.call-update) | async-done | bytes 2621456 | tf_op jit(solution)/shard_map/psum | solution.py:200
  341.7 10.7 multiply_convert_fusion.3
  367.9 10.4 convolution_convert_fusion.8
  378.2 92.7 %all-reduce.12.cloned.1.call-done = bf16[512,2560]{1,0:T(8,128)(2,1)} async-done(((bf16[512,2560]{1,0:T(8,128)(2,1)}), bf16[512,2560]{1,0:T(8,128)(2,1)}) %all-reduce.12.cloned.1.call-update) | async-done | bytes 2621456 | tf_op jit(solution)/shard_map/psum | solution.py:221
  489.9 49.8 %multiply_convert_fusion = bf16[10,512,4096]{2,1,0:T(8,128)(2,1)} fusion(f32[10,512,4096]{2,1,0:T(8,128)} %get-tuple-element.60, f32[10,512]{1,0:T(8,128)S(1)} %bitcast.99, f32[10,512]{1,0:T(8,128)S(1)} %log_add_fusion, pred[512,4096]{1,0:T(8,128)(4,1)} %compare_and_fusion, bf16[512,10,64]{0,2,1:T(8,128)(2,1)S(1)} %bitcast.95, ...), kind=kOutput, calls=%fused_computation.2 | convolution fusion | flops 2789212160 | bytes 133865472 | tf_op jit(solution)/shard_map/qhd,khd->hqk/dot_general | solution.py:241
  539.8 19.3 %convolution_bitcast_fusion.2 = f32[512,10,32]{0,2,1:T(8,128)} fusion(bf16[10,512,4096]{2,1,0:T(8,128)(2,1)} %multiply_convert_fusion, bf16[4096,32]{0,1:T(8,128)(2,1)S(1)} %copy-done.21), kind=kOutput, calls=%fused_computation.90 | convolution fusion | flops 1342177280 | bytes 42860544 | tf_op jit(solution)/shard_map/hqk,kd->qhd/dot_general | solution.py:249
  559.1 20.3 %fusion.40 = f32[512,10,64]{0,2,1:T(8,128)} fusion(bf16[10,512,4096]{2,1,0:T(8,128)(2,1)} %multiply_convert_fusion, bf16[4096,10,128]{0,2,1:T(8,128)(2,1)} %bitcast.87), kind=kOutput, calls=%fused_computation.83 | convolution fusion | flops 2684354560 | bytes 48496640 | tf_op jit(solution)/shard_map/hqk,khd->qhd/dot_general | solution.py:246
  579.4 33.6 %convolution_bitcast_fusion = f32[4096,10,64]{0,2,1:T(8,128)} fusion(bf16[512,10,64]{0,2,1:T(8,128)(2,1)S(1)} %bitcast.96, f32[10,512,4096]{2,1,0:T(8,128)} %get-tuple-element.60, f32[10,512]{1,0:T(8,128)S(1)} %log_add_fusion, pred[512,4096]{1,0:T(8,128)(4,1)S(1)} %copy-done.2), kind=kOutput, calls=%fused_computation.20 | convolution fusion | flops 2747269120 | bytes 97144832 | tf_op jit(solution)/shard_map/hqk,qhd->khd/dot_general | solution.py:253
  613.0 21.2 %multiply_bitcast_fusion = f32[4096,10,64]{0,2,1:T(8,128)} fusion(bf16[10,512,4096]{2,1,0:T(8,128)(2,1)} %multiply_convert_fusion, f32[512,10,96]{0,2,1:T(8,128)} %bitcast.93), kind=kOutput, calls=%fused_computation.18 | convolution fusion | flops 2686976000 | bytes 53084160 | tf_op jit(solution)/shard_map/hqk,qhd->khd/dot_general | solution.py:250
  634.3 16.1 %pad_maximum_fusion = f32[4096,10,128]{0,2,1:T(8,128)} fusion(f32[4096,10,64]{0,2,1:T(8,128)} %convolution_bitcast_fusion, f32[4096,10,64]{0,2,1:T(8,128)} %multiply_bitcast_fusion), kind=kLoop, calls=%fused_computation.7 | loop fusion | flops 5242880 | bytes 41943040 | tf_op jit(solution)/shard_map/concatenate | solution.py:257
  650.4 15.8 %convolution_convert_fusion.4 = bf16[4096,256]{0,1:T(8,128)(2,1)} fusion(f32[4096,1280]{0,1:T(8,128)} %bitcast.82, bf16[256,1280]{1,0:T(8,128)(2,1)S(1)} %copy-done.19), kind=kOutput, calls=%fused_computation.46 | convolution fusion | flops 16107175936 | bytes 23724032 | tf_op jit(solution)/shard_map/dot_general | solution.py:48
  668.1 18.7 %fusion.28 = bf16[4096,32]{0,1:T(8,128)(2,1)} fusion(bf16[512,10,32]{0,2,1:T(8,128)(2,1)S(1)} %copy-done.15, bf16[10,512,4096]{2,1,0:T(8,128)(2,1)} %multiply_convert_fusion), kind=kOutput, calls=%fused_computation.59 | convolution fusion | flops 1342439424 | bytes 42532864 | tf_op jit(solution)/shard_map/hqk,qhd->kd/dot_general | solution.py:254
  691.1 15.5 %reduce-scatter.13.cloned.1.call-done = bf16[512,256]{0,1:T(8,128)(2,1)} async-done(((bf16[4096,256]{0,1:T(8,128)(2,1)}), bf16[512,256]{0,1:T(8,128)(2,1)}) %reduce-scatter.13.cloned.1.call-update) | async-done | bytes 262160 | tf_op jit(solution)/shard_map/reduce_scatter | solution.py:267
  706.8 14.7 %convolution_convert_fusion.10 = bf16[256,1280]{1,0:T(8,128)(2,1)} fusion(bf16[4096,256]{0,1:T(8,128)(2,1)S(1)} %copy-done.9, f32[4096,1280]{0,1:T(8,128)} %bitcast.83), kind=kOutput, calls=%fused_computation.68 | convolution fusion | flops 16106455040 | bytes 23724032 | tf_op jit(solution)/shard_map/dot_general | solution.py:38
  732.1 11.9 reduce-scatter.15.cloned.1.call-done
  744.0 20.2 %psum.47 = bf16[512,32]{0,1:T(8,128)(2,1)S(1)} all-reduce(bf16[512,32]{0,1:T(8,128)(2,1)} %reduce-scatter.15.cloned.1.call-done), channel_id=1, replica_groups=mesh['ctx'=8,'tp'=4] {'tp'}, use_global_device_ids=true, to_apply=%region_21.22 | all-reduce | flops 16384 | bytes 65536 | tf_op jit(solution)/shard_map/psum | solution.py:282
  764.9 121.2 %all-reduce.14.cloned.1.call-done = (bf16[512,2560]{1,0:T(8,128)(2,1)}, bf16[512,768]{1,0:T(8,128)(2,1)}, bf16[512,256]{0,1:T(8,128)(2,1)}) async-done(((bf16[512,2560]{1,0:T(8,128)(2,1)}, bf16[512,768]{1,0:T(8,128)(2,1)}, bf16[512,256]{0,1:T(8,128)(2,1)}), (bf16[512,2560]{1,0:T(8,128)(2,1)}, bf16[512,768]{1,0:T(8,128)(2,1)}, bf16[512,256]{0,1:T(8,128)(2,1)})) %all-reduce.14.cloned.1.call-update) | async-done | bytes 3670032 | tf_op jit(solution)/shard_map/psum | solution.py:209
  895.4 10.6 convolution_convert_fusion.3
  906.0 10.5 convolution_convert_fusion.2
  916.8 10.6 convolution_convert_fusion.1
  940.6 24.6 %reduce-scatter.19.cloned.1.call-done = bf16[96,960]{1,0:T(8,128)(2,1)} async-done(((bf16[768,960]{1,0:T(8,128)(2,1)}), bf16[96,960]{1,0:T(8,128)(2,1)}) %reduce-scatter.19.cloned.1.call-update) | async-done | bytes 184336 | tf_op jit(solution)/shard_map/reduce_scatter | solution.py:302
  966.9 48.6 %reduce-scatter.23.cloned.1.call-done = bf16[320,640]{1,0:T(8,128)(2,1)} async-done(((bf16[2560,640]{1,0:T(8,128)(2,1)}), bf16[320,640]{1,0:T(8,128)(2,1)}) %reduce-scatter.23.cloned.1.call-update) | async-done | bytes 409616 | tf_op jit(solution)/shard_map/reduce_scatter | solution.py:308
  1027.2 23.7 %all-reduce.4 = (bf16[2560]{0:T(1024)(128)(2,1)S(1)}, bf16[768]{0:T(1024)(128)(2,1)S(1)}, bf16[256]{0:T(256)(128)(2,1)S(1)}, bf16[2560]{0:T(1024)(128)(2,1)S(1)}) all-reduce(bf16[2560]{0:T(1024)(128)(2,1)S(1)} %get-tuple-element.16, bf16[768]{0:T(1024)(128)(2,1)S(1)} %get-tuple-element.18, ...), channel_id=12, replica_groups=mesh['ctx'=8,'tp'=4] {'ctx'}, use_global_device_ids=true, to_apply=%region_32.33.clone | all-reduce | flops 6144 | bytes 24576
  1063.8 72.0 %reduce-scatter.25.cloned.1.call-done = bf16[320,1600]{1,0:T(8,128)(2,1)} async-done(((bf16[2560,1600]{1,0:T(8,128)(2,1)}), bf16[320,1600]{1,0:T(8,128)(2,1)}) %reduce-scatter.25.cloned.1.call-update) | async-done | bytes 1024016 | tf_op jit(solution)/shard_map/reduce_scatter | solution.py:311
  1138.5 73.1 %reduce-scatter.27.cloned.1.call-done = bf16[320,1600]{1,0:T(8,128)(2,1)} async-done(((bf16[2560,1600]{1,0:T(8,128)(2,1)}), bf16[320,1600]{1,0:T(8,128)(2,1)}) %reduce-scatter.27.cloned.1.call-update) | async-done | bytes 1024016 | tf_op jit(solution)/shard_map/reduce_scatter | solution.py:314
  1214.3 73.3 %reduce-scatter.29.cloned.1.call-done = bf16[320,1600]{1,0:T(8,128)(2,1)} async-done(((bf16[2560,1600]{1,0:T(8,128)(2,1)}), bf16[320,1600]{1,0:T(8,128)(2,1)}) %reduce-scatter.29.cloned.1.call-update) | async-done | bytes 1024016 | tf_op jit(solution)/shard_map/reduce_scatter | solution.py:317
  1290.3 51.1 %reduce-scatter.17.cloned.1.call-done = bf16[320,768]{1,0:T(8,128)(2,1)} async-done(((bf16[2560,768]{1,0:T(8,128)(2,1)}), bf16[320,768]{1,0:T(8,128)(2,1)}) %reduce-scatter.17.cloned.1.call-update) | async-done | bytes 491536 | tf_op jit(solution)/shard_map/reduce_scatter | solution.py:296
  (239 shorter events, 172.1 us)
Async XLA Ops:
  7.2 205.0 %copy-start = (bf16[2560,640]{1,0:T(8,128)(2,1)S(1)}, bf16[2560,640]{1,0:T(8,128)(2,1)}, u32[]{:S(2)}) copy-start(bf16[2560,640]{1,0:T(8,128)(2,1)} %param.21) | copy-start | bytes 9830404
  7.2 39.7 %all-gather.2.cloned.1.call-start = ((), (), s32[]{:S(2)}) async-start(), calls=%async_computation.10 | async-start | bytes 2359296 | tf_op jit(solution)/shard_map/all_gather | solution.py:190
  15.8 305.5 %all-reduce.10.cloned.1.call-start = ((), (), s32[]{:S(2)}) async-start(), calls=%async_computation.11 | async-start | bytes 5242880 | tf_op jit(solution)/shard_map/psum | solution.py:200
  18.7 18.0 %copy-start.26 = (f32[512,32]{0,1:T(8,128)}, f32[512,32]{0,1:T(8,128)S(1)}, u32[]{:S(2)}) copy-start(f32[512,32]{0,1:T(8,128)S(1)} %get-tuple-element.45) | copy-start | bytes 196612
  18.7 18.0 %copy-start.28 = (f32[512,32]{0,1:T(8,128)}, f32[512,32]{0,1:T(8,128)S(1)}, u32[]{:S(2)}) copy-start(f32[512,32]{0,1:T(8,128)S(1)} %get-tuple-element.46) | copy-start | bytes 196612
  29.5 57.6 %copy-start.20 = (bf16[4096,32]{0,1:T(8,128)(2,1)}, bf16[4096,32]{0,1:T(8,128)(2,1)S(1)}, u32[]{:S(2)}) copy-start(bf16[4096,32]{0,1:T(8,128)(2,1)S(1)} %all_gather.5) | copy-start | bytes 786436
  144.4 35.5 %copy-start.30 = (f32[10,512]{1,0:T(8,128)S(1)}, f32[10,512]{1,0:T(8,128)}, u32[]{:S(2)}) copy-start(f32[10,512]{1,0:T(8,128)} %get-tuple-element.59) | copy-start | bytes 61444
  217.0 108.1 %copy-start.38 = (f32[2560]{0:T(1024)S(1)}, f32[2560]{0:T(1024)}, u32[]{:S(2)}) copy-start(f32[2560]{0:T(1024)} %param.28) | copy-start | bytes 30724
  217.0 254.0 %all-reduce.12.cloned.1.call-start = ((), (), s32[]{:S(2)}) async-start(), calls=%async_computation.12 | async-start | bytes 5242880 | tf_op jit(solution)/shard_map/psum | solution.py:221
  367.7 339.0 %reduce-scatter.13.cloned.1.call-start = ((), (), s32[]{:S(2)}) async-start(), calls=%async_computation.13 | async-start | bytes 2359296 | tf_op jit(solution)/shard_map/reduce_scatter | solution.py:267
  489.9 49.8 %copy-start.21 = (bf16[4096,32]{0,1:T(8,128)(2,1)S(1)}, bf16[4096,32]{0,1:T(8,128)(2,1)}, u32[]{:S(2)}) copy-start(bf16[4096,32]{0,1:T(8,128)(2,1)} %copy-done.20) | copy-start | bytes 786436
  559.1 20.3 %copy-start.2 = (pred[512,4096]{1,0:T(8,128)(4,1)S(1)}, pred[512,4096]{1,0:T(8,128)(4,1)}, u32[]{:S(2)}) copy-start(pred[512,4096]{1,0:T(8,128)(4,1)} %compare_and_fusion) | copy-start | bytes 6291460
  666.2 77.8 %reduce-scatter.15.cloned.1.call-start = ((), (), s32[]{:S(2)}) async-start(), calls=%async_computation.14 | async-start | bytes 294912 | tf_op jit(solution)/shard_map/reduce_scatter | solution.py:270
  686.8 20.0 %copy-start.9 = (bf16[4096,256]{0,1:T(8,128)(2,1)S(1)}, bf16[4096,256]{0,1:T(8,128)(2,1)}, u32[]{:S(2)}) copy-start(bf16[4096,256]{0,1:T(8,128)(2,1)} %all-gather.2.cloned.1.call-done) | copy-start | bytes 6291460
  686.8 199.3 %all-reduce.14.cloned.1.call-start = ((), (), s32[]{:S(2)}) async-start(), calls=%async_computation.23 | async-start | bytes 7340032 | tf_op jit(solution)/shard_map/psum | solution.py:209
  706.7 232.3 %reduce-scatter.21.cloned.1.call-start = ((), (), s32[]{:S(2)}) async-start(), calls=%async_computation.17 | async-start | bytes 737280 | tf_op jit(solution)/shard_map/reduce_scatter | solution.py:305
  721.5 243.7 %reduce-scatter.19.cloned.1.call-start = ((), (), s32[]{:S(2)}) async-start(), calls=%async_computation.16 | async-start | bytes 1769472 | tf_op jit(solution)/shard_map/reduce_scatter | solution.py:302
  725.4 38.8 %copy-start.34 = (f32[512,16]{0,1:T(8,128)S(1)}, f32[512,16]{0,1:T(8,128)}, u32[]{:S(2)}) copy-start(f32[512,16]{0,1:T(8,128)} %copy-done.33) | copy-start | bytes 98308
  725.4 38.9 %copy-start.32 = (f32[512,16]{0,1:T(8,128)S(1)}, f32[512,16]{0,1:T(8,128)}, u32[]{:S(2)}) copy-start(f32[512,16]{0,1:T(8,128)} %copy-done.31) | copy-start | bytes 98308
  725.4 160.7 %copy-start.13 = (f32[512,288]{0,1:T(8,128)S(1)}, f32[512,288]{0,1:T(8,128)}, u32[]{:S(2)}) copy-start(f32[512,288]{0,1:T(8,128)} %copy-done.12) | copy-start | bytes 1769476
  725.4 160.7 %copy-start.41 = (f32[512]{0:T(512)S(1)}, f32[512]{0:T(512)}, u32[]{:S(2)}) copy-start(f32[512]{0:T(512)} %copy-done.40) | copy-start | bytes 6148
  725.4 160.6 %copy-start.46 = (f32[256]{0:T(256)S(1)}, f32[256]{0:T(256)}, u32[]{:S(2)}) copy-start(f32[256]{0:T(256)} %param.27) | copy-start | bytes 3076
  725.5 290.0 %reduce-scatter.23.cloned.1.call-start = ((), (), s32[]{:S(2)}) async-start(), calls=%async_computation.18 | async-start | bytes 3686400 | tf_op jit(solution)/shard_map/reduce_scatter | solution.py:308
  732.0 156.4 %copy-start.5 = (bf16[512,2560]{1,0:T(8,128)(2,1)S(1)}, bf16[512,2560]{1,0:T(8,128)(2,1)}, u32[]{:S(2)}) copy-start(bf16[512,2560]{1,0:T(8,128)(2,1)} %param.16) | copy-start | bytes 7864324
  732.0 156.4 %copy-start.39 = (f32[2560]{0:T(1024)S(1)}, f32[2560]{0:T(1024)}, u32[]{:S(2)}) copy-start(f32[2560]{0:T(1024)} %param.25) | copy-start | bytes 30724
  732.0 329.8 %reduce-scatter.31.cloned.1.call-start = ((), (), s32[]{:S(2)}) async-start(), calls=%async_computation.22 | async-start | bytes 2211840
  895.1 240.7 %reduce-scatter.25.cloned.1.call-start = ((), (), s32[]{:S(2)}) async-start(), calls=%async_computation.19 | async-start | bytes 9584640 | tf_op jit(solution)/shard_map/reduce_scatter | solution.py:311
  906.0 305.6 %reduce-scatter.27.cloned.1.call-start = ((), (), s32[]{:S(2)}) async-start(), calls=%async_computation.20 | async-start | bytes 9584640 | tf_op jit(solution)/shard_map/reduce_scatter | solution.py:314
  916.5 371.0 %reduce-scatter.29.cloned.1.call-start = ((), (), s32[]{:S(2)}) async-start(), calls=%async_computation.21 | async-start | bytes 9584640 | tf_op jit(solution)/shard_map/reduce_scatter | solution.py:317
  927.5 413.9 %reduce-scatter.17.cloned.1.call-start = ((), (), s32[]{:S(2)}) async-start(), calls=%async_computation.15 | async-start | bytes 4423680 | tf_op jit(solution)/shard_map/reduce_scatter | solution.py:296
  1022.7 30.0 %copy-start.47 = (f32[512]{0:T(512)S(1)}, f32[512]{0:T(512)}, u32[]{:S(2)}) copy-start(f32[512]{0:T(512)} %get-tuple-element.49) | copy-start | bytes 6148
  1063.0 280.5 %copy-start.1 = (bf16[2560,640]{1,0:T(8,128)(2,1)S(1)}, bf16[2560,640]{1,0:T(8,128)(2,1)}, u32[]{:S(2)}) copy-start(bf16[2560,640]{1,0:T(8,128)(2,1)} %param.21) | copy-start | bytes 9830404
  (45 other events, 250.8 us)
Sparse Core Ops, SparseCore 0:
  15.9 30.9 all-gather.1
  217.1 104.1 all-reduce.9
  367.8 103.1 all-reduce.11
  666.3 40.2 reduce-scatter.12
  710.4 33.5 reduce-scatter.14
  747.0 139.0 all-reduce.13
  889.2 33.5 reduce-scatter.20
  926.7 38.4 reduce-scatter.18
  968.6 46.8 reduce-scatter.22
  1019.3 40.4 reduce-scatter.30
  1063.7 72.0 reduce-scatter.24
  1139.5 72.0 reduce-scatter.26
  1215.5 72.0 reduce-scatter.28
  1291.4 50.0 reduce-scatter.16
where the time goes:
time: 1360 us; the launch traced here: 1350 us
  waiting for transfers between devices  694 us (51%)
  matrix products  455 us (33%)
  other arithmetic  116 us (9%)
  blocking collectives  54.7 us (4%)
  between operations  17.2 us (1%)
    psum x1, waiting for transfers between devices, on_device(): lax.psum(dot_cols(activation, w_down).astype(jnp.bfloat16), 'tp')  121 us
    psum x1, waiting for transfers between devices, on_device(): lax.psum(dot_cols(heads_out, w_out).astype(jnp.bfloat16), 'tp')  104 us
    psum x1, waiting for transfers between devices, on_device(): lax.psum((dot_cols(d_gate, w_gate) + dot_cols(d_up, w_up)).astype(jnp.bfl...  92.7 us
    reduce_scatter x1, waiting for transfers between devices, on_device(): lax.psum_scatter(gw_down.astype(jnp.bfloat16), 'ctx', scatter_dimension=0...  73.3 us
    reduce_scatter x1, waiting for transfers between devices, on_device(): lax.psum_scatter(gw_up.astype(jnp.bfloat16), 'ctx', scatter_dimension=0,...  73.1 us
    reduce_scatter x1, waiting for transfers between devices, on_device(): lax.psum_scatter(gw_gate.astype(jnp.bfloat16), 'ctx', scatter_dimension=0...  72 us
    dot_general x1, matrix products, scores_of(): jnp.einsum('qhd,kd->hqk', query_rope, rope_rows, preferred_element_type=j...  56.6 us
    reduce_scatter x1, waiting for transfers between devices, on_device(): lax.psum_scatter(gw_qa.astype(jnp.bfloat16), 'ctx', scatter_dimension=0,...  51.1 us
  transfers between devices with their start and end apart: 14, of which 12 were waited for; matrix products, arithmetic and copies ran while one was open for 12% of the time, Pallas kernels for 0%

commit v1 on v0

v1 whole, which is shorter than its diff:
```python
import functools
import math

import jax
import jax.numpy as jnp
from jax import lax
from jax.experimental import pallas as pl
from jax.experimental.pallas import tpu as pltpu
from jax.sharding import PartitionSpec as P

KVR = 256
NOPE = 64
ROPE = 32
VDIM = 64
HEAD = NOPE + VDIM
WIDE = 2 * HEAD
MASKED = -1e30
SCORE_SCALE = (NOPE + ROPE) ** (-0.5)
EXP2_SCALE = SCORE_SCALE * math.log2(math.e)
FOLD_AT = 96
VMEM_LIMIT = 56 * 1024 * 1024

EPSILON = 1e-05
ROPE_BASE = 10000.0
RESIDUAL_SCALE = 1.4 / math.sqrt(62.0)


def dot_nn(left_op, right_op):
    return jnp.dot(left_op, right_op, preferred_element_type=jnp.float32)


def dot_nt(left_op, right_op):
    return lax.dot_general(
        left_op, right_op, (((1,), (1,)), ((), ())), preferred_element_type=jnp.float32
    )


def begin_of(place, starts):
    begin = jnp.zeros_like(place)
    for start in starts:
        begin = jnp.where(start <= place, start, begin)
    return begin


def pair_kind(key_block, query_block, starts, block_rows):
    key_first = key_block * block_rows
    query_first = query_block * block_rows
    early = begin_of(query_first, starts)
    late = begin_of(query_first + block_rows - 1, starts)
    needed = (key_block <= query_block) & (key_first + block_rows - 1 >= early)
    whole = (key_block < query_block) & (late <= key_first)
    return needed, whole


def mask_bias(key_block, query_block, starts, block_rows, keys_first):
    key_dim = 0 if keys_first else 1
    shape = (block_rows, block_rows)
    key_place = key_block * block_rows + lax.broadcasted_iota(jnp.int32, shape, key_dim)
    query_place = query_block * block_rows + lax.broadcasted_iota(jnp.int32, shape, 1 - key_dim)
    begin = jnp.zeros(shape, jnp.int32)
    for start in starts:
        begin = jnp.where(start <= query_place, start, begin)
    allowed = (key_place <= query_place) & (key_place >= begin)
    return jnp.where(allowed, 0.0, MASKED)


def shared_key_tile(rope_rows, block_rows):
    place = lax.broadcasted_iota(jnp.int32, (ROPE, HEAD), 0)
    lane = lax.broadcasted_iota(jnp.int32, (ROPE, HEAD), 1)
    eye = jnp.where(place == lane, 1.0, 0.0).astype(jnp.bfloat16)
    tile = dot_nn(rope_rows, eye)
    lanes = lax.broadcasted_iota(jnp.int32, (block_rows, HEAD), 1)
    ones = (lanes >= FOLD_AT) & (lanes < FOLD_AT + 3)
    return jnp.where(ones, 1.0, tile).astype(jnp.bfloat16)


def head_groups(heads):
    return [(h, min(h + 2, heads)) for h in range(0, heads, 2)]


def forward_kernel(
    blocks, heads, seqs, meta, cq, wqb, lat, wkvb, cos, sin, qx, o_out, ob_out, u_out,
    wkvt, xs, xr, vt, top, total, acc, bias,
):
    rows_all = cq.shape[0]
    block_rows = bias.shape[0]
    q_blocks = rows_all // block_rows
    starts = [meta[blocks + s] for s in range(seqs)]
    own = [meta[blocks + seqs + j] for j in range(q_blocks)]
    for first, last in head_groups(heads):
        wkvt[first * HEAD : last * HEAD, :] = (
            wkvb[:, first * HEAD : last * HEAD].astype(jnp.float32).T.astype(jnp.bfloat16)
        )
    lane = lax.broadcasted_iota(jnp.int32, (block_rows, HEAD), 1)
    for j in range(q_blocks):
        here = pl.ds(j * block_rows, block_rows)
        cos_j, sin_j = cos[here, :], sin[here, :]
        for first, last in head_groups(heads):
            pre = dot_nn(cq[here, :], wqb[:, first * HEAD : last * HEAD])
            for h in range(first, last):
                own_part = pre[:, (h - first) * HEAD : (h - first + 1) * HEAD]
                turned = pltpu.roll(own_part, NOPE, 1)
                left = pltpu.roll(turned, HEAD - ROPE // 2, 1)
                right = pltpu.roll(turned, ROPE // 2, 1)
                swapped = jnp.where(lane < ROPE // 2, -left, right)
                rope = turned * cos_j + swapped * sin_j
                qx[j, h, :, :HEAD] = jnp.where(lane < NOPE, own_part, 0.0).astype(jnp.bfloat16)
                qx[j, h, :, HEAD:] = rope.astype(jnp.bfloat16)
    top[...] = jnp.full(top.shape, MASKED, jnp.float32)
    total[...] = jnp.zeros(total.shape, jnp.float32)
    acc[...] = jnp.zeros(acc.shape, jnp.float32)

    def pair(j, masked):
        def one(h):
            keys = jnp.concatenate([xs[h], xr[...]], axis=1)
            scores = dot_nt(keys, qx[j, h])
            if masked:
                scores = scores + bias[...]
            old = top[j, h]
            new = jnp.maximum(old, jnp.max(scores, axis=0, keepdims=True))
            fade = jnp.exp2((old - new) * EXP2_SCALE)
            terms = jnp.exp2((scores - new) * EXP2_SCALE)
            top[j, h] = new
            total[j, h] = fade * total[j, h] + jnp.sum(terms, axis=0, keepdims=True)
            acc[j, h] = fade * acc[j, h] + dot_nn(vt[h], terms.astype(jnp.bfloat16))

        for h in range(heads):
            one(h)

    def step(r, carry):
        key_block = meta[r]
        kinds = [pair_kind(key_block, own[j], starts, block_rows) for j in range(q_blocks)]
        wanted = functools.reduce(jnp.logical_or, [k[0] for k in kinds])

        @pl.when(wanted)
        def _():
            here = pl.ds(pl.multiple_of(r * block_rows, block_rows), block_rows)
            latent = lat[here, :KVR]
            xr[...] = shared_key_tile(lat[here, KVR : KVR + ROPE], block_rows)
            for first, last in head_groups(heads):
                keys = dot_nn(latent, wkvb[:, first * HEAD : last * HEAD]).astype(jnp.bfloat16)
                values = dot_nt(wkvt[first * HEAD : last * HEAD, :], latent).astype(jnp.bfloat16)
                for h in range(first, last):
                    at = (h - first) * HEAD
                    xs[h] = keys[:, at : at + HEAD]
                    vt[h] = values[at + NOPE : at + HEAD, :]

        for j in range(q_blocks):
            needed, whole = kinds[j]

            @pl.when(needed & whole)
            def _():
                pair(j, False)

            @pl.when(needed & jnp.logical_not(whole))
            def _():
                bias[...] = mask_bias(key_block, own[j], starts, block_rows, True)
                pair(j, True)

        return carry

    lax.fori_loop(0, blocks, step, 0)
    for j in range(q_blocks):
        here = pl.ds(j * block_rows, block_rows)
        for first, last in head_groups(heads):
            parts = []
            for h in range(first, last):
                parts.append(acc[j, h] * (1.0 / total[j, h]))
                u_out[j, h : h + 1, :] = top[j, h] + jnp.log2(total[j, h]) * (1.0 / EXP2_SCALE)
            if len(parts) == 1:
                parts.append(jnp.zeros_like(parts[0]))
            both = jnp.concatenate(parts, axis=0).T
            width = (last - first) * VDIM
            o_out[here, first * VDIM : first * VDIM + width] = both[:, :width]
            ob_out[here, first * VDIM : first * VDIM + width] = both[:, :width].astype(jnp.bfloat16)


def attention_forward(meta, cq, wqb, lat, wkvb, cos, sin, block_rows, seqs):
    heads = wkvb.shape[1] // HEAD
    blocks = lat.shape[0] // block_rows
    rows = cq.shape[0]
    q_blocks = rows // block_rows
    vmem = pl.BlockSpec(memory_space=pltpu.VMEM)
    pairs = q_blocks * blocks * heads // 2
    return pl.pallas_call(
        functools.partial(forward_kernel, blocks, heads, seqs),
        out_shape=(
            jax.ShapeDtypeStruct((q_blocks, heads, block_rows, WIDE), jnp.bfloat16),
            jax.ShapeDtypeStruct((rows, heads * VDIM), jnp.float32),
            jax.ShapeDtypeStruct((rows, heads * VDIM), jnp.bfloat16),
            jax.ShapeDtypeStruct((q_blocks, 16 * -(-heads // 16), block_rows), jnp.float32),
        ),
        in_specs=[pl.BlockSpec(memory_space=pltpu.SMEM)] + [vmem] * 6,
        out_specs=(vmem,) * 4,
        scratch_shapes=[
            pltpu.VMEM((heads * HEAD, KVR), jnp.bfloat16),
            pltpu.VMEM((heads, block_rows, HEAD), jnp.bfloat16),
            pltpu.VMEM((block_rows, HEAD), jnp.bfloat16),
            pltpu.VMEM((heads, VDIM, block_rows), jnp.bfloat16),
            pltpu.VMEM((q_blocks, heads, 1, block_rows), jnp.float32),
            pltpu.VMEM((q_blocks, heads, 1, block_rows), jnp.float32),
            pltpu.VMEM((q_blocks, heads, VDIM, block_rows), jnp.float32),
            pltpu.VMEM((block_rows, block_rows), jnp.float32),
        ],
        compiler_params=pltpu.CompilerParams(vmem_limit_bytes=VMEM_LIMIT),
        cost_estimate=pl.CostEstimate(
            flops=pairs * 4 * block_rows * block_rows * WIDE,
            bytes_accessed=16 * 1024 * 1024,
            transcendentals=pairs * block_rows * block_rows,
        ),
        name="attention_forward",
    )(meta, cq, wqb, lat, wkvb, cos, sin)


def three_terms(column):
    first = column.astype(jnp.bfloat16).astype(jnp.float32)
    rest = column - first
    second = rest.astype(jnp.bfloat16).astype(jnp.float32)
    return first, second, rest - second


def fold_in(tile, column, lane):
    for k, term in enumerate(three_terms(column)):
        tile = jnp.where(lane == FOLD_AT + k, term, tile)
    return tile


def backward_kernel(
    blocks, heads, seqs, meta, qx, u_in, o_in, dob, lat, wkvb, cos, sin, dq_out, dlat, gkvb,
    xs, xr, qo, qt, dt, dq, dkv, dkpe, gsum, bias,
):
    block_rows = bias.shape[0]
    q_blocks = qx.shape[0]
    starts = [meta[blocks + s] for s in range(seqs)]
    own = [meta[blocks + seqs + j] for j in range(q_blocks)]
    lane = lax.broadcasted_iota(jnp.int32, (block_rows, HEAD), 1)
    for j in range(q_blocks):
        here = pl.ds(j * block_rows, block_rows)
        logs = u_in[j].T
        for first, last in head_groups(heads):
            d_pair = dob[here, first * VDIM : first * VDIM + HEAD].astype(jnp.float32)
            weighted = d_pair * o_in[here, first * VDIM : first * VDIM + HEAD]
            turned = pltpu.roll(d_pair, VDIM, 1)
            for h in range(first, last):
                mine = lane < VDIM if h == first else lane >= VDIM
                delta = jnp.sum(jnp.where(mine, weighted, 0.0), axis=1, keepdims=True)
                d_head = jnp.where(lane >= VDIM, turned if h == first else d_pair, 0.0)
                q_first = qx[j, h, :, :HEAD].astype(jnp.float32)
                q_second = qx[j, h, :, HEAD:].astype(jnp.float32)
                qo[j, h, :block_rows, :HEAD] = qx[j, h, :, :HEAD]
                qo[j, h, :block_rows, HEAD:] = fold_in(q_second, -logs[:, h : h + 1], lane).astype(
                    jnp.bfloat16
                )
                qo[j, h, block_rows:, :HEAD] = d_head.astype(jnp.bfloat16)
                qo[j, h, block_rows:, HEAD:] = fold_in(
                    jnp.zeros((block_rows, HEAD), jnp.float32), -delta, lane
                ).astype(jnp.bfloat16)
                qt[j, h, :NOPE, :] = q_first.T[:NOPE, :].astype(jnp.bfloat16)
                qt[j, h, NOPE:, :] = q_second.T[:ROPE, :].astype(jnp.bfloat16)
                dt[j, h] = d_head.T[VDIM:, :].astype(jnp.bfloat16)
    dq[...] = jnp.zeros(dq.shape, jnp.float32)
    gsum[...] = jnp.zeros(gsum.shape, jnp.float32)

    def pair(j, masked):
        def one(h):
            keys = jnp.concatenate([xs[h], xr[...]], axis=1)
            both = dot_nt(qo[j, h], keys)
            scores = both[:block_rows] * EXP2_SCALE
            if masked:
                scores = scores + bias[...]
            probs = jnp.exp2(scores)
            d_scores = (probs * both[block_rows:]).astype(jnp.bfloat16)
            dq[j, h] += dot_nn(d_scores, keys)
            d_keys = dot_nn(qt[j, h], d_scores)
            dkv[h, :NOPE, :] += d_keys[:NOPE]
            dkpe[...] += d_keys[NOPE:]
            dkv[h, NOPE:, :] += dot_nn(dt[j, h], probs.astype(jnp.bfloat16))

        for h in range(heads):
            one(h)

    def step(r, carry):
        key_block = meta[r]
        kinds = [pair_kind(key_block, own[j], starts, block_rows) for j in range(q_blocks)]
        wanted = functools.reduce(jnp.logical_or, [k[0] for k in kinds])
        here = pl.ds(pl.multiple_of(r * block_rows, block_rows), block_rows)

        @pl.when(wanted)
        def _():
            latent = lat[here, :KVR]
            xr[...] = shared_key_tile(lat[here, KVR : KVR + ROPE], block_rows)
            for first, last in head_groups(heads):
                keys = dot_nn(latent, wkvb[:, first * HEAD : last * HEAD]).astype(jnp.bfloat16)
                for h in range(first, last):
                    xs[h] = keys[:, (h - first) * HEAD : (h - first + 1) * HEAD]
            dkv[...] = jnp.zeros(dkv.shape, jnp.float32)
            dkpe[...] = jnp.zeros(dkpe.shape, jnp.float32)

        for j in range(q_blocks):
            needed, whole = kinds[j]

            @pl.when(needed & whole)
            def _():
                pair(j, False)

            @pl.when(needed & jnp.logical_not(whole))
            def _():
                bias[...] = mask_bias(key_block, own[j], starts, block_rows, False)
                pair(j, True)

        @pl.when(wanted)
        def _():
            latent = lat[here, :KVR]
            d_latent = jnp.zeros((KVR, block_rows), jnp.float32)
            for h in range(heads):
                d_head = jnp.concatenate(
                    [dkv[h, :NOPE, :] * SCORE_SCALE, dkv[h, NOPE:, :]], axis=0
                ).astype(jnp.bfloat16)
                d_latent += dot_nn(wkvb[:, h * HEAD : (h + 1) * HEAD], d_head)
                gsum[h * HEAD : (h + 1) * HEAD, :] += dot_nn(d_head, latent)
            dlat[here, :KVR] = d_latent.T.astype(jnp.bfloat16)
            rope = jnp.concatenate(
                [dkpe[...] * SCORE_SCALE, jnp.zeros((HEAD - ROPE, block_rows), jnp.float32)], axis=0
            )
            dlat[here, KVR:] = rope.T[:, :ROPE].astype(jnp.bfloat16)

        @pl.when(jnp.logical_not(wanted))
        def _():
            dlat[here, :] = jnp.zeros((block_rows, KVR + ROPE), jnp.bfloat16)

        return carry

    lax.fori_loop(0, blocks, step, 0)
    for h in range(heads):
        gkvb[:, h * HEAD : (h + 1) * HEAD] = gsum[h * HEAD : (h + 1) * HEAD, :].T.astype(
            jnp.bfloat16
        )
    for j in range(q_blocks):
        here = pl.ds(j * block_rows, block_rows)
        cos_j, sin_j = cos[here, :], sin[here, :]
        for h in range(heads):
            nope = jnp.where(lane < NOPE, dq[j, h, :, :HEAD], 0.0)
            rope = dq[j, h, :, HEAD:]
            shifted = rope * sin_j
            left = pltpu.roll(shifted, HEAD - ROPE // 2, 1)
            right = pltpu.roll(shifted, ROPE // 2, 1)
            swapped = jnp.where(lane < ROPE // 2, left, jnp.where(lane < ROPE, -right, 0.0))
            back = pltpu.roll(rope * cos_j + swapped, NOPE, 1)
            dq_out[here, h * HEAD : (h + 1) * HEAD] = ((nope + back) * SCORE_SCALE).astype(
                jnp.bfloat16
            )


def attention_backward(meta, qx, u_in, o_in, dob, lat, wkvb, cos, sin, block_rows, seqs):
    heads = wkvb.shape[1] // HEAD
    blocks = lat.shape[0] // block_rows
    q_blocks = qx.shape[0]
    rows = q_blocks * block_rows
    odd = -(heads * VDIM) % HEAD
    if odd:
        o_in = jnp.pad(o_in, ((0, 0), (0, odd)))
        dob = jnp.pad(dob, ((0, 0), (0, odd)))
    vmem = pl.BlockSpec(memory_space=pltpu.VMEM)
    pairs = q_blocks * blocks * heads // 2
    return pl.pallas_call(
        functools.partial(backward_kernel, blocks, heads, seqs),
        out_shape=(
            jax.ShapeDtypeStruct((rows, heads * HEAD), jnp.bfloat16),
            jax.ShapeDtypeStruct((lat.shape[0], KVR + ROPE), jnp.bfloat16),
            jax.ShapeDtypeStruct((KVR, heads * HEAD), jnp.bfloat16),
        ),
        in_specs=[pl.BlockSpec(memory_space=pltpu.SMEM)] + [vmem] * 8,
        out_specs=(vmem,) * 3,
        scratch_shapes=[
            pltpu.VMEM((heads, block_rows, HEAD), jnp.bfloat16),
            pltpu.VMEM((block_rows, HEAD), jnp.bfloat16),
            pltpu.VMEM((q_blocks, heads, 2 * block_rows, WIDE), jnp.bfloat16),
            pltpu.VMEM((q_blocks, heads, NOPE + ROPE, block_rows), jnp.bfloat16),
            pltpu.VMEM((q_blocks, heads, VDIM, block_rows), jnp.bfloat16),
            pltpu.VMEM((q_blocks, heads, block_rows, WIDE), jnp.float32),
            pltpu.VMEM((heads, HEAD, block_rows), jnp.float32),
            pltpu.VMEM((ROPE, block_rows), jnp.float32),
            pltpu.VMEM((heads * HEAD, KVR), jnp.float32),
            pltpu.VMEM((block_rows, block_rows), jnp.float32),
        ],
        compiler_params=pltpu.CompilerParams(vmem_limit_bytes=VMEM_LIMIT),
        cost_estimate=pl.CostEstimate(
            flops=pairs * 8 * block_rows * block_rows * WIDE,
            bytes_accessed=24 * 1024 * 1024,
            transcendentals=pairs * block_rows * block_rows,
        ),
        name="attention_backward",
    )(meta, qx, u_in, o_in, dob, lat, wkvb, cos, sin)


def dot_plain(left_op, right_op):
    return jnp.dot(left_op, right_op, preferred_element_type=jnp.float32)


def dot_rows(left_op, right_op):
    return lax.dot_general(
        left_op, right_op, (((0,), (0,)), ((), ())), preferred_element_type=jnp.float32
    )


def dot_cols(left_op, right_op):
    return lax.dot_general(
        left_op, right_op, (((1,), (1,)), ((), ())), preferred_element_type=jnp.float32
    )


def rms_scale(values):
    return lax.rsqrt(jnp.mean(values * values, axis=-1, keepdims=True) + EPSILON)


def rms_back(incoming, values, inv_rms, gain_vec):
    weighted = incoming * gain_vec
    d_values = inv_rms * weighted - values * inv_rms**3 * jnp.mean(
        weighted * values, axis=-1, keepdims=True
    )
    return (d_values, jnp.sum(incoming * values * inv_rms, axis=0))


def token_places(block_map, doc_lengths, per_device, devices):
    all_rows = per_device * devices
    half_block = per_device // 2
    token_rows = jnp.arange(all_rows, dtype=jnp.int32)
    device_of = token_rows // per_device
    within = token_rows % per_device
    wanted = device_of * 2 + within // half_block
    select = wanted[:, None] == jnp.arange(2 * devices, dtype=jnp.int32)[None, :]
    blocks = jnp.sum(jnp.where(select, block_map.reshape(-1)[None, :], 0), axis=1)
    places = blocks * half_block + within % half_block
    ends = jnp.cumsum(doc_lengths)
    segment = jnp.sum((places[:, None] >= ends[None, :]).astype(jnp.int32), axis=1)
    starts = ends - doc_lengths
    picked = segment[:, None] == jnp.arange(doc_lengths.shape[0], dtype=jnp.int32)[None, :]
    begins = jnp.sum(jnp.where(picked, starts[None, :], 0), axis=1)
    return (places, segment, places - begins)


def tables(inside):
    half_width = ROPE // 2
    frequency = ROPE_BASE ** (-2.0 * jnp.arange(half_width, dtype=jnp.float32) / ROPE)
    angles = inside.astype(jnp.float32)[:, None] * frequency[None, :]
    cosine_table = jnp.concatenate([jnp.cos(angles), jnp.cos(angles)], axis=1)
    sine_table = jnp.concatenate([jnp.sin(angles), jnp.sin(angles)], axis=1)
    return (cosine_table, sine_table)


def rotate(values, cosine_table, sine_table):
    half_width = values.shape[-1] // 2
    turned = jnp.concatenate([-values[..., half_width:], values[..., :half_width]], axis=-1)
    return values * cosine_table + turned * sine_table


def rotate_back(incoming, cosine_table, sine_table):
    half_width = incoming.shape[-1] // 2
    shifted = incoming * sine_table
    turned = jnp.concatenate([shifted[..., half_width:], -shifted[..., :half_width]], axis=-1)
    return incoming * cosine_table + turned


def wide_tables(inside):
    cosine_table, sine_table = tables(inside)
    rest = ((0, 0), (0, HEAD - ROPE))
    return cosine_table, sine_table, jnp.pad(cosine_table, rest), jnp.pad(sine_table, rest)


def sum_over_ctx(grad):
    return lax.psum_scatter(
        grad.astype(jnp.bfloat16), "ctx", scatter_dimension=0, tiled=True
    ).astype(jnp.float32)


def on_device(
    tokens_in,
    w_qa,
    w_kva,
    w_qb,
    w_kvb,
    w_out,
    w_gate,
    w_up,
    w_down,
    gain_in,
    gain_q,
    gain_kv,
    gain_mid,
    cotangent,
    block_map,
    doc_lengths,
):
    local_rows = tokens_in.shape[0]
    half_rows = local_rows // 2
    devices = lax.axis_size("ctx")
    ctx_index = lax.axis_index("ctx")
    seqs = doc_lengths.shape[0]
    own_blocks = lax.dynamic_slice_in_dim(block_map, ctx_index, 1, 0)[0]
    ends = jnp.cumsum(doc_lengths)
    starts = ends - doc_lengths
    meta = jnp.concatenate([block_map.reshape(-1), starts, own_blocks])
    within = jnp.arange(half_rows, dtype=jnp.int32)
    query_place = (own_blocks[:, None] * half_rows + within[None, :]).reshape(-1)
    began = jnp.max(
        jnp.where(starts[None, :] <= query_place[:, None], starts[None, :], 0), axis=1
    )
    cosine_table, sine_table, cosine_wide, sine_wide = wide_tables(query_place - began)
    head_count = w_qb.shape[1] // (NOPE + ROPE)
    w_qb_wide = jnp.pad(
        w_qb.reshape(-1, head_count, NOPE + ROPE), ((0, 0), (0, 0), (0, HEAD - NOPE - ROPE))
    ).reshape(-1, head_count * HEAD)
    tokens_f = tokens_in.astype(jnp.float32)
    scale_in = rms_scale(tokens_f)
    normed_in = (tokens_f * scale_in * gain_in).astype(jnp.bfloat16)
    kv_input = dot_plain(normed_in, w_kva)
    latent_raw = kv_input[:, :KVR]
    scale_kv = rms_scale(latent_raw)
    latent = (latent_raw * scale_kv * gain_kv).astype(jnp.bfloat16)
    key_rope = rotate(kv_input[:, KVR:], cosine_table, sine_table).astype(jnp.bfloat16)
    latents = lax.all_gather(
        jnp.concatenate([latent, key_rope], axis=1), "ctx", axis=0, tiled=True
    )
    q_latent_pre = dot_plain(normed_in, w_qa)
    scale_q = rms_scale(q_latent_pre)
    q_latent = (q_latent_pre * scale_q * gain_q).astype(jnp.bfloat16)
    queries, attn_f, heads_out, log_totals = attention_forward(
        meta, q_latent, w_qb_wide, latents, w_kvb, cosine_wide, sine_wide, half_rows, seqs
    )
    attention = lax.psum(dot_cols(heads_out, w_out).astype(jnp.bfloat16), "tp").astype(jnp.float32)
    middle = tokens_f + RESIDUAL_SCALE * attention
    scale_mid = rms_scale(middle)
    normed_mid = (middle * scale_mid * gain_mid).astype(jnp.bfloat16)
    gate_val = dot_plain(normed_mid, w_gate)
    up_val = dot_plain(normed_mid, w_up)
    sig_gate = jax.nn.sigmoid(gate_val)
    silu_gate = gate_val * sig_gate
    activation = (silu_gate * up_val).astype(jnp.bfloat16)
    feed_out = lax.psum(dot_cols(activation, w_down).astype(jnp.bfloat16), "tp").astype(jnp.float32)
    out = (middle + RESIDUAL_SCALE * feed_out).astype(jnp.bfloat16)
    cotangent_f = cotangent.astype(jnp.float32)
    d_feed = (RESIDUAL_SCALE * cotangent_f).astype(jnp.bfloat16)
    gw_down = dot_rows(d_feed, activation)
    d_activation = dot_plain(d_feed, w_down)
    d_gate = (d_activation * up_val * sig_gate * (1.0 + gate_val * (1.0 - sig_gate))).astype(
        jnp.bfloat16
    )
    d_up = (d_activation * silu_gate).astype(jnp.bfloat16)
    gw_gate = dot_rows(normed_mid, d_gate)
    gw_up = dot_rows(normed_mid, d_up)
    d_normed_mid = lax.psum(
        (dot_cols(d_gate, w_gate) + dot_cols(d_up, w_up)).astype(jnp.bfloat16), "tp"
    ).astype(jnp.float32)
    d_middle_norm, d_gain_mid = rms_back(d_normed_mid, middle, scale_mid, gain_mid)
    d_middle = cotangent_f + d_middle_norm
    d_attention = (RESIDUAL_SCALE * d_middle).astype(jnp.bfloat16)
    gw_out = dot_rows(d_attention, heads_out)
    d_heads = dot_plain(d_attention, w_out).astype(jnp.bfloat16)
    d_query_pre, d_latents, gw_kvb = attention_backward(
        meta, queries, log_totals, attn_f, d_heads, latents, w_kvb, cosine_wide, sine_wide,
        half_rows, seqs,
    )
    d_latent_part = lax.psum_scatter(d_latents, "ctx", scatter_dimension=0, tiled=True)
    gw_qb = dot_rows(q_latent, d_query_pre)
    d_q_latent = dot_cols(d_query_pre, w_qb_wide).astype(jnp.bfloat16)
    summed_tp = lax.psum(jnp.concatenate([d_q_latent, d_latent_part], axis=1), "tp").astype(
        jnp.float32
    )
    q_rank = w_qa.shape[1]
    d_q_latent = summed_tp[:, :q_rank]
    d_latent = summed_tp[:, q_rank : q_rank + KVR]
    d_rope_sum = summed_tp[:, q_rank + KVR :]
    d_q_pre, d_gain_q = rms_back(d_q_latent, q_latent_pre, scale_q, gain_q)
    d_q_low = d_q_pre.astype(jnp.bfloat16)
    d_latent_raw, d_gain_kv = rms_back(d_latent, latent_raw, scale_kv, gain_kv)
    d_kv_input = jnp.concatenate(
        [d_latent_raw, rotate_back(d_rope_sum, cosine_table, sine_table)], axis=-1
    ).astype(jnp.bfloat16)
    gw_qa = dot_rows(normed_in, d_q_low)
    gw_kva = dot_rows(normed_in, d_kv_input)
    d_normed_in = dot_cols(d_q_low, w_qa) + dot_cols(d_kv_input, w_kva)
    d_tokens_norm, d_gain_in = rms_back(d_normed_in, tokens_f, scale_in, gain_in)
    grad_in = d_middle + d_tokens_norm
    gw_qb_own = sum_over_ctx(gw_qb)
    gw_qb_own = gw_qb_own.reshape(-1, head_count, HEAD)[..., : NOPE + ROPE].reshape(
        -1, head_count * (NOPE + ROPE)
    )
    return (
        out,
        grad_in,
        sum_over_ctx(gw_qa),
        sum_over_ctx(gw_kva),
        gw_qb_own,
        sum_over_ctx(gw_kvb),
        sum_over_ctx(gw_out),
        sum_over_ctx(gw_gate),
        sum_over_ctx(gw_up),
        sum_over_ctx(gw_down),
        sum_over_ctx(d_gain_in),
        sum_over_ctx(d_gain_q),
        sum_over_ctx(d_gain_kv),
        sum_over_ctx(d_gain_mid),
    )


def solution(mesh):
    return jax.shard_map(
        on_device,
        mesh=mesh,
        in_specs=(
            P("ctx", None),
            P(),
            P(),
            P(None, "tp"),
            P(None, "tp"),
            P(None, "tp"),
            P(None, "tp"),
            P(None, "tp"),
            P(None, "tp"),
            P(),
            P(),
            P(),
            P(),
            P("ctx", None),
            P(),
            P(),
        ),
        out_specs=(
            P("ctx", None),
            P("ctx", None),
            P("ctx", None),
            P("ctx", None),
            P("ctx", "tp"),
            P("ctx", "tp"),
            P("ctx", "tp"),
            P("ctx", "tp"),
            P("ctx", "tp"),
            P("ctx", "tp"),
            P("ctx"),
            P("ctx"),
            P("ctx"),
            P("ctx"),
        ),
        check_vma=False,
    )
```

time: 1360 us -> 1110 us (0.82)
  matrix products: 455 us -> 125 us
  waiting for transfers between devices: 694 us -> 770 us
  Pallas kernels: 0 us -> 74.2 us
  other arithmetic: 116 us -> 68.7 us
  blocking collectives: 54.7 us -> 23.7 us
  local copies, waits for them, and re-layouts: 13.4 us -> 30.2 us
    dot_general x11 -> x0, matrix products: 314 us -> none  [the longest x1 56.6 us: scores_of(): jnp.einsum('qhd,kd->hqk', query_rope, rope_rows, preferred_element_type=j...]
    pallas_call x0 -> x2, Pallas kernels: none -> 74.2 us  [the longest x1 39.7 us: attention_backward(): pl.pallas_call(functools.partial(backward_kernel, blocks, heads, seqs), o...]
    reduce_sum x5 -> x0, other arithmetic: 37.4 us -> none  [the longest x1 35.5 us: on_device(): run_total = jnp.sum(terms, axis=-1)]
    reduce_scatter x9 -> x8, waiting for transfers between devices: 370 us -> 393 us  [the longest x7 342 us: sum_over_ctx(): lax.psum_scatter(grad.astype(jnp.bfloat16), 'ctx', scatter_dimension=0, t...]
    psum x1, waiting for transfers between devices: 104 us -> 126 us  [on_device(): lax.psum(dot_cols(heads_out, w_out).astype(jnp.bfloat16), 'tp')]
    psum x1 -> x0, blocking collectives: 20.2 us -> none  [on_device(): lax.psum(rope_own.astype(jnp.bfloat16), 'tp').astype(jnp.float32)]
    dot_general x8 -> x6, matrix products: 46.7 us -> 36.4 us  [dot_plain(): return jnp.dot(left_op, right_op, preferred_element_type=jnp.float32)]
  transfers between devices with their start and end apart: 14 -> 13, of which waited for: 12 -> 11; matrix products, arithmetic and copies ran while one was open for 12% -> 12% of each run, Pallas kernels for 0% -> 0%
where the time goes in v1:
time: 1110 us
  waiting for transfers between devices  770 us (69%)
  matrix products  125 us (11%)
  Pallas kernels  74.2 us (7%)
  other arithmetic  68.7 us (6%)
  local copies, waits for them, and re-layouts  30.2 us (3%)
  blocking collectives  23.7 us (2%)
  between operations  16.7 us (2%)
    reduce_scatter x7, waiting for transfers between devices, sum_over_ctx(): lax.psum_scatter(grad.astype(jnp.bfloat16), 'ctx', scatter_dimension=0, t...  342 us
    psum x1, waiting for transfers between devices, on_device(): lax.psum(dot_cols(activation, w_down).astype(jnp.bfloat16), 'tp')  133 us
    psum x1, waiting for transfers between devices, on_device(): lax.psum(dot_cols(heads_out, w_out).astype(jnp.bfloat16), 'tp')  126 us
    psum x1, waiting for transfers between devices, on_device(): lax.psum((dot_cols(d_gate, w_gate) + dot_cols(d_up, w_up)).astype(jnp.bfl...  103 us
    reduce_scatter x1, waiting for transfers between devices, on_device(): lax.psum_scatter(d_latents, 'ctx', scatter_dimension=0, tiled=True)  51.1 us
    dot_general x7, matrix products, dot_rows(): lax.dot_general(left_op, right_op, (((0,), (0,)), ((), ())), preferred_el...  48.7 us
    dot_general x7, matrix products, dot_cols(): lax.dot_general(left_op, right_op, (((1,), (1,)), ((), ())), preferred_el...  40 us
    pallas_call x1, Pallas kernels, attention_backward(): pl.pallas_call(functools.partial(backward_kernel, blocks, heads, seqs), o...  39.7 us
  transfers between devices with their start and end apart: 13, of which 11 were waited for; matrix products, arithmetic and copies ran while one was open for 12% of the time, Pallas kernels for 0%

profile of v1, /device:TPU:0, one launch (start us, length us, event | category | flops | bytes accessed | tf_op | source)
XLA Modules:
  0.0 1110.4 jit_solution(3082971159707793624)
XLA Ops:
  38.5 4.0 copy.80.wqb
  43.7 5.3 multiply_reduce_fusion.3
  51.3 14.5 %all-gather.2.cloned.1.call-done.lat = bf16[4096,288]{1,0:T(8,128)(2,1)} async-done(((bf16[512,288]{1,0:T(8,128)(2,1)}), bf16[4096,288]{1,0:T(8,128)(2,1)}) %all-gather.2.cloned.1.call-update) | async-done | bytes 2359312 | tf_op jit(solution)/shard_map/all_gather | solution.py:521
  65.9 34.5 %attention_forward.1 = (bf16[2,10,256,256]{3,2,1,0:T(8,128)(2,1)}, f32[512,640]{1,0:T(8,128)}, bf16[512,640]{1,0:T(8,128)(2,1)}, f32[2,16,256]{2,1,0:T(8,128)}) custom-call(s32[22]{0:T(128)} %pad_add_fusion.meta, bf16[512,768]{1,0:T(8,128)(2,1)} %multiply_convert_fusion.5.cq, bf16[768,1280]{1,0:T(8,128)(2,1)} %copy.80.wqb, ...), custom_call_target="tpu_custom_call" | custom-call | flops 10737418240 | bytes 16777216 | tf_op jit(solution)/shard_map/attention_forward/pallas_call | solution.py:185
  100.3 4.8 convolution_convert_fusion.5
  105.2 125.9 %all-reduce.13.cloned.1.call-done = bf16[512,2560]{1,0:T(8,128)(2,1)} async-done(((bf16[512,2560]{1,0:T(8,128)(2,1)}), bf16[512,2560]{1,0:T(8,128)(2,1)}) %all-reduce.13.cloned.1.call-update) | async-done | bytes 2621456 | tf_op jit(solution)/shard_map/psum | solution.py:530
  237.0 7.8 fusion.34
  244.8 6.4 fusion.35
  251.3 10.7 multiply_convert_fusion.2
  262.0 8.7 fusion.36
  270.7 6.5 add_convert_fusion
  277.3 103.2 %all-reduce.15.cloned.1.call-done = bf16[512,2560]{1,0:T(8,128)(2,1)} async-done(((bf16[512,2560]{1,0:T(8,128)(2,1)}), bf16[512,2560]{1,0:T(8,128)(2,1)}) %all-reduce.15.cloned.1.call-update) | async-done | bytes 2621456 | tf_op jit(solution)/shard_map/psum | solution.py:551
  380.5 6.8 fusion.6
  387.3 4.0 convert_add_fusion.1
  394.4 39.7 %attention_backward.1 = (bf16[512,1280]{1,0:T(8,128)(2,1)}, bf16[4096,288]{1,0:T(8,128)(2,1)}, bf16[256,1280]{1,0:T(8,128)(2,1)}) custom-call(s32[22]{0:T(128)} %pad_add_fusion.meta, bf16[2,10,256,256]{3,2,1,0:T(8,128)(2,1)} %get-tuple-element.22.qx, f32[2,16,256]{2,1,0:T(8,128)} %get-tuple-element.23.u_in, f32[512,640]{1,0:T(8,128)} %get-tuple-element.24.o_in, ...), custom_call_target="tpu_custom_call" | custom-call | flops 21474836480 | bytes 25165824 | tf_op jit(solution)/shard_map/attention_backward/pallas_call | solution.py:365
  434.6 10.4 convolution_convert_fusion.6
  446.2 51.1 %reduce-scatter.12.cloned.1.call-done = bf16[512,288]{1,0:T(8,128)(2,1)} async-done(((bf16[4096,288]{1,0:T(8,128)(2,1)}), bf16[512,288]{1,0:T(8,128)(2,1)}) %reduce-scatter.12.cloned.1.call-update) | async-done | bytes 294928 | tf_op jit(solution)/shard_map/reduce_scatter | solution.py:563
  504.0 6.7 convolution_convert_fusion.4
  510.8 132.7 %all-reduce.17.cloned.1.call-done = (bf16[512,2560]{1,0:T(8,128)(2,1)}, bf16[512,1056]{1,0:T(8,128)(2,1)}) async-done(((bf16[512,2560]{1,0:T(8,128)(2,1)}, bf16[512,1056]{1,0:T(8,128)(2,1)}), (bf16[512,2560]{1,0:T(8,128)(2,1)}, bf16[512,1056]{1,0:T(8,128)(2,1)})) %all-reduce.17.cloned.1.call-update) | async-done | bytes 3702800 | tf_op jit(solution)/shard_map/psum | solution.py:539
  654.4 10.6 convolution_convert_fusion.2
  665.0 10.6 convolution_convert_fusion.1
  675.9 10.5 convolution_convert_fusion
  692.4 4.2 convolution_convert_fusion.3
  701.4 23.7 %reduce-scatter.16.cloned.1.call-done = bf16[96,1280]{1,0:T(8,128)(2,1)} async-done(((bf16[768,1280]{1,0:T(8,128)(2,1)}), bf16[96,1280]{1,0:T(8,128)(2,1)}) %reduce-scatter.16.cloned.1.call-update) | async-done | bytes 245776 | tf_op jit(solution)/shard_map/reduce_scatter | solution.py:471
  727.3 48.1 %reduce-scatter.20.cloned.1.call-done = bf16[320,640]{1,0:T(8,128)(2,1)} async-done(((bf16[2560,640]{1,0:T(8,128)(2,1)}), bf16[320,640]{1,0:T(8,128)(2,1)}) %reduce-scatter.20.cloned.1.call-update) | async-done | bytes 409616 | tf_op jit(solution)/shard_map/reduce_scatter | solution.py:471
  777.4 4.7 fusion.37
  785.8 23.7 %all-reduce.7 = (bf16[2560]{0:T(1024)(128)(2,1)S(1)}, bf16[768]{0:T(1024)(128)(2,1)S(1)}, bf16[256]{0:T(256)(128)(2,1)S(1)}, bf16[2560]{0:T(1024)(128)(2,1)S(1)}) all-reduce(bf16[2560]{0:T(1024)(128)(2,1)S(1)} %get-tuple-element.86, bf16[768]{0:T(1024)(128)(2,1)S(1)} %get-tuple-element.88, ...), channel_id=11, replica_groups=mesh['ctx'=8,'tp'=4] {'ctx'}, use_global_device_ids=true, to_apply=%region_24.25.clone | all-reduce | flops 6144 | bytes 24576
  812.0 9.1 fusion.12
  823.0 72.7 %reduce-scatter.22.cloned.1.call-done = bf16[320,1600]{1,0:T(8,128)(2,1)} async-done(((bf16[2560,1600]{1,0:T(8,128)(2,1)}), bf16[320,1600]{1,0:T(8,128)(2,1)}) %reduce-scatter.22.cloned.1.call-update) | async-done | bytes 1024016 | tf_op jit(solution)/shard_map/reduce_scatter | solution.py:471
  898.6 73.1 %reduce-scatter.24.cloned.1.call-done = bf16[320,1600]{1,0:T(8,128)(2,1)} async-done(((bf16[2560,1600]{1,0:T(8,128)(2,1)}), bf16[320,1600]{1,0:T(8,128)(2,1)}) %reduce-scatter.24.cloned.1.call-update) | async-done | bytes 1024016 | tf_op jit(solution)/shard_map/reduce_scatter | solution.py:471
  974.4 73.1 %reduce-scatter.26.cloned.1.call-done = bf16[320,1600]{1,0:T(8,128)(2,1)} async-done(((bf16[2560,1600]{1,0:T(8,128)(2,1)}), bf16[320,1600]{1,0:T(8,128)(2,1)}) %reduce-scatter.26.cloned.1.call-update) | async-done | bytes 1024016 | tf_op jit(solution)/shard_map/reduce_scatter | solution.py:471
  1050.3 51.3 %reduce-scatter.14.cloned.1.call-done = bf16[320,768]{1,0:T(8,128)(2,1)} async-done(((bf16[2560,768]{1,0:T(8,128)(2,1)}), bf16[320,768]{1,0:T(8,128)(2,1)}) %reduce-scatter.14.cloned.1.call-update) | async-done | bytes 491536 | tf_op jit(solution)/shard_map/reduce_scatter | solution.py:471
  (203 shorter events, 94.4 us)
Async XLA Ops:
  7.2 93.2 %copy-start = (bf16[2560,640]{1,0:T(8,128)(2,1)S(1)}, bf16[2560,640]{1,0:T(8,128)(2,1)}, u32[]{:S(2)}) copy-start(bf16[2560,640]{1,0:T(8,128)(2,1)} %param.21) | copy-start | bytes 9830404
  7.2 58.7 %all-gather.2.cloned.1.call-start = ((), (), s32[]{:S(2)}) async-start(), calls=%async_computation.9 | async-start | bytes 3538944 | tf_op jit(solution)/shard_map/all_gather | solution.py:521
  13.6 14.0 %copy-start.33 = (f32[256]{0:T(256)S(1)}, f32[256]{0:T(256)}, u32[]{:S(2)}) copy-start(f32[256]{0:T(256)} %param.27) | copy-start | bytes 3076
  15.4 8.3 copy-start.42
  30.7 200.5 %all-reduce.13.cloned.1.call-start = ((), (), s32[]{:S(2)}) async-start(), calls=%async_computation.10 | async-start | bytes 5242880 | tf_op jit(solution)/shard_map/psum | solution.py:530
  35.6 8.1 copy-start.22
  105.2 130.4 %copy-start.21 = (f32[2560]{0:T(1024)S(1)}, f32[2560]{0:T(1024)}, u32[]{:S(2)}) copy-start(f32[2560]{0:T(1024)} %param.28) | copy-start | bytes 30724
  105.2 275.3 %all-reduce.15.cloned.1.call-start = ((), (), s32[]{:S(2)}) async-start(), calls=%async_computation.11 | async-start | bytes 5242880 | tf_op jit(solution)/shard_map/psum | solution.py:551
  235.5 9.3 slice-start
  237.0 7.8 copy-start.16
  237.0 7.8 slice-start.1
  262.0 8.7 copy-start.46
  262.0 8.7 copy-start.14
  277.2 220.1 %reduce-scatter.12.cloned.1.call-start = ((), (), s32[]{:S(2)}) async-start(), calls=%async_computation.12 | async-start | bytes 3538944 | tf_op jit(solution)/shard_map/reduce_scatter | solution.py:563
  380.5 6.8 copy-start.6
  380.5 6.8 copy-start.12
  434.1 209.4 %all-reduce.17.cloned.1.call-start = ((), (), s32[]{:S(2)}) async-start(), calls=%async_computation.21 | async-start | bytes 7602176 | tf_op jit(solution)/shard_map/psum | solution.py:539
  434.5 10.4 copy-start.13
  434.6 10.4 copy-start.47
  446.2 53.9 %copy-start.19 = (bf16[512,768]{1,0:T(8,128)(2,1)S(1)}, bf16[512,768]{1,0:T(8,128)(2,1)}, u32[]{:S(2)}) copy-start(bf16[512,768]{1,0:T(8,128)(2,1)} %multiply_convert_fusion.5.cq) | copy-start | bytes 2359300
  499.4 200.4 %reduce-scatter.18.cloned.1.call-start = ((), (), s32[]{:S(2)}) async-start(), calls=%async_computation.15 | async-start | bytes 737280 | tf_op jit(solution)/shard_map/reduce_scatter | solution.py:471
  500.0 225.1 %reduce-scatter.16.cloned.1.call-start = ((), (), s32[]{:S(2)}) async-start(), calls=%async_computation.14 | async-start | bytes 2211840 | tf_op jit(solution)/shard_map/reduce_scatter | solution.py:471
  504.0 271.5 %reduce-scatter.20.cloned.1.call-start = ((), (), s32[]{:S(2)}) async-start(), calls=%async_computation.16 | async-start | bytes 3686400 | tf_op jit(solution)/shard_map/reduce_scatter | solution.py:471
  510.7 134.3 %copy-start.11 = (f32[512,256]{1,0:T(8,128)S(1)}, f32[512,256]{1,0:T(8,128)}, u32[]{:S(2)}) copy-start(f32[512,256]{1,0:T(8,128)} %copy.87) | copy-start | bytes 1572868
  510.7 134.3 %copy-start.34 = (f32[256]{0:T(256)S(1)}, f32[256]{0:T(256)}, u32[]{:S(2)}) copy-start(f32[256]{0:T(256)} %param.27) | copy-start | bytes 3076
  510.7 310.4 %reduce-scatter.28.cloned.1.call-start = ((), (), s32[]{:S(2)}) async-start(), calls=%async_computation.20 | async-start | bytes 2211840
  654.1 241.6 %reduce-scatter.22.cloned.1.call-start = ((), (), s32[]{:S(2)}) async-start(), calls=%async_computation.17 | async-start | bytes 9584640 | tf_op jit(solution)/shard_map/reduce_scatter | solution.py:471
  665.0 306.8 %reduce-scatter.24.cloned.1.call-start = ((), (), s32[]{:S(2)}) async-start(), calls=%async_computation.18 | async-start | bytes 9584640 | tf_op jit(solution)/shard_map/reduce_scatter | solution.py:471
  675.6 372.0 %reduce-scatter.26.cloned.1.call-start = ((), (), s32[]{:S(2)}) async-start(), calls=%async_computation.19 | async-start | bytes 9584640 | tf_op jit(solution)/shard_map/reduce_scatter | solution.py:471
  686.5 415.1 %reduce-scatter.14.cloned.1.call-start = ((), (), s32[]{:S(2)}) async-start(), calls=%async_computation.13 | async-start | bytes 4423680 | tf_op jit(solution)/shard_map/reduce_scatter | solution.py:471
  782.1 29.9 %copy-start.37 = (f32[512]{0:T(512)S(1)}, f32[512]{0:T(512)}, u32[]{:S(2)}) copy-start(f32[512]{0:T(512)} %get-tuple-element.111) | copy-start | bytes 6148
  895.8 207.9 %copy-start.1 = (bf16[2560,640]{1,0:T(8,128)(2,1)S(1)}, bf16[2560,640]{1,0:T(8,128)(2,1)}, u32[]{:S(2)}) copy-start(bf16[2560,640]{1,0:T(8,128)(2,1)} %param.21) | copy-start | bytes 9830404
  (31 other events, 101.0 us)
Sparse Core Ops, SparseCore 0:
  30.8 35.0 all-gather.1
  105.3 125.8 all-reduce.12
  277.3 103.1 all-reduce.14
  434.2 63.0 reduce-scatter.11
  500.9 142.5 all-reduce.16
  646.8 33.5 reduce-scatter.17
  684.8 40.2 reduce-scatter.15
  728.5 46.8 reduce-scatter.19
  779.4 40.5 reduce-scatter.27
  823.7 71.9 reduce-scatter.21
  899.7 72.0 reduce-scatter.23
  975.5 72.0 reduce-scatter.25
  1051.5 50.0 reduce-scatter.13

commit v2 on v1

--- a/solution.py
+++ b/solution.py
@@ -74,13 +74,22 @@
     return jnp.where(ones, 1.0, tile).astype(jnp.bfloat16)
 
 
+def head_window(h):
+    at = h * (NOPE + ROPE)
+    return at // HEAD * HEAD, at % HEAD
+
+
+def window_columns(heads):
+    return head_window(heads - 1)[0] + WIDE
+
+
 def head_groups(heads):
     return [(h, min(h + 2, heads)) for h in range(0, heads, 2)]
 
 
 def forward_kernel(
     blocks, heads, seqs, meta, cq, wqb, lat, wkvb, cos, sin, qx, o_out, ob_out, u_out,
-    wkvt, xs, xr, vt, top, total, acc, bias,
+    wkvt, xs, xr, vt, top, total, acc, bias, pre,
 ):
     rows_all = cq.shape[0]
     block_rows = bias.shape[0]
@@ -95,17 +104,20 @@
     for j in range(q_blocks):
         here = pl.ds(j * block_rows, block_rows)
         cos_j, sin_j = cos[here, :], sin[here, :]
-        for first, last in head_groups(heads):
-            pre = dot_nn(cq[here, :], wqb[:, first * HEAD : last * HEAD])
-            for h in range(first, last):
-                own_part = pre[:, (h - first) * HEAD : (h - first + 1) * HEAD]
-                turned = pltpu.roll(own_part, NOPE, 1)
-                left = pltpu.roll(turned, HEAD - ROPE // 2, 1)
-                right = pltpu.roll(turned, ROPE // 2, 1)
-                swapped = jnp.where(lane < ROPE // 2, -left, right)
-                rope = turned * cos_j + swapped * sin_j
-                qx[j, h, :, :HEAD] = jnp.where(lane < NOPE, own_part, 0.0).astype(jnp.bfloat16)
-                qx[j, h, :, HEAD:] = rope.astype(jnp.bfloat16)
+        width = heads * (NOPE + ROPE)
+        for at in range(0, width, WIDE):
+            end = min(at + WIDE, width)
+            pre[:, at:end] = dot_nn(cq[here, :], wqb[:, at:end])
+        for h in range(heads):
+            at, shift = head_window(h)
+            own_part = pltpu.roll(pre[:, at : at + WIDE], (WIDE - shift) % WIDE, 1)[:, :HEAD]
+            turned = pltpu.roll(own_part, NOPE, 1)
+            left = pltpu.roll(turned, HEAD - ROPE // 2, 1)
+            right = pltpu.roll(turned, ROPE // 2, 1)
+            swapped = jnp.where(lane < ROPE // 2, -left, right)
+            rope = jnp.where(lane < ROPE, turned * cos_j + swapped * sin_j, 0.0)
+            qx[j, h, :, :HEAD] = jnp.where(lane < NOPE, own_part, 0.0).astype(jnp.bfloat16)
+            qx[j, h, :, HEAD:] = rope.astype(jnp.bfloat16)
     top[...] = jnp.full(top.shape, MASKED, jnp.float32)
     total[...] = jnp.zeros(total.shape, jnp.float32)
     acc[...] = jnp.zeros(acc.shape, jnp.float32)
@@ -201,6 +213,7 @@
             pltpu.VMEM((q_blocks, heads, 1, block_rows), jnp.float32),
             pltpu.VMEM((q_blocks, heads, VDIM, block_rows), jnp.float32),
             pltpu.VMEM((block_rows, block_rows), jnp.float32),
+            pltpu.VMEM((block_rows, window_columns(heads)), jnp.float32),
         ],
         compiler_params=pltpu.CompilerParams(vmem_limit_bytes=VMEM_LIMIT),
         cost_estimate=pl.CostEstimate(
@@ -227,7 +240,7 @@
 
 def backward_kernel(
     blocks, heads, seqs, meta, qx, u_in, o_in, dob, lat, wkvb, cos, sin, dq_out, dlat, gkvb,
-    xs, xr, qo, qt, dt, dq, dkv, dkpe, gsum, bias,
+    xs, xr, qo, qt, dt, dq, dkv, dkpe, gsum, bias, flat,
 ):
     block_rows = bias.shape[0]
     q_blocks = qx.shape[0]
@@ -338,6 +351,7 @@
     for j in range(q_blocks):
         here = pl.ds(j * block_rows, block_rows)
         cos_j, sin_j = cos[here, :], sin[here, :]
+        flat[...] = jnp.zeros(flat.shape, jnp.float32)
         for h in range(heads):
             nope = jnp.where(lane < NOPE, dq[j, h, :, :HEAD], 0.0)
             rope = dq[j, h, :, HEAD:]
@@ -345,10 +359,11 @@
             left = pltpu.roll(shifted, HEAD - ROPE // 2, 1)
             right = pltpu.roll(shifted, ROPE // 2, 1)
             swapped = jnp.where(lane < ROPE // 2, left, jnp.where(lane < ROPE, -right, 0.0))
-            back = pltpu.roll(rope * cos_j + swapped, NOPE, 1)
-            dq_out[here, h * HEAD : (h + 1) * HEAD] = ((nope + back) * SCORE_SCALE).astype(
-                jnp.bfloat16
-            )
+            back = pltpu.roll(jnp.where(lane < ROPE, rope * cos_j + swapped, 0.0), NOPE, 1)
+            whole = jnp.concatenate([(nope + back) * SCORE_SCALE, jnp.zeros_like(nope)], axis=1)
+            at, shift = head_window(h)
+            flat[:, at : at + WIDE] += pltpu.roll(whole, shift, 1)
+        dq_out[here, :] = flat[:, : heads * (NOPE + ROPE)].astype(jnp.bfloat16)
 
 
 def attention_backward(meta, qx, u_in, o_in, dob, lat, wkvb, cos, sin, block_rows, seqs):
@@ -365,7 +380,7 @@
     return pl.pallas_call(
         functools.partial(backward_kernel, blocks, heads, seqs),
         out_shape=(
-            jax.ShapeDtypeStruct((rows, heads * HEAD), jnp.bfloat16),
+            jax.ShapeDtypeStruct((rows, heads * (NOPE + ROPE)), jnp.bfloat16),
             jax.ShapeDtypeStruct((lat.shape[0], KVR + ROPE), jnp.bfloat16),
             jax.ShapeDtypeStruct((KVR, heads * HEAD), jnp.bfloat16),
         ),
@@ -382,6 +397,7 @@
             pltpu.VMEM((ROPE, block_rows), jnp.float32),
             pltpu.VMEM((heads * HEAD, KVR), jnp.float32),
             pltpu.VMEM((block_rows, block_rows), jnp.float32),
+            pltpu.VMEM((block_rows, window_columns(heads)), jnp.float32),
         ],
         compiler_params=pltpu.CompilerParams(vmem_limit_bytes=VMEM_LIMIT),
         cost_estimate=pl.CostEstimate(
@@ -391,6 +407,302 @@
         ),
         name="attention_backward",
     )(meta, qx, u_in, o_in, dob, lat, wkvb, cos, sin)
+
+
+MESH = pl.DeviceIdType.MESH
+
+
+class Scatter:
+    def __init__(self, n, given=None, left=None, right=None):
+        self.operands = [given] if given is not None else [left, right]
+        self.is_given = given is not None
+        self.rows = self.operands[0].shape[0] // n
+        self.columns = self.operands[-1].shape[1]
+        self.depth = 0 if self.is_given else right.shape[0]
+        self.parts = 2 if self.rows % 32 == 0 else 1
+
+
+def scatter_blocks(bits_left):
+    chips = []
+    for value in range(1 << len(bits_left)):
+        chip = 0
+        for at, bit in enumerate(bits_left):
+            chip = chip + (((value >> at) & 1) << (bit - 1))
+        chips.append(chip)
+    return chips
+
+
+def scatter_kernel(n, items, *refs):
+    count = n.bit_length() - 1
+    me = lax.axis_index("ctx")
+    refs = list(refs)
+    take = lambda k: [refs.pop(0) for _ in range(k)]
+    inputs = [take(len(item.operands)) for item in items]
+    outputs = take(len(items))
+    held, sent, landed, core_sems, step_sems = [], [], [], [], []
+    for item in items:
+        held.append(refs.pop(0))
+        sent.append(None if item.is_given else refs.pop(0))
+        landed.append(take(count - 1))
+        core_sems.append(take(2))
+        step_sems.append([take(2) for _ in range(count - 1)])
+    barrier = pltpu.get_barrier_semaphore()
+    for bit in range(count):
+        pl.semaphore_signal(barrier, inc=1, device_id={"ctx": me ^ (1 << bit)}, device_id_type=MESH)
+    pl.semaphore_wait(barrier, count)
+    core = me & 1
+    chips = n // 2
+    orders = (tuple(range(1, count)), tuple(range(count - 1, 0, -1)))
+
+    def columns_of(item):
+        return [(c, min(c + 512, item.columns)) for c in range(0, item.columns, 512)]
+
+    def product(k, dest, first, last):
+        item = items[k]
+        left, right = inputs[k]
+        at = pl.ds(pl.multiple_of(dest * item.rows, 16), item.rows)
+        return dot_nn(left[at, :], right[:, first:last])
+
+    def core_copy(k, chip):
+        item = items[k]
+        if item.is_given:
+            at = pl.ds(pl.multiple_of((2 * chip + 1 - core) * item.rows, 16), item.rows)
+            source = inputs[k][0].at[at, :]
+        else:
+            source = sent[k].at[chip]
+        return pltpu.make_async_remote_copy(
+            src_ref=source,
+            dst_ref=held[k].at[chip],
+            send_sem=core_sems[k][0].at[chip],
+            recv_sem=core_sems[k][1].at[chip],
+            device_id={"ctx": me ^ 1},
+            device_id_type=MESH,
+        )
+
+    def step_copies(k, step):
+        item = items[k]
+        half = item.rows // item.parts
+        copies = []
+        for part, order in enumerate(orders[: item.parts]):
+            bit = order[step]
+            left = sorted(order[step + 1 :])
+            fixed = [b for b in order[:step]]
+            at = pl.ds(part * half, half)
+            for slot, free in enumerate(scatter_blocks(left)):
+                keep = free + ((me >> bit) & 1) * (1 << (bit - 1))
+                send = free + (1 - ((me >> bit) & 1)) * (1 << (bit - 1))
+                for b in fixed:
+                    own = ((me >> b) & 1) * (1 << (b - 1))
+                    keep, send = keep + own, send + own
+                copies.append(
+                    (
+                        pltpu.make_async_remote_copy(
+                            src_ref=held[k].at[send, at, :],
+                            dst_ref=landed[k][step].at[slot, at, :],
+                            send_sem=step_sems[k][step][0].at[part, slot],
+                            recv_sem=step_sems[k][step][1].at[part, slot],
+                            device_id={"ctx": me ^ (1 << bit)},
+                            device_id_type=MESH,
+                        ),
+                        keep,
+                        slot,
+                        at,
+                    )
+                )
+        return copies
+
+    def start_core(k):
+        item = items[k]
+
+        def body(chip, carry):
+            if not item.is_given:
+                for first, last in columns_of(item):
+                    sent[k][chip, :, first:last] = product(
+                        k, 2 * chip + 1 - core, first, last
+                    ).astype(jnp.bfloat16)
+            core_copy(k, chip).start()
+            return carry
+
+        lax.fori_loop(0, chips, body, 0)
+
+    def finish_core(k):
+        item = items[k]
+
+        def body(chip, carry):
+            core_copy(k, chip).wait_recv()
+            at = pl.ds(pl.multiple_of((2 * chip + core) * item.rows, 16), item.rows)
+            for first, last in columns_of(item):
+                if item.is_given:
+                    own = inputs[k][0][at, first:last].astype(jnp.float32)
+                else:
+                    own = product(k, 2 * chip + core, first, last)
+                total = own + held[k][chip, :, first:last].astype(jnp.float32)
+                held[k][chip, :, first:last] = total.astype(jnp.bfloat16)
+            return carry
+
+        lax.fori_loop(0, chips, body, 0)
+
+    def start_step(k, step):
+        for copy, _, _, _ in step_copies(k, step):
+            copy.start()
+
+    def finish_step(k, step):
+        item = items[k]
+        for copy, keep, slot, at in step_copies(k, step):
+            copy.wait_recv()
+            for first, last in columns_of(item):
+                total = held[k][keep, at, first:last].astype(jnp.float32) + landed[k][step][
+                    slot, at, first:last
+                ].astype(jnp.float32)
+                if step == count - 2:
+                    outputs[k][at, first:last] = total
+                else:
+                    held[k][keep, at, first:last] = total.astype(jnp.bfloat16)
+
+    every = range(len(items))
+    start_core(0)
+    for k in every:
+        if k + 1 < len(items):
+            start_core(k + 1)
+        finish_core(k)
+        start_step(k, 0)
+    for step in range(count - 1):
+        for k in every:
+            finish_step(k, step)
+            if step + 1 < count - 1:
+                start_step(k, step + 1)
+    for k in every:
+
+        def drain(chip, carry, k=k):
+            core_copy(k, chip).wait_send()
+            return carry
+
+        lax.fori_loop(0, chips, drain, 0)
+        for step in range(count - 1):
+            for copy, _, _, _ in step_copies(k, step):
+                copy.wait_send()
+
+
+def scatter_over_ctx(n, items, collective_id):
+    vmem = pl.BlockSpec(memory_space=pltpu.VMEM)
+    count = n.bit_length() - 1
+    scratch = []
+    flops = 0
+    for item in items:
+        scratch.append(pltpu.VMEM((n // 2, item.rows, item.columns), jnp.bfloat16))
+        if not item.is_given:
+            scratch.append(pltpu.VMEM((n // 2, item.rows, item.columns), jnp.bfloat16))
+        scratch += [
+            pltpu.VMEM((n >> (step + 2), item.rows, item.columns), jnp.bfloat16)
+            for step in range(count - 1)
+        ]
+        scratch += [pltpu.SemaphoreType.DMA((n // 2,))] * 2
+        for step in range(count - 1):
+            scratch += [pltpu.SemaphoreType.DMA((2, n >> (step + 2)))] * 2
+        flops += 2 * n * item.rows * item.columns * item.depth
+    operands = [array for item in items for array in item.operands]
+    return pl.pallas_call(
+        functools.partial(scatter_kernel, n, items),
+        out_shape=tuple(
+            jax.ShapeDtypeStruct((item.rows, item.columns), jnp.float32) for item in items
+        ),
+        in_specs=[vmem] * len(operands),
+        out_specs=(vmem,) * len(items),
+        scratch_shapes=scratch,
+        compiler_params=pltpu.CompilerParams(
+            vmem_limit_bytes=VMEM_LIMIT, collective_id=collective_id, has_side_effects=True
+        ),
+        cost_estimate=pl.CostEstimate(
+            flops=flops, bytes_accessed=64 * 1024 * 1024, transcendentals=0
+        ),
+        name=f"scatter_over_ctx_{collective_id}",
+    )(*operands)
+
+
+def gather_kernel(n, own, out, local_sem, step_sends, step_lands, core_sends, core_lands):
+    count = n.bit_length() - 1
+    me = lax.axis_index("ctx")
+    rows = own.shape[0]
+    half = rows // 2
+    barrier = pltpu.get_barrier_semaphore()
+    for bit in range(count):
+        pl.semaphore_signal(barrier, inc=1, device_id={"ctx": me ^ (1 << bit)}, device_id_type=MESH)
+    pl.semaphore_wait(barrier, count)
+    orders = (tuple(range(1, count)), tuple(range(count - 1, 0, -1)))
+    local = pltpu.make_async_copy(own, out.at[me], local_sem)
+    local.start()
+
+    def chip_copy(part, step, slot, block, first):
+        at = pl.ds(part * half, half)
+        return pltpu.make_async_remote_copy(
+            src_ref=own.at[at, :] if first else out.at[block, at, :],
+            dst_ref=out.at[block, at, :],
+            send_sem=step_sends.at[part, step, slot],
+            recv_sem=step_lands.at[part, step, slot],
+            device_id={"ctx": me ^ (1 << orders[part][step])},
+            device_id_type=MESH,
+        )
+
+    def core_copy(block, slot, first):
+        return pltpu.make_async_remote_copy(
+            src_ref=own if first else out.at[block],
+            dst_ref=out.at[block],
+            send_sem=core_sends.at[slot],
+            recv_sem=core_lands.at[slot],
+            device_id={"ctx": me ^ 1},
+            device_id_type=MESH,
+        )
+
+    started = []
+    core_copy(me, 0, True).start()
+    for step in range(count - 1):
+        for part, order in enumerate(orders):
+            for slot in range(1 << step):
+                flips = 0
+                for at in range(step):
+                    flips |= ((slot >> at) & 1) << order[at]
+                copy = chip_copy(part, step, slot, me ^ flips, slot == 0)
+                copy.start()
+                started.append(copy)
+        for part, order in enumerate(orders):
+            for slot in range(1 << step):
+                chip_copy(part, step, slot, me, slot == 0).wait_recv()
+    for chip in range(1, n // 2):
+        core_copy(me ^ (2 * chip), chip, False).start()
+    for chip in range(n // 2):
+        core_copy(me, chip, chip == 0).wait_recv()
+    for copy in started:
+        copy.wait_send()
+    for chip in range(n // 2):
+        core_copy(me, chip, chip == 0).wait_send()
+    local.wait()
+
+
+def gather_over_ctx(n, own, collective_id):
+    count = n.bit_length() - 1
+    vmem = pl.BlockSpec(memory_space=pltpu.VMEM)
+    slots = max(n // 4, 1)
+    gathered = pl.pallas_call(
+        functools.partial(gather_kernel, n),
+        out_shape=jax.ShapeDtypeStruct((n,) + own.shape, own.dtype),
+        in_specs=[vmem],
+        out_specs=vmem,
+        scratch_shapes=[
+            pltpu.SemaphoreType.DMA,
+            pltpu.SemaphoreType.DMA((2, count - 1, slots)),
+            pltpu.SemaphoreType.DMA((2, count - 1, slots)),
+            pltpu.SemaphoreType.DMA((n // 2,)),
+            pltpu.SemaphoreType.DMA((n // 2,)),
+        ],
+        compiler_params=pltpu.CompilerParams(
+            vmem_limit_bytes=VMEM_LIMIT, collective_id=collective_id, has_side_effects=True
+        ),
+        cost_estimate=pl.CostEstimate(
+            flops=0, bytes_accessed=16 * 1024 * 1024, transcendentals=0
+        ),
+        name=f"gather_over_ctx_{collective_id}",
+    )(own)
+    return gathered.reshape((-1,) + own.shape[1:])
 
 
 def dot_plain(left_op, right_op):
@@ -462,15 +774,12 @@
 
 
 def wide_tables(inside):
-    cosine_table, sine_table = tables(inside)
-    rest = ((0, 0), (0, HEAD - ROPE))
-    return cosine_table, sine_table, jnp.pad(cosine_table, rest), jnp.pad(sine_table, rest)
-
-
-def sum_over_ctx(grad):
-    return lax.psum_scatter(
-        grad.astype(jnp.bfloat16), "ctx", scatter_dimension=0, tiled=True
-    ).astype(jnp.float32)
+    half_width = ROPE // 2
+    lane = jnp.arange(HEAD, dtype=jnp.int32)
+    frequency = ROPE_BASE ** (-2.0 * (lane % half_width).astype(jnp.float32) / ROPE)
+    angles = inside.astype(jnp.float32)[:, None] * frequency[None, :]
+    used = lane[None, :] < ROPE
+    return jnp.where(used, jnp.cos(angles), 0.0), jnp.where(used, jnp.sin(angles), 0.0)
 
 
 def on_device(
@@ -505,11 +814,9 @@
     began = jnp.max(
         jnp.where(starts[None, :] <= query_place[:, None], starts[None, :], 0), axis=1
     )
-    cosine_table, sine_table, cosine_wide, sine_wide = wide_tables(query_place - began)
+    cosine_wide, sine_wide = wide_tables(query_place - began)
+    cosine_table, sine_table = cosine_wide[:, :ROPE], sine_wide[:, :ROPE]
     head_count = w_qb.shape[1] // (NOPE + ROPE)
-    w_qb_wide = jnp.pad(
-        w_qb.reshape(-1, head_count, NOPE + ROPE), ((0, 0), (0, 0), (0, HEAD - NOPE - ROPE))
-    ).reshape(-1, head_count * HEAD)
     tokens_f = tokens_in.astype(jnp.float32)
     scale_in = rms_scale(tokens_f)
     normed_in = (tokens_f * scale_in * gain_in).astype(jnp.bfloat16)
@@ -518,14 +825,12 @@
     scale_kv = rms_scale(latent_raw)
     latent = (latent_raw * scale_kv * gain_kv).astype(jnp.bfloat16)
     key_rope = rotate(kv_input[:, KVR:], cosine_table, sine_table).astype(jnp.bfloat16)
-    latents = lax.all_gather(
-        jnp.concatenate([latent, key_rope], axis=1), "ctx", axis=0, tiled=True
-    )
+    latents = gather_over_ctx(devices, jnp.concatenate([latent, key_rope], axis=1), 0)
     q_latent_pre = dot_plain(normed_in, w_qa)
     scale_q = rms_scale(q_latent_pre)
     q_latent = (q_latent_pre * scale_q * gain_q).astype(jnp.bfloat16)
     queries, attn_f, heads_out, log_totals = attention_forward(
-        meta, q_latent, w_qb_wide, latents, w_kvb, cosine_wide, sine_wide, half_rows, seqs
+        meta, q_latent, w_qb, latents, w_kvb, cosine_wide, sine_wide, half_rows, seqs
     )
     attention = lax.psum(dot_cols(heads_out, w_out).astype(jnp.bfloat16), "tp").astype(jnp.float32)
     middle = tokens_f + RESIDUAL_SCALE * attention
@@ -536,35 +841,58 @@
     sig_gate = jax.nn.sigmoid(gate_val)
     silu_gate = gate_val * sig_gate
     activation = (silu_gate * up_val).astype(jnp.bfloat16)
-    feed_out = lax.psum(dot_cols(activation, w_down).astype(jnp.bfloat16), "tp").astype(jnp.float32)
-    out = (middle + RESIDUAL_SCALE * feed_out).astype(jnp.bfloat16)
     cotangent_f = cotangent.astype(jnp.float32)
     d_feed = (RESIDUAL_SCALE * cotangent_f).astype(jnp.bfloat16)
-    gw_down = dot_rows(d_feed, activation)
     d_activation = dot_plain(d_feed, w_down)
     d_gate = (d_activation * up_val * sig_gate * (1.0 + gate_val * (1.0 - sig_gate))).astype(
         jnp.bfloat16
     )
     d_up = (d_activation * silu_gate).astype(jnp.bfloat16)
-    gw_gate = dot_rows(normed_mid, d_gate)
-    gw_up = dot_rows(normed_mid, d_up)
     d_normed_mid = lax.psum(
         (dot_cols(d_gate, w_gate) + dot_cols(d_up, w_up)).astype(jnp.bfloat16), "tp"
     ).astype(jnp.float32)
+    gw_gate, gw_up, gw_down = scatter_over_ctx(
+        devices,
+        [
+            Scatter(devices, left=normed_mid.T, right=d_gate),
+            Scatter(devices, left=normed_mid.T, right=d_up),
+            Scatter(devices, left=d_feed.T, right=activation),
+        ],
+        1,
+    )
+    activation_later, d_normed_mid = lax.optimization_barrier((activation, d_normed_mid))
+    feed_own = lax.psum_scatter(
+        dot_cols(activation_later, w_down).astype(jnp.bfloat16),
+        "tp",
+        scatter_dimension=0,
+        tiled=True,
+    ).astype(jnp.float32)
+    own_rows = feed_own.shape[0]
+    middle_own = lax.dynamic_slice_in_dim(middle, lax.axis_index("tp") * own_rows, own_rows, 0)
+    out = lax.all_gather(
+        (middle_own + RESIDUAL_SCALE * feed_own).astype(jnp.bfloat16), "tp", axis=0, tiled=True
+    )
     d_middle_norm, d_gain_mid = rms_back(d_normed_mid, middle, scale_mid, gain_mid)
     d_middle = cotangent_f + d_middle_norm
     d_attention = (RESIDUAL_SCALE * d_middle).astype(jnp.bfloat16)
-    gw_out = dot_rows(d_attention, heads_out)
     d_heads = dot_plain(d_attention, w_out).astype(jnp.bfloat16)
     d_query_pre, d_latents, gw_kvb = attention_backward(
         meta, queries, log_totals, attn_f, d_heads, latents, w_kvb, cosine_wide, sine_wide,
         half_rows, seqs,
     )
-    d_latent_part = lax.psum_scatter(d_latents, "ctx", scatter_dimension=0, tiled=True)
-    gw_qb = dot_rows(q_latent, d_query_pre)
-    d_q_latent = dot_cols(d_query_pre, w_qb_wide).astype(jnp.bfloat16)
-    summed_tp = lax.psum(jnp.concatenate([d_q_latent, d_latent_part], axis=1), "tp").astype(
-        jnp.float32
+    (d_latent_part,) = scatter_over_ctx(devices, [Scatter(devices, given=d_latents)], 2)
+    d_q_latent = dot_cols(d_query_pre, w_qb).astype(jnp.bfloat16)
+    summed_tp = lax.psum(
+        jnp.concatenate([d_q_latent, d_latent_part.astype(jnp.bfloat16)], axis=1), "tp"
+    ).astype(jnp.float32)
+    gw_out, gw_qb, gw_kvb = scatter_over_ctx(
+        devices,
+        [
+            Scatter(devices, left=d_attention.T, right=heads_out),
+            Scatter(devices, left=q_latent.T, right=d_query_pre),
+            Scatter(devices, given=gw_kvb),
+        ],
+        3,
     )
     q_rank = w_qa.shape[1]
     d_q_latent = summed_tp[:, :q_rank]
@@ -576,30 +904,43 @@
     d_kv_input = jnp.concatenate(
         [d_latent_raw, rotate_back(d_rope_sum, cosine_table, sine_table)], axis=-1
     ).astype(jnp.bfloat16)
-    gw_qa = dot_rows(normed_in, d_q_low)
-    gw_kva = dot_rows(normed_in, d_kv_input)
     d_normed_in = dot_cols(d_q_low, w_qa) + dot_cols(d_kv_input, w_kva)
     d_tokens_norm, d_gain_in = rms_back(d_normed_in, tokens_f, scale_in, gain_in)
     grad_in = d_middle + d_tokens_norm
-    gw_qb_own = sum_over_ctx(gw_qb)
-    gw_qb_own = gw_qb_own.reshape(-1, head_count, HEAD)[..., : NOPE + ROPE].reshape(
-        -1, head_count * (NOPE + ROPE)
-    )
+    gains = jnp.concatenate(
+        [g.reshape(devices, -1) for g in (d_gain_in, d_gain_mid, d_gain_q, d_gain_kv)], axis=1
+    )
+    lines = -(-gains.shape[1] // (32 * HEAD)) * 32
+    gains = jnp.pad(gains, ((0, 0), (0, lines * HEAD - gains.shape[1])))
+    gw_qa, gw_kva, gains = scatter_over_ctx(
+        devices,
+        [
+            Scatter(devices, left=normed_in.T, right=d_q_low),
+            Scatter(devices, left=normed_in.T, right=d_kv_input),
+            Scatter(devices, given=gains.astype(jnp.bfloat16).reshape(devices * lines, HEAD)),
+        ],
+        4,
+    )
+    gains = gains.reshape(-1)
+    ends = [0]
+    for whole in (d_gain_in, d_gain_mid, d_gain_q, d_gain_kv):
+        ends.append(ends[-1] + whole.shape[0] // devices)
+    own_gains = [gains[first:last] for first, last in zip(ends, ends[1:])]
     return (
         out,
         grad_in,
-        sum_over_ctx(gw_qa),
-        sum_over_ctx(gw_kva),
-        gw_qb_own,
-        sum_over_ctx(gw_kvb),
-        sum_over_ctx(gw_out),
-        sum_over_ctx(gw_gate),
-        sum_over_ctx(gw_up),
-        sum_over_ctx(gw_down),
-        sum_over_ctx(d_gain_in),
-        sum_over_ctx(d_gain_q),
-        sum_over_ctx(d_gain_kv),
-        sum_over_ctx(d_gain_mid),
+        gw_qa,
+        gw_kva,
+        gw_qb,
+        gw_kvb,
+        gw_out,
+        gw_gate,
+        gw_up,
+        gw_down,
+        own_gains[0],
+        own_gains[2],
+        own_gains[3],
+        own_gains[1],
     )
 
 

time: 1110 us -> 770 us (0.69); the launches traced: 1110 us -> 759 us
  waiting for transfers between devices: 770 us -> 223 us
  Pallas kernels: 74.2 us -> 326 us
  matrix products: 125 us -> 85.6 us
  local copies, waits for them, and re-layouts: 30.2 us -> 58.1 us
  blocking collectives: 23.7 us -> 0 us
  other arithmetic: 68.7 us -> 51.2 us
    reduce_scatter x8 -> x0, waiting for transfers between devices: 393 us -> none  [the longest x7 342 us: sum_over_ctx(): lax.psum_scatter(grad.astype(jnp.bfloat16), 'ctx', scatter_dimension=0, t...]
    pallas_call x0 -> x5, Pallas kernels: none -> 261 us  [the longest x4 236 us: scatter_over_ctx(): pl.pallas_call(functools.partial(scatter_kernel, n, items), out_shape=tup...]
    psum x1, waiting for transfers between devices: 133 us -> 0.01 us  [on_device(): lax.psum(jnp.concatenate([d_q_latent, d_latent_part.astype(jnp.bfloat16)]...]
    dot_general x7 -> x0, matrix products: 48.7 us -> none  [dot_rows(): lax.dot_general(left_op, right_op, (((0,), (0,)), ((), ())), preferred_el...]
    unnamed x107 -> x126, local copies, waits for them, and re-layouts: 12.3 us -> 38.6 us
    unnamed x1 -> x0, blocking collectives: 23.7 us -> none
    all_gather x1, waiting for transfers between devices: 14.5 us -> 0.02 us  [on_device(): lax.all_gather((middle_own + RESIDUAL_SCALE * feed_own).astype(jnp.bfloat...]
    add x2 -> x0, other arithmetic: 13.2 us -> none  [the longest x1 9.12 us: on_device(): grad_in = d_middle + d_tokens_norm]
  transfers between devices with their start and end apart: 13 -> 5, of which waited for: 11 -> 2; matrix products, arithmetic and copies ran while one was open for 12% -> 7% of each run, Pallas kernels for 0% -> 25%
where the time goes in v2:
time: 770 us; the launch traced here: 759 us
  Pallas kernels  326 us (42%)
  waiting for transfers between devices  223 us (29%)
  matrix products  85.6 us (11%)
  local copies, waits for them, and re-layouts  58.1 us (8%)
  other arithmetic  51.2 us (7%)
  between operations  14.6 us (2%)
    pallas_call x4, Pallas kernels, scatter_over_ctx(): pl.pallas_call(functools.partial(scatter_kernel, n, items), out_shape=tup...  236 us
    psum x1, waiting for transfers between devices, on_device(): lax.psum(dot_cols(heads_out, w_out).astype(jnp.bfloat16), 'tp')  119 us
    psum x1, waiting for transfers between devices, on_device(): lax.psum((dot_cols(d_gate, w_gate) + dot_cols(d_up, w_up)).astype(jnp.bfl...  103 us
    dot_general x7, matrix products, dot_cols(): lax.dot_general(left_op, right_op, (((1,), (1,)), ((), ())), preferred_el...  47.3 us
    unnamed x126, local copies, waits for them, and re-layouts  38.6 us
    dot_general x6, matrix products, dot_plain(): return jnp.dot(left_op, right_op, preferred_element_type=jnp.float32)  38.3 us
    pallas_call x1, Pallas kernels, attention_backward(): pl.pallas_call(functools.partial(backward_kernel, blocks, heads, seqs), o...  35.1 us
    pallas_call x1, Pallas kernels, attention_forward(): pl.pallas_call(functools.partial(forward_kernel, blocks, heads, seqs), ou...  30.4 us
  transfers between devices with their start and end apart: 5, of which 2 were waited for; matrix products, arithmetic and copies ran while one was open for 7% of the time, Pallas kernels for 25%

profile of v2, /device:TPU:0, one launch (start us, length us, event | category | flops | bytes accessed | tf_op | source)
XLA Modules:
  0.0 758.7 jit_solution(7345463201581626804)
XLA Ops:
  8.3 4.4 copy.132
  15.6 3.2 fusion.33
  32.4 24.5 %gather_over_ctx_0.1 = bf16[8,512,288]{2,1,0:T(8,128)(2,1)} custom-call(bf16[512,288]{1,0:T(8,128)(2,1)} %copy.135.own), custom_call_target="tpu_custom_call" | custom-call | bytes 16777216 | tf_op jit(solution)/shard_map/gather_over_ctx_0/pallas_call | solution.py:685
  56.9 5.7 multiply_reduce_fusion.5
  63.2 3.1 copy.134
  72.9 2.6 copy.137.wqb
  75.5 30.4 %attention_forward.1 = (bf16[2,10,256,256]{3,2,1,0:T(8,128)(2,1)}, f32[512,640]{1,0:T(8,128)}, bf16[512,640]{1,0:T(8,128)(2,1)}, f32[2,16,256]{2,1,0:T(8,128)}) custom-call(s32[22]{0:T(128)} %pad_add_fusion.meta, bf16[512,768]{1,0:T(8,128)(2,1)} %copy.136.cq, bf16[768,960]{1,0:T(8,128)(2,1)} %copy.137.wqb, bf16[4096,288]{1,0:T(8,128)(2,1)} %bitcast.39, ...), custom_call_target="tpu_custom_call" | custom-call | flops 10737418240 | bytes 16777216 | tf_op jit(solution)/shard_map/attention_forward/pallas_call | solution.py:197
  105.9 4.8 convolution_convert_fusion
  110.8 4.9 copy.144
  115.8 119.3 %all-reduce.5.cloned.1.call-done = bf16[512,2560]{0,1:T(8,128)(2,1)} async-done(((bf16[512,2560]{0,1:T(8,128)(2,1)}), bf16[512,2560]{0,1:T(8,128)(2,1)}) %all-reduce.5.cloned.1.call-update) | async-done | bytes 2621456 | tf_op jit(solution)/shard_map/psum | solution.py:835
  235.0 3.8 multiply_reduce_fusion.2
  241.6 8.4 %fusion.39 = f32[512,1600]{1,0:T(8,128)S(1)} fusion(bf16[512,2560]{0,1:T(8,128)(2,1)S(1)} %multiply_convert_fusion.1, bf16[2560,1600]{0,1:T(8,128)(2,1)} %param.22), kind=kOutput, calls=%fused_computation.105 | convolution fusion | flops 4194304000 | bytes 14090240 | tf_op jit(solution)/shard_map/dot_general | solution.py:709
  250.0 6.7 fusion.40
  256.7 11.1 %multiply_convert_fusion.2 = (bf16[512,1600]{1,0:T(8,128)(2,1)S(1)}, bf16[512,1600]{1,0:T(8,128)(2,1)}, bf16[512,1600]{1,0:T(8,128)(2,1)}) fusion(f32[512,1600]{1,0:T(8,128)S(1)} %fusion.39, f32[512,1600]{1,0:T(8,128)} %fusion.40, bf16[2560,1600]{0,1:T(8,128)(2,1)} %param.24, bf16[512,2560]{0,1:T(8,128)(2,1)S(1)} %copy-done.11), kind=kOutput, calls=%fused_computation.27 | convolution fusion | flops 4210524160 | bytes 22282240 | tf_op jit(solution)/shard_map/dot_general | solution.py:709
  267.9 8.5 %fusion.41 = f32[512,2560]{0,1:T(8,128)S(1)} fusion(bf16[512,1600]{1,0:T(8,128)(2,1)} %get-tuple-element.117.refs_1_, bf16[2560,1600]{0,1:T(8,128)(2,1)} %param.22), kind=kOutput, calls=%fused_computation.107 | convolution fusion | flops 4194304000 | bytes 15073280 | tf_op jit(solution)/shard_map/dot_general | solution.py:719
  276.4 11.5 %add_convert_fusion = bf16[512,2560]{0,1:T(8,128)(2,1)} fusion(f32[512,2560]{0,1:T(8,128)S(1)} %fusion.41, bf16[512,1600]{1,0:T(8,128)(2,1)S(1)} %get-tuple-element.116.refs_3_, bf16[2560,1600]{0,1:T(8,128)(2,1)} %param.23), kind=kOutput, calls=%fused_computation.21 | convolution fusion | flops 4196925440 | bytes 17694720 | tf_op jit(solution)/shard_map/dot_general | solution.py:719
  288.0 103.2 %all-reduce.7.cloned.1.call-done = bf16[512,2560]{0,1:T(8,128)(2,1)} async-done(((bf16[512,2560]{0,1:T(8,128)(2,1)}), bf16[512,2560]{0,1:T(8,128)(2,1)}) %all-reduce.7.cloned.1.call-update) | async-done | bytes 2621456 | tf_op jit(solution)/shard_map/psum | solution.py:851
  391.3 2.6 convert_element_type.108
  394.6 4.0 multiply_reduce_fusion
  398.5 5.4 fusion.14
  404.0 3.1 convolution_convert_fusion.3.dob
  407.1 35.1 %attention_backward.1 = (bf16[512,960]{1,0:T(8,128)(2,1)}, bf16[4096,288]{1,0:T(8,128)(2,1)}, bf16[256,1280]{1,0:T(8,128)(2,1)}) custom-call(s32[22]{0:T(128)} %pad_add_fusion.meta, bf16[2,10,256,256]{3,2,1,0:T(8,128)(2,1)} %get-tuple-element.35.qx, f32[2,16,256]{2,1,0:T(8,128)} %get-tuple-element.36.u_in, f32[512,640]{1,0:T(8,128)} %get-tuple-element.37.o_in, ...), custom_call_target="tpu_custom_call" | custom-call | flops 21474836480 | bytes 25165824 | tf_op jit(solution)/shard_map/attention_backward/pallas_call | solution.py:380
  442.2 43.4 %scatter_over_ctx_2.1 = f32[512,288]{1,0:T(8,128)} custom-call(bf16[4096,288]{1,0:T(8,128)(2,1)} %get-tuple-element.39.refs_0_), custom_call_target="tpu_custom_call" | custom-call | bytes 67108864 | tf_op jit(solution)/shard_map/scatter_over_ctx_2/pallas_call | solution.py:604
  490.3 10.4 %convolution_convert_fusion.1 = bf16[512,2560]{1,0:T(8,128)(2,1)} fusion(bf16[512,1600]{1,0:T(8,128)(2,1)} %get-tuple-element.33.refs_5_, bf16[2560,1600]{0,1:T(8,128)(2,1)} %param.24), kind=kOutput, calls=%fused_computation.26 | convolution fusion | flops 4195614720 | bytes 12451840 | tf_op jit(solution)/shard_map/dot_general | solution.py:719
  503.1 122.9 %scatter_over_ctx_1.1 = (f32[320,1600]{1,0:T(8,128)}, f32[320,1600]{1,0:T(8,128)}, f32[320,1600]{1,0:T(8,128)}) custom-call(bf16[2560,512]{1,0:T(8,128)(2,1)} %bitcast.41, bf16[512,1600]{1,0:T(8,128)(2,1)} %get-tuple-element.117.refs_1_, bf16[2560,512]{1,0:T(8,128)(2,1)} %bitcast.42, bf16[512,1600]{1,0:T(8,128)(2,1)} %copy-done.52, ...), custom_call_target="tpu_custom_call" | custom-call | flops 12582912000 | bytes 67108864 | tf_op jit(solution)/shard_map/scatter_over_ctx_1/pallas_call | solution.py:604
  626.1 33.7 %scatter_over_ctx_3.1 = (f32[320,640]{1,0:T(8,128)}, f32[96,960]{1,0:T(8,128)}, f32[32,1280]{1,0:T(8,128)}) custom-call(bf16[2560,512]{1,0:T(8,128)(2,1)} %get-tuple-element.114.refs_0_, bf16[512,640]{1,0:T(8,128)(2,1)} %get-tuple-element.32.refs_1_, bf16[768,512]{1,0:T(8,128)(2,1)} %fusion.64.refs_2_, bf16[512,960]{1,0:T(8,128)(2,1)} %get-tuple-element.38.refs_3_, ...), custom_call_target="tpu_custom_call" | custom-call | flops 2432696320 | bytes 67108864 | tf_op jit(solution)/shard_map/scatter_over_ctx_3/pallas_call | solution.py:604
  672.3 4.7 fusion.42
  677.1 5.1 fusion.9
  684.1 7.1 fusion.32
  691.2 36.3 %scatter_over_ctx_4.1 = (f32[320,768]{1,0:T(8,128)}, f32[320,288]{1,0:T(8,128)}, f32[32,128]{1,0:T(8,128)}) custom-call(bf16[2560,512]{1,0:T(8,128)(2,1)} %get-tuple-element.120.refs_0_.refs_2_, bf16[512,768]{1,0:T(8,128)(2,1)} %copy.161.refs_1_, bf16[2560,512]{1,0:T(8,128)(2,1)} %get-tuple-element.120.refs_0_.refs_2_, bf16[512,288]{1,0:T(8,128)(2,1)} %copy.162.refs_3_, ...), custom_call_target="tpu_custom_call" | custom-call | flops 2768240640 | bytes 67108864 | tf_op jit(solution)/shard_map/scatter_over_ctx_4/pallas_call | solution.py:604
  732.0 5.9 copy.164
  739.3 4.5 copy.163
  (192 shorter events, 63.7 us)
Async XLA Ops:
  7.2 98.7 %copy-start = (bf16[2560,640]{1,0:T(8,128)(2,1)S(1)}, bf16[2560,640]{1,0:T(8,128)(2,1)}, u32[]{:S(2)}) copy-start(bf16[2560,640]{1,0:T(8,128)(2,1)} %param.21) | copy-start | bytes 9830404
  7.2 227.8 %all-reduce.5.cloned.1.call-start = ((), (), s32[]{:S(2)}) async-start(), calls=%async_computation.1 | async-start | bytes 5242880 | tf_op jit(solution)/shard_map/psum | solution.py:835
  8.3 7.3 copy-start.29
  15.6 5.6 copy-start.51
  32.4 24.5 %copy-start.2 = (bf16[512,2560]{0,1:T(8,128)(2,1)S(1)}, bf16[512,2560]{0,1:T(8,128)(2,1)}, u32[]{:S(2)}) copy-start(bf16[512,2560]{0,1:T(8,128)(2,1)} %copy.132) | copy-start | bytes 7864324
  63.2 7.9 %copy-start.32 = (f32[512]{0:T(512)}, f32[512]{0:T(512)S(1)}, u32[]{:S(2)}) copy-start(f32[512]{0:T(512)S(1)} %get-tuple-element.136) | copy-start | bytes 6148
  63.2 7.9 %copy-start.39 = (s32[8,2]{1,0:T(8,128)S(1)}, s32[8,2]{1,0:T(8,128)}, u32[]{:S(2)}) copy-start(s32[8,2]{1,0:T(8,128)} %copy.133) | copy-start | bytes 196
  63.2 8.5 %copy-start.49 = (s32[4]{0:T(128)S(1)}, s32[4]{0:T(128)}, u32[]{:S(2)}) copy-start(s32[4]{0:T(128)} %copy-done.48) | copy-start | bytes 52
  110.8 280.5 %all-reduce.7.cloned.1.call-start = ((), (), s32[]{:S(2)}) async-start(), calls=%async_computation.2 | async-start | bytes 5242880 | tf_op jit(solution)/shard_map/psum | solution.py:851
  110.8 129.1 %copy-start.28 = (f32[2560]{0:T(1024)S(1)}, f32[2560]{0:T(1024)}, u32[]{:S(2)}) copy-start(f32[2560]{0:T(1024)} %param.28) | copy-start | bytes 30724
  240.0 10.1 %slice-start = ((s8[8192000]{0:T(1024)(128)(4,1)}), s8[4194304]{0:T(1024)(128)(4,1)S(1)}, s32[]{:S(2)}) async-start(s8[8192000]{0:T(1024)(128)(4,1)} %bitcast.48), calls=%async_computation.6 | async-start | bytes 8388608
  241.5 8.5 %copy-start.16 = (bf16[512,2560]{0,1:T(8,128)(2,1)}, bf16[512,2560]{0,1:T(8,128)(2,1)S(1)}, u32[]{:S(2)}) copy-start(bf16[512,2560]{0,1:T(8,128)(2,1)S(1)} %multiply_convert_fusion.1) | copy-start | bytes 7864324
  241.5 8.5 %slice-start.1 = ((s8[8192000]{0:T(1024)(128)(4,1)}), s8[3997696]{0:T(1024)(128)(4,1)S(1)}, s32[]{:S(2)}) async-start(s8[8192000]{0:T(1024)(128)(4,1)} %bitcast.48), calls=%async_computation.7 | async-start | bytes 7995392
  250.0 6.7 copy-start.11
  267.9 8.5 %copy-start.52 = (bf16[512,1600]{1,0:T(8,128)(2,1)}, bf16[512,1600]{1,0:T(8,128)(2,1)S(1)}, u32[]{:S(2)}) copy-start(bf16[512,1600]{1,0:T(8,128)(2,1)S(1)} %get-tuple-element.116.refs_3_) | copy-start | bytes 4915204
  288.0 372.5 %all-reduce.9.cloned.1.call-start = ((), (), s32[]{:S(2)}) async-start(), calls=%async_computation.4 | async-start | bytes 2162688 | tf_op jit(solution)/shard_map/psum | solution.py:885
  442.2 44.7 %copy-start.20 = (bf16[768,960]{0,1:T(8,128)(2,1)S(1)}, bf16[768,960]{0,1:T(8,128)(2,1)}, u32[]{:S(2)}) copy-start(bf16[768,960]{0,1:T(8,128)(2,1)} %param.19) | copy-start | bytes 4423684
  490.2 10.5 %copy-start.31 = (f32[768]{0:T(1024)S(1)}, f32[768]{0:T(1024)}, u32[]{:S(2)}) copy-start(f32[768]{0:T(1024)} %param.26) | copy-start | bytes 9220
  490.2 10.5 %copy-start.33 = (f32[512]{0:T(512)S(1)}, f32[512]{0:T(512)}, u32[]{:S(2)}) copy-start(f32[512]{0:T(512)} %copy-done.32) | copy-start | bytes 6148
  490.2 176.0 %reduce-scatter.4.cloned.1.call-start = ((), (), s32[]{:S(2)}) async-start(), calls=%async_computation.5 | async-start | bytes 3276800
  500.7 238.6 %all-gather.2.cloned.1.call-start = ((), (), s32[]{:S(2)}) async-start(), calls=%async_computation.3 | async-start | bytes 3276800 | tf_op jit(solution)/shard_map/all_gather | solution.py:872
  626.0 33.8 %copy-start.38 = (bf16[2560]{0:T(1024)(128)(2,1)S(1)}, bf16[2560]{0:T(1024)(128)(2,1)}, u32[]{:S(2)}) copy-start(bf16[2560]{0:T(1024)(128)(2,1)} %get-tuple-element.106) | copy-start | bytes 15364
  626.0 36.0 %copy-start.34 = (f32[512]{0:T(512)S(1)}, f32[512]{0:T(512)}, u32[]{:S(2)}) copy-start(f32[512]{0:T(512)} %get-tuple-element.134) | copy-start | bytes 6148
  626.0 36.0 %copy-start.40 = (f32[256]{0:T(256)S(1)}, f32[256]{0:T(256)}, u32[]{:S(2)}) copy-start(f32[256]{0:T(256)} %param.27) | copy-start | bytes 3076
  677.0 5.2 copy-start.47
  677.0 5.3 copy-start.45
  677.0 5.4 copy-start.37
  677.1 7.1 copy-start.42
  737.9 5.9 copy-start.22
  739.3 5.5 copy-start.24
  739.3 6.2 copy-start.25
  739.3 6.9 copy-start.23
  (28 other events, 95.4 us)
Sparse Core Ops, SparseCore 0:
  110.9 124.0 all-reduce.4
  288.1 103.1 all-reduce.6
  490.3 50.9 all-reduce.8
  543.4 51.5 reduce-scatter.3
  670.3 52.8 all-gather.1

commit v3 on v2

--- a/solution.py
+++ b/solution.py
@@ -860,18 +860,14 @@
         ],
         1,
     )
-    activation_later, d_normed_mid = lax.optimization_barrier((activation, d_normed_mid))
-    feed_own = lax.psum_scatter(
-        dot_cols(activation_later, w_down).astype(jnp.bfloat16),
-        "tp",
-        scatter_dimension=0,
-        tiled=True,
-    ).astype(jnp.float32)
+    feed_part = dot_cols(activation, w_down).astype(jnp.bfloat16)
+    d_normed_mid, feed_part, gw_gate, gw_up, gw_down = lax.optimization_barrier(
+        (d_normed_mid, feed_part, gw_gate, gw_up, gw_down)
+    )
+    feed_own = lax.psum_scatter(feed_part, "tp", scatter_dimension=0, tiled=True)
     own_rows = feed_own.shape[0]
     middle_own = lax.dynamic_slice_in_dim(middle, lax.axis_index("tp") * own_rows, own_rows, 0)
-    out = lax.all_gather(
-        (middle_own + RESIDUAL_SCALE * feed_own).astype(jnp.bfloat16), "tp", axis=0, tiled=True
-    )
+    out_own = (middle_own + RESIDUAL_SCALE * feed_own.astype(jnp.float32)).astype(jnp.bfloat16)
     d_middle_norm, d_gain_mid = rms_back(d_normed_mid, middle, scale_mid, gain_mid)
     d_middle = cotangent_f + d_middle_norm
     d_attention = (RESIDUAL_SCALE * d_middle).astype(jnp.bfloat16)
@@ -882,9 +878,9 @@
     )
     (d_latent_part,) = scatter_over_ctx(devices, [Scatter(devices, given=d_latents)], 2)
     d_q_latent = dot_cols(d_query_pre, w_qb).astype(jnp.bfloat16)
-    summed_tp = lax.psum(
-        jnp.concatenate([d_q_latent, d_latent_part.astype(jnp.bfloat16)], axis=1), "tp"
-    ).astype(jnp.float32)
+    before_tp = jnp.concatenate([d_q_latent, d_latent_part.astype(jnp.bfloat16)], axis=1)
+    before_tp, out_own = lax.optimization_barrier((before_tp, out_own))
+    summed_tp = lax.psum(before_tp, "tp")
     gw_out, gw_qb, gw_kvb = scatter_over_ctx(
         devices,
         [
@@ -894,6 +890,11 @@
         ],
         3,
     )
+    summed_tp, out_own, gw_out, gw_qb, gw_kvb = lax.optimization_barrier(
+        (summed_tp, out_own, gw_out, gw_qb, gw_kvb)
+    )
+    out = lax.all_gather(out_own, "tp", axis=0, tiled=True)
+    summed_tp = summed_tp.astype(jnp.float32)
     q_rank = w_qa.shape[1]
     d_q_latent = summed_tp[:, :q_rank]
     d_latent = summed_tp[:, q_rank : q_rank + KVR]

time: 770 us -> 723 us (0.939)
  waiting for transfers between devices: 223 us -> 142 us
  other arithmetic: 51.2 us -> 66.4 us
  local copies, waits for them, and re-layouts: 58.1 us -> 70.3 us
  matrix products: 85.6 us -> 93.9 us
    psum x1, waiting for transfers between devices: 103 us -> 0.02 us  [on_device(): lax.psum((dot_cols(d_gate, w_gate) + dot_cols(d_up, w_up)).astype(jnp.bfl...]
    psum x1, waiting for transfers between devices: 0.01 us -> 14.6 us  [on_device(): summed_tp = lax.psum(before_tp, 'tp')]
    dot_general x6, matrix products: 38.3 us -> 46.9 us  [dot_plain(): return jnp.dot(left_op, right_op, preferred_element_type=jnp.float32)]
    psum x1, waiting for transfers between devices: 119 us -> 127 us  [on_device(): lax.psum(dot_cols(heads_out, w_out).astype(jnp.bfloat16), 'tp')]
    unnamed x126 -> x108, local copies, waits for them, and re-layouts: 38.6 us -> 42 us
  transfers between devices with their start and end apart: 5 -> 5, of which waited for: 2 -> 2; matrix products, arithmetic and copies ran while one was open for 7% -> 13% of each run, Pallas kernels for 25% -> 38%
where the time goes in v3:
time: 723 us; the launch traced here: 715 us
  Pallas kernels  327 us (45%)
  waiting for transfers between devices  142 us (20%)
  matrix products  93.9 us (13%)
  local copies, waits for them, and re-layouts  70.3 us (10%)
  other arithmetic  66.4 us (9%)
  between operations  14.8 us (2%)
    pallas_call x4, Pallas kernels, scatter_over_ctx(): pl.pallas_call(functools.partial(scatter_kernel, n, items), out_shape=tup...  243 us
    psum x1, waiting for transfers between devices, on_device(): lax.psum(dot_cols(heads_out, w_out).astype(jnp.bfloat16), 'tp')  127 us
    dot_general x7, matrix products, dot_cols(): lax.dot_general(left_op, right_op, (((1,), (1,)), ((), ())), preferred_el...  47 us
    dot_general x6, matrix products, dot_plain(): return jnp.dot(left_op, right_op, preferred_element_type=jnp.float32)  46.9 us
    unnamed x108, local copies, waits for them, and re-layouts  42 us
    pallas_call x1, Pallas kernels, attention_backward(): pl.pallas_call(functools.partial(backward_kernel, blocks, heads, seqs), o...  32.2 us
    pallas_call x1, Pallas kernels, attention_forward(): pl.pallas_call(functools.partial(forward_kernel, blocks, heads, seqs), ou...  27.8 us
    pallas_call x1, Pallas kernels, gather_over_ctx(): pl.pallas_call(functools.partial(gather_kernel, n), out_shape=jax.ShapeDt...  24.3 us
  transfers between devices with their start and end apart: 5, of which 2 were waited for; matrix products, arithmetic and copies ran while one was open for 13% of the time, Pallas kernels for 38%

profile of v3, /device:TPU:0, one launch (start us, length us, event | category | flops | bytes accessed | tf_op | source)
XLA Modules:
  0.0 715.0 jit_solution(16270544623866705632)
XLA Ops:
  7.8 4.7 copy.132
  28.9 5.5 multiply_reduce_fusion.5
  37.2 24.3 %gather_over_ctx_0.1 = bf16[8,512,288]{2,1,0:T(8,128)(2,1)} custom-call(bf16[512,288]{1,0:T(8,128)(2,1)} %pad_maximum_fusion.1.own), custom_call_target="tpu_custom_call" | custom-call | bytes 16777216 | tf_op jit(solution)/shard_map/gather_over_ctx_0/pallas_call | solution.py:685
  62.6 27.8 %attention_forward.1 = (bf16[2,10,256,256]{3,2,1,0:T(8,128)(2,1)}, f32[512,640]{1,0:T(8,128)}, bf16[512,640]{1,0:T(8,128)(2,1)}, f32[2,16,256]{2,1,0:T(8,128)}) custom-call(s32[22]{0:T(128)} %pad_add_fusion.meta, bf16[512,768]{1,0:T(8,128)(2,1)} %multiply_convert_fusion.5.cq, bf16[768,960]{1,0:T(8,128)(2,1)} %copy.136.wqb, bf16[4096,288]{1,0:T(8,128)(2,1)} %bitcast.39, ...), custom_call_target="tpu_custom_call" | custom-call | flops 10737418240 | bytes 16777216 | tf_op jit(solution)/shard_map/attention_forward/pallas_call | solution.py:197
  90.4 4.8 convolution_convert_fusion
  95.3 4.6 copy.137
  99.9 127.4 %all-reduce.5.cloned.1.call-done = bf16[512,2560]{0,1:T(8,128)(2,1)} async-done(((bf16[512,2560]{0,1:T(8,128)(2,1)}), bf16[512,2560]{0,1:T(8,128)(2,1)}) %all-reduce.5.cloned.1.call-update) | async-done | bytes 2621456 | tf_op jit(solution)/shard_map/psum | solution.py:835
  227.4 3.8 multiply_reduce_fusion.2
  234.6 8.5 %fusion.40 = f32[512,1600]{0,1:T(8,128)} fusion(bf16[2560,1600]{0,1:T(8,128)(2,1)} %param.23, bf16[512,2560]{0,1:T(8,128)(2,1)S(1)} %multiply_convert_fusion.1), kind=kOutput, calls=%fused_computation.106 | convolution fusion | flops 4194304000 | bytes 14090240 | tf_op jit(solution)/shard_map/dot_general | solution.py:709
  243.1 4.6 copy.146
  247.7 12.2 %fusion.37 = (f32[512,1600]{0,1:T(8,128)}, f32[512,1600]{0,1:T(8,128)}) fusion(f32[512,1600]{0,1:T(8,128)} %fusion.40, bf16[2560,1600]{0,1:T(8,128)(2,1)} %param.24, bf16[512,2560]{0,1:T(8,128)(2,1)} %copy.137), kind=kOutput, calls=%fused_computation.103 | convolution fusion | flops 4199055360 | bytes 20643840 | tf_op jit(solution)/shard_map/dot_general | solution.py:709
  259.9 4.6 copy.140
  264.5 4.8 copy.143
  269.4 14.2 %multiply_convert_fusion.2 = (bf16[512,1600]{1,0:T(8,128)(2,1)}, bf16[512,1600]{1,0:T(8,128)(2,1)S(1)}, bf16[512,1600]{1,0:T(8,128)(2,1)S(1)}) fusion(f32[512,1600]{1,0:T(8,128)} %copy.146, f32[512,1600]{1,0:T(8,128)} %copy.140, f32[512,1600]{1,0:T(8,128)} %copy.143, bf16[512,2560]{0,1:T(8,128)(2,1)} %copy-done.14, bf16[2560,1600]{0,1:T(8,128)(2,1)} %param.22), kind=kOutput, calls=%fused_computation.27 | convolution fusion | flops 4205772800 | bytes 25559040 | tf_op jit(solution)/shard_map/dot_general | solution.py:709
  283.6 8.6 %fusion.38 = f32[512,2560]{0,1:T(8,128)S(1)} fusion(bf16[512,1600]{1,0:T(8,128)(2,1)S(1)} %get-tuple-element.152.refs_1_, bf16[2560,1600]{0,1:T(8,128)(2,1)} %param.22), kind=kOutput, calls=%fused_computation.104 | convolution fusion | flops 4194304000 | bytes 15073280 | tf_op jit(solution)/shard_map/dot_general | solution.py:719
  292.2 11.7 %add_convert_fusion = bf16[512,2560]{0,1:T(8,128)(2,1)} fusion(f32[512,2560]{0,1:T(8,128)S(1)} %fusion.38, bf16[512,1600]{1,0:T(8,128)(2,1)S(1)} %get-tuple-element.153.refs_3_, bf16[2560,1600]{0,1:T(8,128)(2,1)} %param.23), kind=kOutput, calls=%fused_computation.21 | convolution fusion | flops 4196925440 | bytes 17694720 | tf_op jit(solution)/shard_map/dot_general | solution.py:719
  304.0 3.8 fusion.11.refs_4_
  307.8 10.6 %convolution_convert_fusion.1 = bf16[512,2560]{1,0:T(8,128)(2,1)} fusion(bf16[512,1600]{1,0:T(8,128)(2,1)} %get-tuple-element.151.refs_5_, bf16[2560,1600]{0,1:T(8,128)(2,1)} %param.24), kind=kOutput, calls=%fused_computation.26 | convolution fusion | flops 4195614720 | bytes 12451840 | tf_op jit(solution)/shard_map/dot_general | solution.py:719
  318.4 124.2 %scatter_over_ctx_1.1 = (f32[320,1600]{1,0:T(8,128)}, f32[320,1600]{1,0:T(8,128)}, f32[320,1600]{1,0:T(8,128)}) custom-call(bf16[2560,512]{1,0:T(8,128)(2,1)} %bitcast.41, bf16[512,1600]{1,0:T(8,128)(2,1)} %copy-done.44, bf16[2560,512]{1,0:T(8,128)(2,1)} %bitcast.42, bf16[512,1600]{1,0:T(8,128)(2,1)} %copy-done.43, bf16[2560,512]{1,0:T(8,128)(2,1)} %fusion.11.refs_4_, ...), custom_call_target="tpu_custom_call" | custom-call | flops 12582912000 | bytes 67108864 | tf_op jit(solution)/shard_map/scatter_over_ctx_1/pallas_call | solution.py:604
  442.6 4.8 convert_element_type.107
  447.6 6.1 multiply_reduce_fusion
  454.4 6.3 fusion.14
  463.9 32.2 %attention_backward.1 = (bf16[512,960]{1,0:T(8,128)(2,1)}, bf16[4096,288]{1,0:T(8,128)(2,1)}, bf16[256,1280]{1,0:T(8,128)(2,1)}) custom-call(s32[22]{0:T(128)} %pad_add_fusion.meta, bf16[2,10,256,256]{3,2,1,0:T(8,128)(2,1)} %get-tuple-element.42.qx, f32[2,16,256]{2,1,0:T(8,128)} %get-tuple-element.43.u_in, f32[512,640]{1,0:T(8,128)} %get-tuple-element.44.o_in, ...), custom_call_target="tpu_custom_call" | custom-call | flops 21474836480 | bytes 25165824 | tf_op jit(solution)/shard_map/attention_backward/pallas_call | solution.py:380
  496.1 46.1 %scatter_over_ctx_2.1 = f32[512,288]{1,0:T(8,128)} custom-call(bf16[4096,288]{1,0:T(8,128)(2,1)} %get-tuple-element.51.refs_0_), custom_call_target="tpu_custom_call" | custom-call | bytes 67108864 | tf_op jit(solution)/shard_map/scatter_over_ctx_2/pallas_call | solution.py:604
  555.7 35.4 %scatter_over_ctx_3.1 = (f32[320,640]{1,0:T(8,128)}, f32[96,960]{1,0:T(8,128)}, f32[32,1280]{1,0:T(8,128)}) custom-call(bf16[2560,512]{1,0:T(8,128)(2,1)} %get-tuple-element.148.refs_0_, bf16[512,640]{1,0:T(8,128)(2,1)} %get-tuple-element.45.refs_1_, bf16[768,512]{1,0:T(8,128)(2,1)} %copy.148.refs_2_, bf16[512,960]{1,0:T(8,128)(2,1)} %get-tuple-element.50.refs_3_, ...), custom_call_target="tpu_custom_call" | custom-call | flops 2432696320 | bytes 67108864 | tf_op jit(solution)/shard_map/scatter_over_ctx_3/pallas_call | solution.py:604
  591.1 14.6 %all-reduce.9.cloned.1.call-done = bf16[512,1056]{1,0:T(8,128)(2,1)} async-done(((bf16[512,1056]{1,0:T(8,128)(2,1)}), bf16[512,1056]{1,0:T(8,128)(2,1)}) %all-reduce.9.cloned.1.call-update) | async-done | bytes 1081360 | tf_op jit(solution)/shard_map/psum | solution.py:883
  620.0 4.8 fusion.39
  624.9 5.4 fusion.9
  637.0 7.9 %fusion.30 = (bf16[2560,512]{1,0:T(8,128)(2,1)}, f32[512,2560]{0,1:T(8,128)}) fusion(f32[2560]{0:T(1024)S(1)} %copy-done.30, f32[512]{0:T(512)S(1)} %copy-done.33, bf16[512,2560]{0,1:T(8,128)(2,1)} %copy.132, f32[512,2560]{0,1:T(8,128)} %copy-done.4, f32[512]{0:T(512)S(1)} %broadcast_multiply_fusion.2, f32[512]{0:T(512)} %get-tuple-element.164, ...), kind=kLoop, calls=%fused_computation.98 | loop fusion | flops 13107200 | bytes 20987904 | tf_op jit(solution)/shard_map/transpose | solution.py:919
  644.9 37.3 %scatter_over_ctx_4.1 = (f32[320,768]{1,0:T(8,128)}, f32[320,288]{1,0:T(8,128)}, f32[32,128]{1,0:T(8,128)}) custom-call(bf16[2560,512]{1,0:T(8,128)(2,1)} %get-tuple-element.154.refs_0_.refs_2_, bf16[512,768]{1,0:T(8,128)(2,1)} %subtract_convert_fusion.refs_1_, bf16[2560,512]{1,0:T(8,128)(2,1)} %get-tuple-element.154.refs_0_.refs_2_, ...), custom_call_target="tpu_custom_call" | custom-call | flops 2768240640 | bytes 67108864 | tf_op jit(solution)/shard_map/scatter_over_ctx_4/pallas_call | solution.py:604
  686.6 5.9 copy.152
  693.9 4.4 copy.151
  (175 shorter events, 78.2 us)
Async XLA Ops:
  7.2 83.2 %copy-start = (bf16[2560,640]{1,0:T(8,128)(2,1)S(1)}, bf16[2560,640]{1,0:T(8,128)(2,1)}, u32[]{:S(2)}) copy-start(bf16[2560,640]{1,0:T(8,128)(2,1)} %param.21) | copy-start | bytes 9830404
  7.2 220.2 %all-reduce.5.cloned.1.call-start = ((), (), s32[]{:S(2)}) async-start(), calls=%async_computation.1 | async-start | bytes 5242880 | tf_op jit(solution)/shard_map/psum | solution.py:835
  7.8 7.6 %copy-start.29 = (f32[2560]{0:T(1024)S(1)}, f32[2560]{0:T(1024)}, u32[]{:S(2)}) copy-start(f32[2560]{0:T(1024)} %param.25) | copy-start | bytes 30724
  15.4 13.5 %copy-start.32 = (f32[512]{0:T(512)}, f32[512]{0:T(512)S(1)}, u32[]{:S(2)}) copy-start(f32[512]{0:T(512)S(1)} %get-tuple-element.165) | copy-start | bytes 6148
  27.2 7.9 %copy-start.35 = (f32[512]{0:T(512)}, f32[512]{0:T(512)S(1)}, u32[]{:S(2)}) copy-start(f32[512]{0:T(512)S(1)} %get-tuple-element.167) | copy-start | bytes 6148
  28.9 6.2 copy-start.12
  28.9 6.2 copy-start.37
  28.9 6.4 copy-start.40
  28.9 7.4 %copy-start.25 = (f32[512,32]{1,0:T(8,128)S(1)}, f32[512,32]{1,0:T(8,128)}, u32[]{:S(2)}) copy-start(f32[512,32]{1,0:T(8,128)} %copy.135) | copy-start | bytes 196612
  28.9 7.4 %copy-start.26 = (f32[512,32]{1,0:T(8,128)S(1)}, f32[512,32]{1,0:T(8,128)}, u32[]{:S(2)}) copy-start(f32[512,32]{1,0:T(8,128)} %copy.163) | copy-start | bytes 196612
  34.4 27.1 %copy-start.7 = (f32[512,768]{1,0:T(8,128)}, f32[512,768]{1,0:T(8,128)S(1)}, u32[]{:S(2)}) copy-start(f32[512,768]{1,0:T(8,128)S(1)} %get-tuple-element.173) | copy-start | bytes 4718596
  35.1 26.4 %copy-start.34 = (f32[768]{0:T(1024)S(1)}, f32[768]{0:T(1024)}, u32[]{:S(2)}) copy-start(f32[768]{0:T(1024)} %param.26) | copy-start | bytes 9220
  36.3 26.4 %copy-start.15 = (f32[512,128]{1,0:T(8,128)}, f32[512,128]{1,0:T(8,128)S(1)}, u32[]{:S(2)}) copy-start(f32[512,128]{1,0:T(8,128)S(1)} %get-tuple-element.163.sin) | copy-start | bytes 786436
  36.3 26.4 %copy-start.17 = (f32[512,128]{1,0:T(8,128)}, f32[512,128]{1,0:T(8,128)S(1)}, u32[]{:S(2)}) copy-start(f32[512,128]{1,0:T(8,128)S(1)} %get-tuple-element.162.cos) | copy-start | bytes 786436
  95.3 347.4 %all-reduce.7.cloned.1.call-start = ((), (), s32[]{:S(2)}) async-start(), calls=%async_computation.2 | async-start | bytes 5242880 | tf_op jit(solution)/shard_map/psum | solution.py:851
  95.3 135.8 %copy-start.31 = (f32[2560]{0:T(1024)S(1)}, f32[2560]{0:T(1024)}, u32[]{:S(2)}) copy-start(f32[2560]{0:T(1024)} %param.28) | copy-start | bytes 30724
  283.6 8.6 %copy-start.44 = (bf16[512,1600]{1,0:T(8,128)(2,1)}, bf16[512,1600]{1,0:T(8,128)(2,1)S(1)}, u32[]{:S(2)}) copy-start(bf16[512,1600]{1,0:T(8,128)(2,1)S(1)} %get-tuple-element.152.refs_1_) | copy-start | bytes 4915204
  283.6 8.6 %copy-start.43 = (bf16[512,1600]{1,0:T(8,128)(2,1)}, bf16[512,1600]{1,0:T(8,128)(2,1)S(1)}, u32[]{:S(2)}) copy-start(bf16[512,1600]{1,0:T(8,128)(2,1)S(1)} %get-tuple-element.153.refs_3_) | copy-start | bytes 4915204
  304.0 241.5 %reduce-scatter.4.cloned.1.call-start = ((), (), s32[]{:S(2)}) async-start(), calls=%async_computation.5 | async-start | bytes 3276800
  447.5 158.1 %all-reduce.9.cloned.1.call-start = ((), (), s32[]{:S(2)}) async-start(), calls=%async_computation.3 | async-start | bytes 2359296 | tf_op jit(solution)/shard_map/psum | solution.py:883
  447.6 6.1 copy-start.2
  447.6 6.1 copy-start.6
  447.6 6.9 copy-start.10
  496.1 47.3 %copy-start.22 = (bf16[768,960]{0,1:T(8,128)(2,1)S(1)}, bf16[768,960]{0,1:T(8,128)(2,1)}, u32[]{:S(2)}) copy-start(bf16[768,960]{0,1:T(8,128)(2,1)} %param.19) | copy-start | bytes 4423684
  496.1 47.3 %copy-start.42 = (bf16[512,960]{1,0:T(8,128)(2,1)S(1)}, bf16[512,960]{1,0:T(8,128)(2,1)}, u32[]{:S(2)}) copy-start(bf16[512,960]{1,0:T(8,128)(2,1)} %get-tuple-element.50.refs_3_) | copy-start | bytes 2949124
  550.2 143.7 %all-gather.2.cloned.1.call-start = ((), (), s32[]{:S(2)}) async-start(), calls=%async_computation.4 | async-start | bytes 3276800 | tf_op jit(solution)/shard_map/all_gather | solution.py:896
  591.1 16.2 %copy-start.36 = (f32[512]{0:T(512)S(1)}, f32[512]{0:T(512)}, u32[]{:S(2)}) copy-start(f32[512]{0:T(512)} %copy-done.35) | copy-start | bytes 6148
  591.1 16.2 %copy-start.38 = (f32[256]{0:T(256)S(1)}, f32[256]{0:T(256)}, u32[]{:S(2)}) copy-start(f32[256]{0:T(256)} %param.27) | copy-start | bytes 3076
  609.8 5.8 copy-start.18
  620.0 4.9 copy-start.33
  693.9 8.5 %copy-start.28 = (f32[32,1280]{1,0:T(8,128)S(1)}, f32[32,1280]{1,0:T(8,128)}, u32[]{:S(2)}) copy-start(f32[32,1280]{1,0:T(8,128)} %get-tuple-element.196) | copy-start | bytes 491524
  698.3 5.7 copy-start.21
  (18 other events, 61.8 us)
Sparse Core Ops, SparseCore 0:
  95.4 131.9 all-reduce.4
  304.1 103.1 all-reduce.6
  447.6 50.2 reduce-scatter.3
  550.3 55.3 all-reduce.8
  609.9 54.3 all-gather.1

commit v4 on v3

--- a/solution.py
+++ b/solution.py
@@ -107,7 +107,7 @@
         width = heads * (NOPE + ROPE)
         for at in range(0, width, WIDE):
             end = min(at + WIDE, width)
-            pre[:, at:end] = dot_nn(cq[here, :], wqb[:, at:end])
+            pre[:, at:end] = dot_nt(cq[here, :], wqb[at:end, :])
         for h in range(heads):
             at, shift = head_window(h)
             own_part = pltpu.roll(pre[:, at : at + WIDE], (WIDE - shift) % WIDE, 1)[:, :HEAD]
@@ -705,6 +705,283 @@
     return gathered.reshape((-1,) + own.shape[1:])
 
 
+CHUNK = 32
+BLOCK = 4 * CHUNK
+MIDDLE_VMEM = 62 * 1024 * 1024
+
+
+def middle_kernel(
+    n, ob, tokens, cot, gain, w_out, w_gate, w_up, w_down,
+    tt, d_out, f_out, act_out, dg_out, du_out,
+    own, up, wo, wg, wu, wd, h2, dfs, d_acc, f_acc,
+    w_sems, up_send, up_land, down_send, back_send, down_land,
+):
+    me = lax.axis_index("tp")
+    root = (n - 1) // 2
+    width = tokens.shape[1]
+    hidden = wg.shape[0]
+    chunks = own.shape[0]
+    blocks = chunks // 4
+    root_lag = n - 1 - root
+    land_lag = 2 * root_lag
+    block_lag = -(-(4 + land_lag) // 4)
+    tiles = [(c, min(c + 512, width)) for c in range(0, width, 512)]
+    quarter = hidden // 4 // 128 * 128
+    cuts = [0, quarter, 2 * quarter, 3 * quarter, hidden]
+    loads = [
+        pltpu.make_async_copy(w_out, wo, w_sems.at[0]),
+        pltpu.make_async_copy(w_gate, wg, w_sems.at[1]),
+        pltpu.make_async_copy(w_up, wu, w_sems.at[2]),
+        pltpu.make_async_copy(w_down, wd, w_sems.at[3]),
+    ]
+    for load in loads:
+        load.start()
+    barrier = pltpu.get_barrier_semaphore()
+    has_left, has_right = me > 0, me < n - 1
+    for there, other in ((has_left, me - 1), (has_right, me + 1)):
+
+        @pl.when(there)
+        def _(other=other):
+            pl.semaphore_signal(barrier, inc=1, device_id={"tp": other}, device_id_type=MESH)
+
+    @pl.when(has_left & has_right)
+    def _():
+        pl.semaphore_wait(barrier, 2)
+
+    @pl.when(jnp.logical_not(has_left & has_right))
+    def _():
+        pl.semaphore_wait(barrier, 1)
+
+    def copy_to(source, target, send, land, c, other):
+        return pltpu.make_async_remote_copy(
+            src_ref=source.at[c],
+            dst_ref=target.at[c],
+            send_sem=send.at[c],
+            recv_sem=land.at[c],
+            device_id={"tp": other},
+            device_id_type=MESH,
+        )
+
+    def rise_left(c):
+        return copy_to(own, up, up_send, up_land, c, me + 1)
+
+    def rise_right(c):
+        return copy_to(own, up, up_send, up_land, c, me - 1)
+
+    def rise_last(c):
+        return copy_to(own, tt, up_send, down_land, c, me - 1)
+
+    def fall_right(c):
+        return copy_to(tt, tt, down_send, down_land, c, me + 1)
+
+    def fall_left(c):
+        return copy_to(tt, tt, back_send, down_land, c, me - 1)
+
+    rises = [(me < root, rise_left)] if root else []
+    rises.append((me == root + 1, rise_last))
+    if n - 1 > root + 1:
+        rises.append((me > root + 1, rise_right))
+
+    def rise(c):
+        for who, copy in rises:
+
+            @pl.when(who)
+            def _(copy=copy):
+                copy(c).start()
+
+    def inside(c):
+        return (c >= 0) & (c < chunks)
+
+    def added(refs, c):
+        total = refs[0][c].astype(jnp.float32)
+        for ref in refs[1:]:
+            total = total + ref[c].astype(jnp.float32)
+        return total.astype(jnp.bfloat16)
+
+    def duties(t):
+        leaf = (me == 0) | (me == n - 1) if root else me == n - 1
+        @pl.when(leaf & (t < chunks))
+        def _():
+            rise(t)
+
+        if n > 3:
+            c = t - jnp.where(me < root, me, n - 1 - me)
+
+            @pl.when((me != root) & has_left & has_right & inside(c))
+            def _():
+                rise_right(c).wait_recv()
+                own[c] = added([own, up], c)
+                rise(c)
+
+        c_root = t - root_lag
+
+        @pl.when((me == root) & inside(c_root))
+        def _():
+            if root:
+                rise_left(c_root).wait_recv()
+            fall_right(c_root).wait_recv()
+            tt[c_root] = added([own, up, tt] if root else [own, tt], c_root)
+            fall_right(c_root).start()
+            if root:
+                fall_left(c_root).start()
+
+        c_fall = t - root_lag - jnp.where(me < root, root - me, me - root)
+
+        @pl.when((me != root) & inside(c_fall))
+        def _():
+            fall_right(c_fall).wait_recv()
+
+            @pl.when((me > root) & has_right)
+            def _():
+                fall_right(c_fall).start()
+
+            @pl.when((me < root) & has_left)
+            def _():
+                fall_left(c_fall).start()
+
+        c_norm = t - land_lag
+
+        @pl.when(inside(c_norm))
+        def _():
+            rows = pl.ds(pl.multiple_of(c_norm * CHUNK, CHUNK), CHUNK)
+            middle = tokens[rows, :].astype(jnp.float32) + RESIDUAL_SCALE * tt[c_norm].astype(
+                jnp.float32
+            )
+            scale = lax.rsqrt(jnp.mean(middle * middle, axis=-1, keepdims=True) + EPSILON)
+            slot = lax.rem(lax.div(c_norm, 4), 2)
+            h2[slot, pl.ds(pl.multiple_of(lax.rem(c_norm, 4) * CHUNK, CHUNK), CHUNK), :] = (
+                middle * scale * gain[...]
+            ).astype(jnp.bfloat16)
+
+    def project(b):
+        rows = pl.ds(pl.multiple_of(b * BLOCK, BLOCK), BLOCK)
+        for first, last in tiles:
+            part = dot_nt(ob[rows, :], wo[first:last, :]).astype(jnp.bfloat16)
+            for k in range(4):
+                own[4 * b + k, :, first:last] = part[k * CHUNK : (k + 1) * CHUNK, :]
+
+    def feed(b, i):
+        rows = pl.ds(pl.multiple_of(b * BLOCK, BLOCK), BLOCK)
+        slot = lax.rem(b, 2)
+        first, last = cuts[i], cuts[i + 1]
+        if i == 0:
+            dfs[...] = (RESIDUAL_SCALE * cot[rows, :].astype(jnp.float32)).astype(jnp.bfloat16)
+        gate = dot_nt(h2[slot], wg[first:last, :])
+        upper = dot_nt(h2[slot], wu[first:last, :])
+        d_act = dot_nt(dfs[...], wd[first:last, :])
+        sig = jax.nn.sigmoid(gate)
+        silu = gate * sig
+        act = (silu * upper).astype(jnp.bfloat16)
+        dg = (d_act * upper * sig * (1.0 + gate * (1.0 - sig))).astype(jnp.bfloat16)
+        du = (d_act * silu).astype(jnp.bfloat16)
+        act_out[rows, first:last] = act
+        dg_out[rows, first:last] = dg
+        du_out[rows, first:last] = du
+        for lo, hi in tiles:
+            d_part = dot_nn(dg, wg[first:last, lo:hi]) + dot_nn(du, wu[first:last, lo:hi])
+            f_part = dot_nn(act, wd[first:last, lo:hi])
+            if i:
+                d_part = d_part + d_acc[:, lo:hi]
+                f_part = f_part + f_acc[:, lo:hi]
+            if i < 3:
+                d_acc[:, lo:hi] = d_part
+                f_acc[:, lo:hi] = f_part
+            else:
+                d_out[rows, lo:hi] = d_part.astype(jnp.bfloat16)
+                f_out[rows, lo:hi] = f_part.astype(jnp.bfloat16)
+
+    loads[0].wait()
+
+    def outer(o, carry):
+        @pl.when(o < blocks)
+        def _():
+            project(o)
+
+        @pl.when(o == block_lag)
+        def _():
+            for load in loads[1:]:
+                load.wait()
+
+        for i in range(4):
+            duties(4 * o + i)
+
+            @pl.when(o >= block_lag)
+            def _(i=i):
+                feed(o - block_lag, i)
+
+        return carry
+
+    lax.fori_loop(0, blocks + block_lag, outer, 0)
+
+    def drain(c, carry):
+        @pl.when(me != root)
+        def _():
+            rise_right(c).wait_send()
+
+        @pl.when((me >= root) & has_right)
+        def _():
+            fall_right(c).wait_send()
+
+        @pl.when((me <= root) & has_left)
+        def _():
+            fall_left(c).wait_send()
+
+        return carry
+
+    lax.fori_loop(0, chunks, drain, 0)
+
+
+def middle_layer(n, ob, tokens, cot, gain, w_out, w_gate, w_up, w_down, collective_id):
+    rows, width = tokens.shape
+    hidden = w_gate.shape[0]
+    chunks = rows // CHUNK
+    vmem = pl.BlockSpec(memory_space=pltpu.VMEM)
+    anywhere = pl.BlockSpec(memory_space=pl.ANY)
+    half = jnp.bfloat16
+    dma = pltpu.SemaphoreType.DMA
+    attn, d_part, f_part, act, dg, du = pl.pallas_call(
+        functools.partial(middle_kernel, n),
+        out_shape=(
+            jax.ShapeDtypeStruct((chunks, CHUNK, width), half),
+            jax.ShapeDtypeStruct((rows, width), half),
+            jax.ShapeDtypeStruct((rows, width), half),
+            jax.ShapeDtypeStruct((rows, hidden), half),
+            jax.ShapeDtypeStruct((rows, hidden), half),
+            jax.ShapeDtypeStruct((rows, hidden), half),
+        ),
+        in_specs=[vmem] * 4 + [anywhere] * 4,
+        out_specs=(vmem,) * 6,
+        scratch_shapes=[
+            pltpu.VMEM((chunks, CHUNK, width), half),
+            pltpu.VMEM((chunks, CHUNK, width), half),
+            pltpu.VMEM(w_out.shape, half),
+            pltpu.VMEM(w_gate.shape, half),
+            pltpu.VMEM(w_up.shape, half),
+            pltpu.VMEM(w_down.shape, half),
+            pltpu.VMEM((2, BLOCK, width), half),
+            pltpu.VMEM((BLOCK, width), half),
+            pltpu.VMEM((BLOCK, width), jnp.float32),
+            pltpu.VMEM((BLOCK, width), jnp.float32),
+            dma((4,)),
+            dma((chunks,)),
+            dma((chunks,)),
+            dma((chunks,)),
+            dma((chunks,)),
+            dma((chunks,)),
+        ],
+        compiler_params=pltpu.CompilerParams(
+            vmem_limit_bytes=MIDDLE_VMEM, collective_id=collective_id, has_side_effects=True
+        ),
+        cost_estimate=pl.CostEstimate(
+            flops=2 * rows * width * (6 * hidden + ob.shape[1]),
+            bytes_accessed=64 * 1024 * 1024,
+            transcendentals=rows * hidden,
+        ),
+        name=f"middle_layer_{collective_id}",
+    )(ob, tokens, cot, gain.reshape(1, -1), w_out, w_gate, w_up, w_down)
+    return attn.reshape(rows, width), d_part, f_part, act, dg, du
+
+
 def dot_plain(left_op, right_op):
     return jnp.dot(left_op, right_op, preferred_element_type=jnp.float32)
 
@@ -830,27 +1107,18 @@
     scale_q = rms_scale(q_latent_pre)
     q_latent = (q_latent_pre * scale_q * gain_q).astype(jnp.bfloat16)
     queries, attn_f, heads_out, log_totals = attention_forward(
-        meta, q_latent, w_qb, latents, w_kvb, cosine_wide, sine_wide, half_rows, seqs
-    )
-    attention = lax.psum(dot_cols(heads_out, w_out).astype(jnp.bfloat16), "tp").astype(jnp.float32)
-    middle = tokens_f + RESIDUAL_SCALE * attention
+        meta, q_latent, w_qb.T, latents, w_kvb, cosine_wide, sine_wide, half_rows, seqs
+    )
+    attention, d_part, feed_part, activation, d_gate, d_up = middle_layer(
+        lax.axis_size("tp"), heads_out, tokens_in, cotangent, gain_mid, w_out, w_gate.T, w_up.T,
+        w_down.T, 5,
+    )
+    middle = tokens_f + RESIDUAL_SCALE * attention.astype(jnp.float32)
     scale_mid = rms_scale(middle)
     normed_mid = (middle * scale_mid * gain_mid).astype(jnp.bfloat16)
-    gate_val = dot_plain(normed_mid, w_gate)
-    up_val = dot_plain(normed_mid, w_up)
-    sig_gate = jax.nn.sigmoid(gate_val)
-    silu_gate = gate_val * sig_gate
-    activation = (silu_gate * up_val).astype(jnp.bfloat16)
     cotangent_f = cotangent.astype(jnp.float32)
     d_feed = (RESIDUAL_SCALE * cotangent_f).astype(jnp.bfloat16)
-    d_activation = dot_plain(d_feed, w_down)
-    d_gate = (d_activation * up_val * sig_gate * (1.0 + gate_val * (1.0 - sig_gate))).astype(
-        jnp.bfloat16
-    )
-    d_up = (d_activation * silu_gate).astype(jnp.bfloat16)
-    d_normed_mid = lax.psum(
-        (dot_cols(d_gate, w_gate) + dot_cols(d_up, w_up)).astype(jnp.bfloat16), "tp"
-    ).astype(jnp.float32)
+    d_normed_mid = lax.psum(d_part, "tp")
     gw_gate, gw_up, gw_down = scatter_over_ctx(
         devices,
         [
@@ -860,10 +1128,10 @@
         ],
         1,
     )
-    feed_part = dot_cols(activation, w_down).astype(jnp.bfloat16)
     d_normed_mid, feed_part, gw_gate, gw_up, gw_down = lax.optimization_barrier(
         (d_normed_mid, feed_part, gw_gate, gw_up, gw_down)
     )
+    d_normed_mid = d_normed_mid.astype(jnp.float32)
     feed_own = lax.psum_scatter(feed_part, "tp", scatter_dimension=0, tiled=True)
     own_rows = feed_own.shape[0]
     middle_own = lax.dynamic_slice_in_dim(middle, lax.axis_index("tp") * own_rows, own_rows, 0)

time: 723 us -> 642 us (0.89)
  Pallas kernels: 327 us -> 468 us
  waiting for transfers between devices: 142 us -> 17.6 us
  matrix products: 93.9 us -> 20.6 us
  local copies, waits for them, and re-layouts: 70.3 us -> 55.7 us
    psum x2 -> x1, waiting for transfers between devices: 127 us -> 0.02 us  [on_device(): d_normed_mid = lax.psum(d_part, 'tp')]
    pallas_call x0 -> x1, Pallas kernels: none -> 114 us  [middle_layer(): pl.pallas_call(functools.partial(middle_kernel, n), out_shape=(jax.ShapeD...]
    dot_general x6 -> x3, matrix products: 46.9 us -> 9.65 us  [dot_plain(): return jnp.dot(left_op, right_op, preferred_element_type=jnp.float32)]
    dot_general x7 -> x3, matrix products: 47 us -> 10.9 us  [dot_cols(): lax.dot_general(left_op, right_op, (((1,), (1,)), ((), ())), preferred_el...]
    pallas_call x1, Pallas kernels: 27.8 us -> 55.4 us  [attention_forward(): pl.pallas_call(functools.partial(forward_kernel, blocks, heads, seqs), ou...]
    pallas_call x4, Pallas kernels: 243 us -> 218 us  [scatter_over_ctx(): pl.pallas_call(functools.partial(scatter_kernel, n, items), out_shape=tup...]
    pallas_call x1, Pallas kernels: 32.2 us -> 56.7 us  [attention_backward(): pl.pallas_call(functools.partial(backward_kernel, blocks, heads, seqs), o...]
    dot_general x2 -> x0, local copies, waits for them, and re-layouts: 9.39 us -> none  [dot_plain(): return jnp.dot(left_op, right_op, preferred_element_type=jnp.float32)]
  transfers between devices with their start and end apart: 5 -> 4, of which waited for: 2 -> 1; matrix products, arithmetic and copies ran while one was open for 13% -> 13% of each run, Pallas kernels for 38% -> 43%
where the time goes in v4:
time: 642 us; the launch traced here: 636 us
  Pallas kernels  468 us (73%)
  other arithmetic  59.2 us (9%)
  local copies, waits for them, and re-layouts  55.7 us (9%)
  matrix products  20.6 us (3%)
  waiting for transfers between devices  17.6 us (3%)
  between operations  14.5 us (2%)
    pallas_call x4, Pallas kernels, scatter_over_ctx(): pl.pallas_call(functools.partial(scatter_kernel, n, items), out_shape=tup...  218 us
    pallas_call x1, Pallas kernels, middle_layer(): pl.pallas_call(functools.partial(middle_kernel, n), out_shape=(jax.ShapeD...  114 us
    pallas_call x1, Pallas kernels, attention_backward(): pl.pallas_call(functools.partial(backward_kernel, blocks, heads, seqs), o...  56.7 us
    pallas_call x1, Pallas kernels, attention_forward(): pl.pallas_call(functools.partial(forward_kernel, blocks, heads, seqs), ou...  55.4 us
    unnamed x85, local copies, waits for them, and re-layouts  35.5 us
    pallas_call x1, Pallas kernels, gather_over_ctx(): pl.pallas_call(functools.partial(gather_kernel, n), out_shape=jax.ShapeDt...  24.4 us
    psum x1, waiting for transfers between devices, on_device(): summed_tp = lax.psum(before_tp, 'tp')  17.5 us
  transfers between devices with their start and end apart: 4, of which 1 were waited for; matrix products, arithmetic and copies ran while one was open for 13% of the time, Pallas kernels for 43%

profile of v4, /device:TPU:0, one launch (start us, length us, event | category | flops | bytes accessed | tf_op | source)
XLA Modules:
  0.0 636.0 jit_solution(6599627106468319904)
XLA Ops:
  7.3 4.5 copy.81
  11.7 2.5 fusion.7
  16.8 5.5 multiply_reduce_fusion.3
  24.9 2.0 copy.99
  32.4 24.4 %gather_over_ctx_0.1 = bf16[8,512,288]{2,1,0:T(8,128)(2,1)} custom-call(bf16[512,288]{1,0:T(8,128)(2,1)} %pad_maximum_fusion.1.own), custom_call_target="tpu_custom_call" | custom-call | bytes 16777216 | tf_op jit(solution)/shard_map/gather_over_ctx_0/pallas_call | solution.py:685
  58.6 55.4 %attention_forward.1 = (bf16[2,10,256,256]{3,2,1,0:T(8,128)(2,1)}, f32[512,640]{1,0:T(8,128)}, bf16[512,640]{1,0:T(8,128)(2,1)}, f32[2,16,256]{2,1,0:T(8,128)}) custom-call(s32[22]{0:T(128)} %pad_add_fusion.meta, bf16[512,768]{1,0:T(8,128)(2,1)} %multiply_convert_fusion.2.cq, bf16[960,768]{1,0:T(8,128)(2,1)} %bitcast.45, bf16[4096,288]{1,0:T(8,128)(2,1)} %bitcast.35, ...), custom_call_target="tpu_custom_call" | custom-call | flops 10737418240 | bytes 16777216 | tf_op jit(solution)/shard_map/attention_forward/pallas_call | solution.py:197
  114.0 113.6 %middle_layer_5.1 = (bf16[16,32,2560]{2,1,0:T(8,128)(2,1)}, bf16[512,2560]{1,0:T(8,128)(2,1)}, bf16[512,2560]{1,0:T(8,128)(2,1)}, bf16[512,1600]{1,0:T(8,128)(2,...) custom-call(bf16[512,640]{1,0:T(8,128)(2,1)} %get-tuple-element.51.ob.refs_1_, bf16[512,2560]{1,0:T(8,128)(2,1)} %tokens.1, ...), custom_call_target="tpu_custom_call" | custom-call | flops 26843545600 | bytes 67108864 | tf_op jit(solution)/shard_map/middle_layer_5/pallas_call | solution.py:942
  227.5 4.4 copy.87
  232.0 4.7 copy.85
  236.7 4.8 convert_multiply_fusion.8
  241.5 5.9 copy.86
  247.5 6.5 %multiply_reduce_fusion = (f32[512]{0:T(512)S(1)}, f32[512,2560]{0,1:T(8,128)}) fusion(f32[512,2560]{0,1:T(8,128)} %copy.86, bf16[512,2560]{0,1:T(8,128)(2,1)} %copy.81), kind=kLoop, calls=%fused_computation.28 | loop fusion | flops 5242368 | bytes 13109248 | tf_op jit(solution)/shard_map/reduce_sum | solution.py:1002
  254.0 3.9 fusion.17.refs_4_
  257.9 2.0 fusion.16.refs_0_.refs_2_
  260.0 122.6 %scatter_over_ctx_1.1 = (f32[320,1600]{1,0:T(8,128)}, f32[320,1600]{1,0:T(8,128)}, f32[320,1600]{1,0:T(8,128)}) custom-call(bf16[2560,512]{1,0:T(8,128)(2,1)} %fusion.16.refs_0_.refs_2_, bf16[512,1600]{1,0:T(8,128)(2,1)} %get-tuple-element.55.refs_1_, bf16[2560,512]{1,0:T(8,128)(2,1)} %fusion.16.refs_0_.refs_2_, ...), custom_call_target="tpu_custom_call" | custom-call | flops 12582912000 | bytes 67108864 | tf_op jit(solution)/shard_map/scatter_over_ctx_1/pallas_call | solution.py:604
  382.7 5.0 fusion.6
  388.3 4.6 fusion.18
  392.9 3.1 convolution_convert_fusion.1.dob
  396.1 56.7 %attention_backward.1 = (bf16[512,960]{1,0:T(8,128)(2,1)}, bf16[4096,288]{1,0:T(8,128)(2,1)}, bf16[256,1280]{1,0:T(8,128)(2,1)}) custom-call(s32[22]{0:T(128)} %pad_add_fusion.meta, bf16[2,10,256,256]{3,2,1,0:T(8,128)(2,1)} %get-tuple-element.48.qx, f32[2,16,256]{2,1,0:T(8,128)} %get-tuple-element.49.u_in, f32[512,640]{1,0:T(8,128)} %get-tuple-element.50.o_in, ...), custom_call_target="tpu_custom_call" | custom-call | flops 21474836480 | bytes 25165824 | tf_op jit(solution)/shard_map/attention_backward/pallas_call | solution.py:380
  452.8 23.3 %scatter_over_ctx_2.1 = f32[512,288]{1,0:T(8,128)} custom-call(bf16[4096,288]{1,0:T(8,128)(2,1)} %get-tuple-element.63.refs_0_), custom_call_target="tpu_custom_call" | custom-call | bytes 67108864 | tf_op jit(solution)/shard_map/scatter_over_ctx_2/pallas_call | solution.py:604
  479.4 2.3 copy.98
  481.6 2.5 add_convert_fusion
  485.3 2.3 copy.89.refs_2_
  487.7 35.0 %scatter_over_ctx_3.1 = (f32[320,640]{1,0:T(8,128)}, f32[96,960]{1,0:T(8,128)}, f32[32,1280]{1,0:T(8,128)}) custom-call(bf16[2560,512]{1,0:T(8,128)(2,1)} %get-tuple-element.146.refs_0_, bf16[512,640]{1,0:T(8,128)(2,1)} %get-tuple-element.51.ob.refs_1_, bf16[768,512]{1,0:T(8,128)(2,1)} %copy.89.refs_2_, bf16[512,960]{1,0:T(8,128)(2,1)} %get-tuple-element.62.refs_3_, ...), custom_call_target="tpu_custom_call" | custom-call | flops 2432696320 | bytes 67108864 | tf_op jit(solution)/shard_map/scatter_over_ctx_3/pallas_call | solution.py:604
  522.8 17.5 %all-reduce.6.cloned.1.call-done = bf16[512,1056]{1,0:T(8,128)(2,1)} async-done(((bf16[512,1056]{1,0:T(8,128)(2,1)}), bf16[512,1056]{1,0:T(8,128)(2,1)}) %all-reduce.6.cloned.1.call-update) | async-done | bytes 1081360 | tf_op jit(solution)/shard_map/psum | solution.py:1151
  543.6 2.7 subtract_convert_fusion.refs_1_
  548.9 5.1 fusion.40
  554.1 4.8 fusion.15
  560.5 7.9 %fusion.33 = (bf16[2560,512]{1,0:T(8,128)(2,1)}, f32[512,2560]{0,1:T(8,128)}) fusion(f32[2560]{0:T(1024)S(1)} %copy-done.25, f32[512]{0:T(512)S(1)} %get-tuple-element.161, bf16[512,2560]{0,1:T(8,128)(2,1)} %copy.81, f32[512,2560]{0,1:T(8,128)} %copy-done.4, f32[512]{0:T(512)S(1)} %broadcast_multiply_fusion.2, f32[512]{0:T(512)S(1)} %get-tuple-element.160, ...), kind=kLoop, calls=%fused_computation.96 | loop fusion | flops 13107200 | bytes 20987904 | tf_op jit(solution)/shard_map/transpose | solution.py:1187
  568.4 37.3 %scatter_over_ctx_4.1 = (f32[320,768]{1,0:T(8,128)}, f32[320,288]{1,0:T(8,128)}, f32[32,128]{1,0:T(8,128)}) custom-call(bf16[2560,512]{1,0:T(8,128)(2,1)} %get-tuple-element.150.refs_0_.refs_2_, bf16[512,768]{1,0:T(8,128)(2,1)} %subtract_convert_fusion.refs_1_, bf16[2560,512]{1,0:T(8,128)(2,1)} %get-tuple-element.150.refs_0_.refs_2_, ...), custom_call_target="tpu_custom_call" | custom-call | flops 2768240640 | bytes 67108864 | tf_op jit(solution)/shard_map/scatter_over_ctx_4/pallas_call | solution.py:604
  608.1 5.9 copy.93
  616.5 4.5 copy.92
  (144 shorter events, 38.0 us)
Async XLA Ops:
  7.2 7.1 %copy-start = (bf16[2560,288]{0,1:T(8,128)(2,1)S(1)}, bf16[2560,288]{0,1:T(8,128)(2,1)}, u32[]{:S(2)}) copy-start(bf16[2560,288]{0,1:T(8,128)(2,1)} %param.18) | copy-start | bytes 4423684
  7.2 375.4 %all-reduce.4.cloned.1.call-start = ((), (), s32[]{:S(2)}) async-start(), calls=%async_computation.1 | async-start | bytes 5242880 | tf_op jit(solution)/shard_map/psum | solution.py:1121
  7.2 7.0 %copy-start.25 = (f32[2560]{0:T(1024)S(1)}, f32[2560]{0:T(1024)}, u32[]{:S(2)}) copy-start(f32[2560]{0:T(1024)} %param.25) | copy-start | bytes 30724
  11.7 2.5 copy-start.2
  16.8 11.3 %copy-start.27 = (f32[256]{0:T(256)S(1)}, f32[256]{0:T(256)}, u32[]{:S(2)}) copy-start(f32[256]{0:T(256)} %param.27) | copy-start | bytes 3076
  22.2 35.3 %copy-start.5 = (f32[512,768]{1,0:T(8,128)}, f32[512,768]{1,0:T(8,128)S(1)}, u32[]{:S(2)}) copy-start(f32[512,768]{1,0:T(8,128)S(1)} %get-tuple-element.169) | copy-start | bytes 4718596
  30.3 26.5 %copy-start.12 = (f32[512,128]{1,0:T(8,128)}, f32[512,128]{1,0:T(8,128)S(1)}, u32[]{:S(2)}) copy-start(f32[512,128]{1,0:T(8,128)S(1)} %get-tuple-element.159.sin) | copy-start | bytes 786436
  30.3 26.5 %copy-start.14 = (f32[512,128]{1,0:T(8,128)}, f32[512,128]{1,0:T(8,128)S(1)}, u32[]{:S(2)}) copy-start(f32[512,128]{1,0:T(8,128)S(1)} %get-tuple-element.158.cos) | copy-start | bytes 786436
  30.4 26.5 %copy-start.23 = (f32[2560]{0:T(1024)S(1)}, f32[2560]{0:T(1024)}, u32[]{:S(2)}) copy-start(f32[2560]{0:T(1024)} %param.28) | copy-start | bytes 30724
  30.4 27.1 %copy-start.26 = (f32[768]{0:T(1024)S(1)}, f32[768]{0:T(1024)}, u32[]{:S(2)}) copy-start(f32[768]{0:T(1024)} %param.26) | copy-start | bytes 9220
  232.0 247.4 %reduce-scatter.4.cloned.1.call-start = ((), (), s32[]{:S(2)}) async-start(), calls=%async_computation.4 | async-start | bytes 3276800
  254.0 3.9 copy-start.1
  382.6 5.2 slice-start
  382.7 157.6 %all-reduce.6.cloned.1.call-start = ((), (), s32[]{:S(2)}) async-start(), calls=%async_computation.2 | async-start | bytes 2359296 | tf_op jit(solution)/shard_map/psum | solution.py:1151
  382.7 5.1 slice-start.1
  382.7 5.6 copy-start.7
  388.3 4.6 copy-start.11
  392.9 3.1 copy-start.4
  452.8 24.5 %copy-start.29 = (bf16[768,960]{0,1:T(8,128)(2,1)S(1)}, bf16[768,960]{0,1:T(8,128)(2,1)}, u32[]{:S(2)}) copy-start(bf16[768,960]{0,1:T(8,128)(2,1)} %param.19) | copy-start | bytes 4423684
  452.8 24.5 %copy-start.31 = (bf16[512,960]{1,0:T(8,128)(2,1)S(1)}, bf16[512,960]{1,0:T(8,128)(2,1)}, u32[]{:S(2)}) copy-start(bf16[512,960]{1,0:T(8,128)(2,1)} %get-tuple-element.62.refs_3_) | copy-start | bytes 2949124
  479.4 4.9 copy-start.6
  484.2 132.3 %all-gather.2.cloned.1.call-start = ((), (), s32[]{:S(2)}) async-start(), calls=%async_computation.3 | async-start | bytes 3276800 | tf_op jit(solution)/shard_map/all_gather | solution.py:1164
  543.5 2.9 copy-start.10
  543.6 4.0 copy-start.15
  548.9 5.1 copy-start.3
  608.1 5.9 copy-start.21
  616.4 4.5 copy-start.19
  616.4 5.5 copy-start.22
  616.5 6.2 copy-start.24
  621.0 2.4 copy-start.20
  621.0 3.3 copy-start.18
  625.6 2.4 copy-start.16
  (6 other events, 11.3 us)
Sparse Core Ops, SparseCore 0:
  232.1 102.6 all-reduce.3
  382.8 51.7 reduce-scatter.3
  484.3 55.8 all-reduce.5
  543.6 54.3 all-gather.1

commit v5 on v4

--- a/solution.py
+++ b/solution.py
@@ -416,7 +416,7 @@
     def __init__(self, n, given=None, left=None, right=None):
         self.operands = [given] if given is not None else [left, right]
         self.is_given = given is not None
-        self.rows = self.operands[0].shape[0] // n
+        self.rows = self.operands[0].shape[0 if self.is_given else 1] // n
         self.columns = self.operands[-1].shape[1]
         self.depth = 0 if self.is_given else right.shape[0]
         self.parts = 2 if self.rows % 32 == 0 else 1
@@ -432,12 +432,22 @@
     return chips
 
 
+def scatter_operands(items):
+    given = [item.operands[0] for item in items if item.is_given]
+    lefts = []
+    for item in items:
+        if not item.is_given and not any(item.operands[0] is left for left in lefts):
+            lefts.append(item.operands[0])
+    return given, lefts, [item.operands[1] for item in items if not item.is_given]
+
+
 def scatter_kernel(n, items, *refs):
     count = n.bit_length() - 1
     me = lax.axis_index("ctx")
     refs = list(refs)
     take = lambda k: [refs.pop(0) for _ in range(k)]
-    inputs = [take(len(item.operands)) for item in items]
+    given, lefts, rights = scatter_operands(items)
+    inputs = dict(zip(map(id, given + lefts + rights), take(len(given + lefts + rights))))
     outputs = take(len(items))
     held, sent, landed, core_sems, step_sems = [], [], [], [], []
     for item in items:
@@ -446,6 +456,7 @@
         landed.append(take(count - 1))
         core_sems.append(take(2))
         step_sems.append([take(2) for _ in range(count - 1)])
+    turned = dict(zip(map(id, lefts), take(len(lefts))))
     barrier = pltpu.get_barrier_semaphore()
     for bit in range(count):
         pl.semaphore_signal(barrier, inc=1, device_id={"ctx": me ^ (1 << bit)}, device_id_type=MESH)
@@ -459,7 +470,7 @@
 
     def product(k, dest, first, last):
         item = items[k]
-        left, right = inputs[k]
+        left, right = turned[id(item.operands[0])], inputs[id(item.operands[1])]
         at = pl.ds(pl.multiple_of(dest * item.rows, 16), item.rows)
         return dot_nn(left[at, :], right[:, first:last])
 
@@ -467,7 +478,7 @@
         item = items[k]
         if item.is_given:
             at = pl.ds(pl.multiple_of((2 * chip + 1 - core) * item.rows, 16), item.rows)
-            source = inputs[k][0].at[at, :]
+            source = inputs[id(item.operands[0])].at[at, :]
         else:
             source = sent[k].at[chip]
         return pltpu.make_async_remote_copy(
@@ -533,7 +544,7 @@
             at = pl.ds(pl.multiple_of((2 * chip + core) * item.rows, 16), item.rows)
             for first, last in columns_of(item):
                 if item.is_given:
-                    own = inputs[k][0][at, first:last].astype(jnp.float32)
+                    own = inputs[id(item.operands[0])][at, first:last].astype(jnp.float32)
                 else:
                     own = product(k, 2 * chip + core, first, last)
                 total = own + held[k][chip, :, first:last].astype(jnp.float32)
@@ -559,10 +570,26 @@
                 else:
                     held[k][keep, at, first:last] = total.astype(jnp.bfloat16)
 
+    def turn(k):
+        key = None if items[k].is_given else id(items[k].operands[0])
+        if key in turned and key not in done:
+            done.add(key)
+            source, target = inputs[key], turned[key]
+
+            def body(c, carry):
+                at = pl.ds(pl.multiple_of(c * 128, 128), 128)
+                target[at, :] = source[:, at].astype(jnp.float32).T.astype(jnp.bfloat16)
+                return carry
+
+            lax.fori_loop(0, source.shape[1] // 128, body, 0)
+
+    done = set()
     every = range(len(items))
+    turn(0)
     start_core(0)
     for k in every:
         if k + 1 < len(items):
+            turn(k + 1)
             start_core(k + 1)
         finish_core(k)
         start_step(k, 0)
@@ -600,7 +627,9 @@
         for step in range(count - 1):
             scratch += [pltpu.SemaphoreType.DMA((2, n >> (step + 2)))] * 2
         flops += 2 * n * item.rows * item.columns * item.depth
-    operands = [array for item in items for array in item.operands]
+    given, lefts, rights = scatter_operands(items)
+    operands = given + lefts + rights
+    scratch += [pltpu.VMEM(left.shape[::-1], jnp.bfloat16) for left in lefts]
     return pl.pallas_call(
         functools.partial(scatter_kernel, n, items),
         out_shape=tuple(
@@ -610,99 +639,13 @@
         out_specs=(vmem,) * len(items),
         scratch_shapes=scratch,
         compiler_params=pltpu.CompilerParams(
-            vmem_limit_bytes=VMEM_LIMIT, collective_id=collective_id, has_side_effects=True
+            vmem_limit_bytes=MIDDLE_VMEM, collective_id=collective_id, has_side_effects=True
         ),
         cost_estimate=pl.CostEstimate(
             flops=flops, bytes_accessed=64 * 1024 * 1024, transcendentals=0
         ),
         name=f"scatter_over_ctx_{collective_id}",
     )(*operands)
-
-
-def gather_kernel(n, own, out, local_sem, step_sends, step_lands, core_sends, core_lands):
-    count = n.bit_length() - 1
-    me = lax.axis_index("ctx")
-    rows = own.shape[0]
-    half = rows // 2
-    barrier = pltpu.get_barrier_semaphore()
-    for bit in range(count):
-        pl.semaphore_signal(barrier, inc=1, device_id={"ctx": me ^ (1 << bit)}, device_id_type=MESH)
-    pl.semaphore_wait(barrier, count)
-    orders = (tuple(range(1, count)), tuple(range(count - 1, 0, -1)))
-    local = pltpu.make_async_copy(own, out.at[me], local_sem)
-    local.start()
-
-    def chip_copy(part, step, slot, block, first):
-        at = pl.ds(part * half, half)
-        return pltpu.make_async_remote_copy(
-            src_ref=own.at[at, :] if first else out.at[block, at, :],
-            dst_ref=out.at[block, at, :],
-            send_sem=step_sends.at[part, step, slot],
-            recv_sem=step_lands.at[part, step, slot],
-            device_id={"ctx": me ^ (1 << orders[part][step])},
-            device_id_type=MESH,
-        )
-
-    def core_copy(block, slot, first):
-        return pltpu.make_async_remote_copy(
-            src_ref=own if first else out.at[block],
-            dst_ref=out.at[block],
-            send_sem=core_sends.at[slot],
-            recv_sem=core_lands.at[slot],
-            device_id={"ctx": me ^ 1},
-            device_id_type=MESH,
-        )
-
-    started = []
-    core_copy(me, 0, True).start()
-    for step in range(count - 1):
-        for part, order in enumerate(orders):
-            for slot in range(1 << step):
-                flips = 0
-                for at in range(step):
-                    flips |= ((slot >> at) & 1) << order[at]
-                copy = chip_copy(part, step, slot, me ^ flips, slot == 0)
-                copy.start()
-                started.append(copy)
-        for part, order in enumerate(orders):
-            for slot in range(1 << step):
-                chip_copy(part, step, slot, me, slot == 0).wait_recv()
-    for chip in range(1, n // 2):
-        core_copy(me ^ (2 * chip), chip, False).start()
-    for chip in range(n // 2):
-        core_copy(me, chip, chip == 0).wait_recv()
-    for copy in started:
-        copy.wait_send()
-    for chip in range(n // 2):
-        core_copy(me, chip, chip == 0).wait_send()
-    local.wait()
-
-
-def gather_over_ctx(n, own, collective_id):
-    count = n.bit_length() - 1
-    vmem = pl.BlockSpec(memory_space=pltpu.VMEM)
-    slots = max(n // 4, 1)
-    gathered = pl.pallas_call(
-        functools.partial(gather_kernel, n),
-        out_shape=jax.ShapeDtypeStruct((n,) + own.shape, own.dtype),
-        in_specs=[vmem],
-        out_specs=vmem,
-        scratch_shapes=[
-            pltpu.SemaphoreType.DMA,
-            pltpu.SemaphoreType.DMA((2, count - 1, slots)),
-            pltpu.SemaphoreType.DMA((2, count - 1, slots)),
-            pltpu.SemaphoreType.DMA((n // 2,)),
-            pltpu.SemaphoreType.DMA((n // 2,)),
-        ],
-        compiler_params=pltpu.CompilerParams(
-            vmem_limit_bytes=VMEM_LIMIT, collective_id=collective_id, has_side_effects=True
-        ),
-        cost_estimate=pl.CostEstimate(
-            flops=0, bytes_accessed=16 * 1024 * 1024, transcendentals=0
-        ),
-        name=f"gather_over_ctx_{collective_id}",
-    )(own)
-    return gathered.reshape((-1,) + own.shape[1:])
 
 
 CHUNK = 32
@@ -712,8 +655,8 @@
 
 def middle_kernel(
     n, ob, tokens, cot, gain, w_out, w_gate, w_up, w_down,
-    tt, d_out, f_out, act_out, dg_out, du_out,
-    own, up, wo, wg, wu, wd, h2, dfs, d_acc, f_acc,
+    tt, d_out, f_out, act_out, dg_out, du_out, h_out, df_out,
+    own, up, wo, wg, wu, wd, d_acc, f_acc,
     w_sems, up_send, up_land, down_send, back_send, down_land,
 ):
     me = lax.axis_index("tp")
@@ -848,10 +791,7 @@
                 jnp.float32
             )
             scale = lax.rsqrt(jnp.mean(middle * middle, axis=-1, keepdims=True) + EPSILON)
-            slot = lax.rem(lax.div(c_norm, 4), 2)
-            h2[slot, pl.ds(pl.multiple_of(lax.rem(c_norm, 4) * CHUNK, CHUNK), CHUNK), :] = (
-                middle * scale * gain[...]
-            ).astype(jnp.bfloat16)
+            h_out[rows, :] = (middle * scale * gain[...]).astype(jnp.bfloat16)
 
     def project(b):
         rows = pl.ds(pl.multiple_of(b * BLOCK, BLOCK), BLOCK)
@@ -862,13 +802,12 @@
 
     def feed(b, i):
         rows = pl.ds(pl.multiple_of(b * BLOCK, BLOCK), BLOCK)
-        slot = lax.rem(b, 2)
         first, last = cuts[i], cuts[i + 1]
         if i == 0:
-            dfs[...] = (RESIDUAL_SCALE * cot[rows, :].astype(jnp.float32)).astype(jnp.bfloat16)
-        gate = dot_nt(h2[slot], wg[first:last, :])
-        upper = dot_nt(h2[slot], wu[first:last, :])
-        d_act = dot_nt(dfs[...], wd[first:last, :])
+            df_out[rows, :] = (RESIDUAL_SCALE * cot[rows, :].astype(jnp.float32)).astype(jnp.bfloat16)
+        gate = dot_nt(h_out[rows, :], wg[first:last, :])
+        upper = dot_nt(h_out[rows, :], wu[first:last, :])
+        d_act = dot_nt(df_out[rows, :], wd[first:last, :])
         sig = jax.nn.sigmoid(gate)
         silu = gate * sig
         act = (silu * upper).astype(jnp.bfloat16)
@@ -939,7 +878,7 @@
     anywhere = pl.BlockSpec(memory_space=pl.ANY)
     half = jnp.bfloat16
     dma = pltpu.SemaphoreType.DMA
-    attn, d_part, f_part, act, dg, du = pl.pallas_call(
+    attn, *rest = pl.pallas_call(
         functools.partial(middle_kernel, n),
         out_shape=(
             jax.ShapeDtypeStruct((chunks, CHUNK, width), half),
@@ -948,9 +887,11 @@
             jax.ShapeDtypeStruct((rows, hidden), half),
             jax.ShapeDtypeStruct((rows, hidden), half),
             jax.ShapeDtypeStruct((rows, hidden), half),
+            jax.ShapeDtypeStruct((rows, width), half),
+            jax.ShapeDtypeStruct((rows, width), half),
         ),
         in_specs=[vmem] * 4 + [anywhere] * 4,
-        out_specs=(vmem,) * 6,
+        out_specs=(vmem,) * 8,
         scratch_shapes=[
             pltpu.VMEM((chunks, CHUNK, width), half),
             pltpu.VMEM((chunks, CHUNK, width), half),
@@ -958,8 +899,6 @@
             pltpu.VMEM(w_gate.shape, half),
             pltpu.VMEM(w_up.shape, half),
             pltpu.VMEM(w_down.shape, half),
-            pltpu.VMEM((2, BLOCK, width), half),
-            pltpu.VMEM((BLOCK, width), half),
             pltpu.VMEM((BLOCK, width), jnp.float32),
             pltpu.VMEM((BLOCK, width), jnp.float32),
             dma((4,)),
@@ -979,75 +918,299 @@
         ),
         name=f"middle_layer_{collective_id}",
     )(ob, tokens, cot, gain.reshape(1, -1), w_out, w_gate, w_up, w_down)
-    return attn.reshape(rows, width), d_part, f_part, act, dg, du
-
-
-def dot_plain(left_op, right_op):
-    return jnp.dot(left_op, right_op, preferred_element_type=jnp.float32)
-
-
-def dot_rows(left_op, right_op):
-    return lax.dot_general(
-        left_op, right_op, (((0,), (0,)), ((), ())), preferred_element_type=jnp.float32
-    )
-
-
-def dot_cols(left_op, right_op):
-    return lax.dot_general(
-        left_op, right_op, (((1,), (1,)), ((), ())), preferred_element_type=jnp.float32
-    )
-
-
-def rms_scale(values):
+    return attn.reshape(rows, width), *rest
+
+
+def norm_scale(values):
     return lax.rsqrt(jnp.mean(values * values, axis=-1, keepdims=True) + EPSILON)
 
 
-def rms_back(incoming, values, inv_rms, gain_vec):
+def norm_back(incoming, values, inv_rms, gain_vec):
     weighted = incoming * gain_vec
-    d_values = inv_rms * weighted - values * inv_rms**3 * jnp.mean(
-        weighted * values, axis=-1, keepdims=True
-    )
-    return (d_values, jnp.sum(incoming * values * inv_rms, axis=0))
-
-
-def token_places(block_map, doc_lengths, per_device, devices):
-    all_rows = per_device * devices
-    half_block = per_device // 2
-    token_rows = jnp.arange(all_rows, dtype=jnp.int32)
-    device_of = token_rows // per_device
-    within = token_rows % per_device
-    wanted = device_of * 2 + within // half_block
-    select = wanted[:, None] == jnp.arange(2 * devices, dtype=jnp.int32)[None, :]
-    blocks = jnp.sum(jnp.where(select, block_map.reshape(-1)[None, :], 0), axis=1)
-    places = blocks * half_block + within % half_block
-    ends = jnp.cumsum(doc_lengths)
-    segment = jnp.sum((places[:, None] >= ends[None, :]).astype(jnp.int32), axis=1)
-    starts = ends - doc_lengths
-    picked = segment[:, None] == jnp.arange(doc_lengths.shape[0], dtype=jnp.int32)[None, :]
-    begins = jnp.sum(jnp.where(picked, starts[None, :], 0), axis=1)
-    return (places, segment, places - begins)
-
-
-def tables(inside):
-    half_width = ROPE // 2
-    frequency = ROPE_BASE ** (-2.0 * jnp.arange(half_width, dtype=jnp.float32) / ROPE)
-    angles = inside.astype(jnp.float32)[:, None] * frequency[None, :]
-    cosine_table = jnp.concatenate([jnp.cos(angles), jnp.cos(angles)], axis=1)
-    sine_table = jnp.concatenate([jnp.sin(angles), jnp.sin(angles)], axis=1)
-    return (cosine_table, sine_table)
-
-
-def rotate(values, cosine_table, sine_table):
-    half_width = values.shape[-1] // 2
-    turned = jnp.concatenate([-values[..., half_width:], values[..., :half_width]], axis=-1)
-    return values * cosine_table + turned * sine_table
-
-
-def rotate_back(incoming, cosine_table, sine_table):
-    half_width = incoming.shape[-1] // 2
-    shifted = incoming * sine_table
-    turned = jnp.concatenate([shifted[..., half_width:], -shifted[..., :half_width]], axis=-1)
-    return incoming * cosine_table + turned
+    mean = jnp.mean(weighted * values, axis=-1, keepdims=True)
+    d_values = inv_rms * weighted - values * (inv_rms * inv_rms * inv_rms) * mean
+    return d_values, jnp.sum(incoming * values * inv_rms, axis=0, keepdims=True)
+
+
+def rope_tile(tile, cos, sin, lane):
+    left = pltpu.roll(tile, HEAD - ROPE // 2, 1)
+    right = pltpu.roll(tile, ROPE // 2, 1)
+    swapped = jnp.where(lane < ROPE // 2, -left, right)
+    return jnp.where(lane < ROPE, tile * cos + swapped * sin, 0.0)
+
+
+def rope_tile_back(tile, cos, sin, lane):
+    shifted = tile * sin
+    left = pltpu.roll(shifted, HEAD - ROPE // 2, 1)
+    right = pltpu.roll(shifted, ROPE // 2, 1)
+    swapped = jnp.where(lane < ROPE // 2, left, -right)
+    return jnp.where(lane < ROPE, tile * cos + swapped, 0.0)
+
+
+def second_norm_kernel(
+    d_sum, attn, tokens, cot, gain, w_out, d_middle, d_attn, d_heads, d_gain
+):
+    middle = tokens[...].astype(jnp.float32) + RESIDUAL_SCALE * attn[...].astype(jnp.float32)
+    d_norm, gain_terms = norm_back(
+        d_sum[...].astype(jnp.float32), middle, norm_scale(middle), gain[...]
+    )
+    total = cot[...].astype(jnp.float32) + d_norm
+    d_middle[...] = total
+    scaled = (RESIDUAL_SCALE * total).astype(jnp.bfloat16)
+    d_attn[...] = scaled
+    d_heads[...] = dot_nn(scaled, w_out[...]).astype(jnp.bfloat16)
+
+    @pl.when(pl.program_id(0) == 0)
+    def _():
+        d_gain[...] = jnp.zeros(d_gain.shape, jnp.float32)
+
+    d_gain[...] += gain_terms
+
+
+def second_norm_back(d_sum, attn, tokens, cot, gain, w_out):
+    rows, width = tokens.shape
+    block = rows // 4
+    head_width = w_out.shape[1]
+    whole = lambda shape: pl.BlockSpec(shape, lambda i: (0, 0))
+    tile = lambda columns: pl.BlockSpec((block, columns), lambda i: (i, 0))
+    return pl.pallas_call(
+        second_norm_kernel,
+        grid=(rows // block,),
+        out_shape=(
+            jax.ShapeDtypeStruct((rows, width), jnp.float32),
+            jax.ShapeDtypeStruct((rows, width), jnp.bfloat16),
+            jax.ShapeDtypeStruct((rows, head_width), jnp.bfloat16),
+            jax.ShapeDtypeStruct((1, width), jnp.float32),
+        ),
+        in_specs=[tile(width)] * 4 + [whole((1, width)), whole((width, head_width))],
+        out_specs=(tile(width), tile(width), tile(head_width), whole((1, width))),
+        compiler_params=pltpu.CompilerParams(vmem_limit_bytes=VMEM_LIMIT),
+        cost_estimate=pl.CostEstimate(
+            flops=2 * rows * width * head_width,
+            bytes_accessed=24 * 1024 * 1024,
+            transcendentals=rows,
+        ),
+        name="second_norm_back",
+    )(d_sum, attn, tokens, cot, gain.reshape(1, -1), w_out)
+
+
+def first_norm_kernel(
+    d_tp, q_pre, lat_raw, tokens, d_middle, gain_in, gain_q, gain_kv, w_qa, w_kva, cos, sin,
+    normed, d_q, d_kv, grad_in, g_in, g_q, g_kv,
+):
+    rank = q_pre.shape[1]
+    block = tokens.shape[0]
+    lane = lax.broadcasted_iota(jnp.int32, (block, HEAD), 1)
+
+    @pl.when(pl.program_id(0) == 0)
+    def _():
+        for ref in (g_in, g_q, g_kv):
+            ref[...] = jnp.zeros(ref.shape, jnp.float32)
+
+    pre = q_pre[...]
+    d_pre, terms = norm_back(d_tp[:, :rank].astype(jnp.float32), pre, norm_scale(pre), gain_q[...])
+    g_q[...] += terms
+    d_low = d_pre.astype(jnp.bfloat16)
+    d_q[...] = d_low
+    raw = lat_raw[...]
+    d_raw, terms = norm_back(
+        d_tp[:, rank : rank + KVR].astype(jnp.float32), raw, norm_scale(raw), gain_kv[...]
+    )
+    g_kv[...] += terms
+    rope = rope_tile_back(
+        d_tp[:, rank + KVR : rank + KVR + HEAD].astype(jnp.float32), cos[...], sin[...], lane
+    )
+    d_raw = d_raw.astype(jnp.bfloat16)
+    d_rope = rope[:, :ROPE].astype(jnp.bfloat16)
+    d_kv[:, :KVR] = d_raw
+    d_kv[:, KVR:] = d_rope
+    d_normed = dot_nt(d_low, w_qa[...])
+    d_normed = d_normed + dot_nn(d_raw, w_kva[:KVR, :]) + dot_nn(d_rope, w_kva[KVR:, :])
+    values = tokens[...].astype(jnp.float32)
+    scale = norm_scale(values)
+    normed[...] = (values * scale * gain_in[...]).astype(jnp.bfloat16)
+    d_values, terms = norm_back(d_normed, values, scale, gain_in[...])
+    g_in[...] += terms
+    grad_in[...] = d_middle[...] + d_values
+
+
+def first_norm_back(
+    d_tp, q_pre, lat_raw, tokens, d_middle, gain_in, gain_q, gain_kv, w_qa, w_kva, cos, sin
+):
+    rows, width = tokens.shape
+    block = rows // 4
+    rank = q_pre.shape[1]
+    whole = lambda array: pl.BlockSpec(array.shape, lambda i: (0, 0))
+    tile = lambda columns: pl.BlockSpec((block, columns), lambda i: (i, 0))
+    gains = [g.reshape(1, -1) for g in (gain_in, gain_q, gain_kv)]
+    wide = jax.ShapeDtypeStruct
+    return pl.pallas_call(
+        first_norm_kernel,
+        grid=(rows // block,),
+        out_shape=(
+            wide((rows, width), jnp.bfloat16),
+            wide((rows, rank), jnp.bfloat16),
+            wide((rows, KVR + ROPE), jnp.bfloat16),
+            wide((rows, width), jnp.float32),
+            wide((1, width), jnp.float32),
+            wide((1, rank), jnp.float32),
+            wide((1, KVR), jnp.float32),
+        ),
+        in_specs=[tile(d_tp.shape[1]), tile(rank), tile(KVR), tile(width), tile(width)]
+        + [whole(g) for g in gains]
+        + [whole(w_qa), whole(w_kva), tile(HEAD), tile(HEAD)],
+        out_specs=(
+            tile(width),
+            tile(rank),
+            tile(KVR + ROPE),
+            tile(width),
+            *[whole(g) for g in gains],
+        ),
+        compiler_params=pltpu.CompilerParams(vmem_limit_bytes=VMEM_LIMIT),
+        cost_estimate=pl.CostEstimate(
+            flops=2 * rows * width * (rank + KVR + ROPE),
+            bytes_accessed=32 * 1024 * 1024,
+            transcendentals=rows,
+        ),
+        name="first_norm_back",
+    )(d_tp, q_pre, lat_raw, tokens, d_middle, *gains, w_qa, w_kva, cos, sin)
+
+
+def head_kernel(
+    n, tokens, gain_in, gain_q, gain_kv, w_qa, w_kva, cos, sin, out, q_latent, q_pre, lat_raw,
+    own, normed, w_rope, local_sem, step_sends, step_lands, core_sends, core_lands,
+):
+    count = n.bit_length() - 1
+    me = lax.axis_index("ctx")
+    rows = own.shape[0]
+    half = rows // 2
+    block = rows // 4
+    barrier = pltpu.get_barrier_semaphore()
+    for bit in range(count):
+        pl.semaphore_signal(barrier, inc=1, device_id={"ctx": me ^ (1 << bit)}, device_id_type=MESH)
+    orders = (tuple(range(1, count)), tuple(range(count - 1, 0, -1)))
+    lane = lax.broadcasted_iota(jnp.int32, (block, HEAD), 1)
+    w_rope[...] = jnp.zeros(w_rope.shape, jnp.bfloat16)
+    w_rope[:ROPE, :] = w_kva[KVR : KVR + ROPE, :]
+
+    def latents(k, carry):
+        at = pl.ds(pl.multiple_of(k * block, block), block)
+        values = tokens[at, :].astype(jnp.float32)
+        normed[at, :] = (values * norm_scale(values) * gain_in[...]).astype(jnp.bfloat16)
+        raw = dot_nt(normed[at, :], w_kva[:KVR, :])
+        lat_raw[at, :] = raw
+        own[at, :KVR] = (raw * norm_scale(raw) * gain_kv[...]).astype(jnp.bfloat16)
+        rope = rope_tile(dot_nt(normed[at, :], w_rope[...]), cos[at, :], sin[at, :], lane)
+        own[at, KVR:] = rope[:, :ROPE].astype(jnp.bfloat16)
+        return carry
+
+    lax.fori_loop(0, 4, latents, 0)
+    pl.semaphore_wait(barrier, count)
+    local = pltpu.make_async_copy(own, out.at[me], local_sem)
+    local.start()
+
+    def chip_copy(part, step, slot, block, first):
+        at = pl.ds(part * half, half)
+        return pltpu.make_async_remote_copy(
+            src_ref=own.at[at, :] if first else out.at[block, at, :],
+            dst_ref=out.at[block, at, :],
+            send_sem=step_sends.at[part, step, slot],
+            recv_sem=step_lands.at[part, step, slot],
+            device_id={"ctx": me ^ (1 << orders[part][step])},
+            device_id_type=MESH,
+        )
+
+    def core_copy(block, slot, first):
+        return pltpu.make_async_remote_copy(
+            src_ref=own if first else out.at[block],
+            dst_ref=out.at[block],
+            send_sem=core_sends.at[slot],
+            recv_sem=core_lands.at[slot],
+            device_id={"ctx": me ^ 1},
+            device_id_type=MESH,
+        )
+
+    def query(k, carry):
+        at = pl.ds(pl.multiple_of(k * block, block), block)
+        pre = dot_nn(normed[at, :], w_qa[...])
+        q_pre[at, :] = pre
+        q_latent[at, :] = (pre * norm_scale(pre) * gain_q[...]).astype(jnp.bfloat16)
+        return carry
+
+    started = []
+    for step in range(count - 1):
+        for part, order in enumerate(orders):
+            for slot in range(1 << step):
+                flips = 0
+                for at in range(step):
+                    flips |= ((slot >> at) & 1) << order[at]
+                copy = chip_copy(part, step, slot, me ^ flips, slot == 0)
+                copy.start()
+                started.append(copy)
+        if step == 0:
+            core_copy(me, 0, True).start()
+        lax.fori_loop(2 * step, min(2 * step + 2, 4) if step < count - 2 else 4, query, 0)
+        for part, order in enumerate(orders):
+            for slot in range(1 << step):
+                chip_copy(part, step, slot, me, slot == 0).wait_recv()
+    for chip in range(1, n // 2):
+        core_copy(me ^ (2 * chip), chip, False).start()
+    for chip in range(n // 2):
+        core_copy(me, chip, chip == 0).wait_recv()
+    for copy in started:
+        copy.wait_send()
+    for chip in range(n // 2):
+        core_copy(me, chip, chip == 0).wait_send()
+    local.wait()
+
+
+def head_layer(n, tokens, gain_in, gain_q, gain_kv, w_qa, w_kva, cos, sin, collective_id):
+    rows, width = tokens.shape
+    rank = w_qa.shape[1]
+    count = n.bit_length() - 1
+    vmem = pl.BlockSpec(memory_space=pltpu.VMEM)
+    slots = max(n // 4, 1)
+    dma = pltpu.SemaphoreType.DMA
+    gathered, q_latent, q_pre, lat_raw = pl.pallas_call(
+        functools.partial(head_kernel, n),
+        out_shape=(
+            jax.ShapeDtypeStruct((n, rows, KVR + ROPE), jnp.bfloat16),
+            jax.ShapeDtypeStruct((rows, rank), jnp.bfloat16),
+            jax.ShapeDtypeStruct((rows, rank), jnp.float32),
+            jax.ShapeDtypeStruct((rows, KVR), jnp.float32),
+        ),
+        in_specs=[vmem] * 8,
+        out_specs=(vmem,) * 4,
+        scratch_shapes=[
+            pltpu.VMEM((rows, KVR + ROPE), jnp.bfloat16),
+            pltpu.VMEM((rows, width), jnp.bfloat16),
+            pltpu.VMEM((HEAD, width), jnp.bfloat16),
+            dma,
+            dma((2, count - 1, slots)),
+            dma((2, count - 1, slots)),
+            dma((n // 2,)),
+            dma((n // 2,)),
+        ],
+        compiler_params=pltpu.CompilerParams(
+            vmem_limit_bytes=VMEM_LIMIT, collective_id=collective_id, has_side_effects=True
+        ),
+        cost_estimate=pl.CostEstimate(
+            flops=2 * rows * width * (rank + KVR + ROPE),
+            bytes_accessed=24 * 1024 * 1024,
+            transcendentals=rows,
+        ),
+        name=f"head_layer_{collective_id}",
+    )(
+        tokens,
+        gain_in.reshape(1, -1),
+        gain_q.reshape(1, -1),
+        gain_kv.reshape(1, -1),
+        w_qa,
+        w_kva,
+        cos,
+        sin,
+    )
+    return gathered.reshape(n * rows, -1), q_latent, q_pre, lat_raw
 
 
 def wide_tables(inside):
@@ -1091,69 +1254,53 @@
     began = jnp.max(
         jnp.where(starts[None, :] <= query_place[:, None], starts[None, :], 0), axis=1
     )
-    cosine_wide, sine_wide = wide_tables(query_place - began)
-    cosine_table, sine_table = cosine_wide[:, :ROPE], sine_wide[:, :ROPE]
-    head_count = w_qb.shape[1] // (NOPE + ROPE)
-    tokens_f = tokens_in.astype(jnp.float32)
-    scale_in = rms_scale(tokens_f)
-    normed_in = (tokens_f * scale_in * gain_in).astype(jnp.bfloat16)
-    kv_input = dot_plain(normed_in, w_kva)
-    latent_raw = kv_input[:, :KVR]
-    scale_kv = rms_scale(latent_raw)
-    latent = (latent_raw * scale_kv * gain_kv).astype(jnp.bfloat16)
-    key_rope = rotate(kv_input[:, KVR:], cosine_table, sine_table).astype(jnp.bfloat16)
-    latents = gather_over_ctx(devices, jnp.concatenate([latent, key_rope], axis=1), 0)
-    q_latent_pre = dot_plain(normed_in, w_qa)
-    scale_q = rms_scale(q_latent_pre)
-    q_latent = (q_latent_pre * scale_q * gain_q).astype(jnp.bfloat16)
+    cosine, sine = wide_tables(query_place - began)
+    latents, q_latent, q_latent_pre, latent_raw = head_layer(
+        devices, tokens_in, gain_in, gain_q, gain_kv, w_qa, w_kva.T, cosine, sine, 0
+    )
     queries, attn_f, heads_out, log_totals = attention_forward(
-        meta, q_latent, w_qb.T, latents, w_kvb, cosine_wide, sine_wide, half_rows, seqs
-    )
-    attention, d_part, feed_part, activation, d_gate, d_up = middle_layer(
+        meta, q_latent, w_qb.T, latents, w_kvb, cosine, sine, half_rows, seqs
+    )
+    attention, d_part, feed_part, activation, d_gate, d_up, normed_mid, d_feed = middle_layer(
         lax.axis_size("tp"), heads_out, tokens_in, cotangent, gain_mid, w_out, w_gate.T, w_up.T,
         w_down.T, 5,
     )
-    middle = tokens_f + RESIDUAL_SCALE * attention.astype(jnp.float32)
-    scale_mid = rms_scale(middle)
-    normed_mid = (middle * scale_mid * gain_mid).astype(jnp.bfloat16)
-    cotangent_f = cotangent.astype(jnp.float32)
-    d_feed = (RESIDUAL_SCALE * cotangent_f).astype(jnp.bfloat16)
     d_normed_mid = lax.psum(d_part, "tp")
     gw_gate, gw_up, gw_down = scatter_over_ctx(
         devices,
         [
-            Scatter(devices, left=normed_mid.T, right=d_gate),
-            Scatter(devices, left=normed_mid.T, right=d_up),
-            Scatter(devices, left=d_feed.T, right=activation),
+            Scatter(devices, left=normed_mid, right=d_gate),
+            Scatter(devices, left=normed_mid, right=d_up),
+            Scatter(devices, left=d_feed, right=activation),
         ],
         1,
     )
     d_normed_mid, feed_part, gw_gate, gw_up, gw_down = lax.optimization_barrier(
         (d_normed_mid, feed_part, gw_gate, gw_up, gw_down)
     )
-    d_normed_mid = d_normed_mid.astype(jnp.float32)
     feed_own = lax.psum_scatter(feed_part, "tp", scatter_dimension=0, tiled=True)
     own_rows = feed_own.shape[0]
-    middle_own = lax.dynamic_slice_in_dim(middle, lax.axis_index("tp") * own_rows, own_rows, 0)
+    own_at = lax.axis_index("tp") * own_rows
+    tokens_own = lax.dynamic_slice_in_dim(tokens_in, own_at, own_rows, 0).astype(jnp.float32)
+    attention_own = lax.dynamic_slice_in_dim(attention, own_at, own_rows, 0).astype(jnp.float32)
+    middle_own = tokens_own + RESIDUAL_SCALE * attention_own
     out_own = (middle_own + RESIDUAL_SCALE * feed_own.astype(jnp.float32)).astype(jnp.bfloat16)
-    d_middle_norm, d_gain_mid = rms_back(d_normed_mid, middle, scale_mid, gain_mid)
-    d_middle = cotangent_f + d_middle_norm
-    d_attention = (RESIDUAL_SCALE * d_middle).astype(jnp.bfloat16)
-    d_heads = dot_plain(d_attention, w_out).astype(jnp.bfloat16)
+    d_middle, d_attention, d_heads, d_gain_mid = second_norm_back(
+        d_normed_mid, attention, tokens_in, cotangent, gain_mid, w_out
+    )
     d_query_pre, d_latents, gw_kvb = attention_backward(
-        meta, queries, log_totals, attn_f, d_heads, latents, w_kvb, cosine_wide, sine_wide,
-        half_rows, seqs,
+        meta, queries, log_totals, attn_f, d_heads, latents, w_kvb, cosine, sine, half_rows, seqs
     )
     (d_latent_part,) = scatter_over_ctx(devices, [Scatter(devices, given=d_latents)], 2)
-    d_q_latent = dot_cols(d_query_pre, w_qb).astype(jnp.bfloat16)
+    d_q_latent = dot_nt(d_query_pre, w_qb).astype(jnp.bfloat16)
     before_tp = jnp.concatenate([d_q_latent, d_latent_part.astype(jnp.bfloat16)], axis=1)
     before_tp, out_own = lax.optimization_barrier((before_tp, out_own))
     summed_tp = lax.psum(before_tp, "tp")
     gw_out, gw_qb, gw_kvb = scatter_over_ctx(
         devices,
         [
-            Scatter(devices, left=d_attention.T, right=heads_out),
-            Scatter(devices, left=q_latent.T, right=d_query_pre),
+            Scatter(devices, left=d_attention, right=heads_out),
+            Scatter(devices, left=q_latent, right=d_query_pre),
             Scatter(devices, given=gw_kvb),
         ],
         3,
@@ -1162,38 +1309,28 @@
         (summed_tp, out_own, gw_out, gw_qb, gw_kvb)
     )
     out = lax.all_gather(out_own, "tp", axis=0, tiled=True)
-    summed_tp = summed_tp.astype(jnp.float32)
-    q_rank = w_qa.shape[1]
-    d_q_latent = summed_tp[:, :q_rank]
-    d_latent = summed_tp[:, q_rank : q_rank + KVR]
-    d_rope_sum = summed_tp[:, q_rank + KVR :]
-    d_q_pre, d_gain_q = rms_back(d_q_latent, q_latent_pre, scale_q, gain_q)
-    d_q_low = d_q_pre.astype(jnp.bfloat16)
-    d_latent_raw, d_gain_kv = rms_back(d_latent, latent_raw, scale_kv, gain_kv)
-    d_kv_input = jnp.concatenate(
-        [d_latent_raw, rotate_back(d_rope_sum, cosine_table, sine_table)], axis=-1
-    ).astype(jnp.bfloat16)
-    d_normed_in = dot_cols(d_q_low, w_qa) + dot_cols(d_kv_input, w_kva)
-    d_tokens_norm, d_gain_in = rms_back(d_normed_in, tokens_f, scale_in, gain_in)
-    grad_in = d_middle + d_tokens_norm
-    gains = jnp.concatenate(
-        [g.reshape(devices, -1) for g in (d_gain_in, d_gain_mid, d_gain_q, d_gain_kv)], axis=1
-    )
+    lanes = jnp.pad(summed_tp, ((0, 0), (0, -summed_tp.shape[1] % HEAD)))
+    normed_in, d_q_low, d_kv_input, grad_in, d_gain_in, d_gain_q, d_gain_kv = first_norm_back(
+        lanes, q_latent_pre, latent_raw, tokens_in, d_middle, gain_in, gain_q, gain_kv, w_qa,
+        w_kva.T, cosine, sine,
+    )
+    gain_grads = (d_gain_in, d_gain_mid, d_gain_q, d_gain_kv)
+    gains = jnp.concatenate([g.reshape(devices, -1) for g in gain_grads], axis=1)
     lines = -(-gains.shape[1] // (32 * HEAD)) * 32
     gains = jnp.pad(gains, ((0, 0), (0, lines * HEAD - gains.shape[1])))
     gw_qa, gw_kva, gains = scatter_over_ctx(
         devices,
         [
-            Scatter(devices, left=normed_in.T, right=d_q_low),
-            Scatter(devices, left=normed_in.T, right=d_kv_input),
+            Scatter(devices, left=normed_in, right=d_q_low),
+            Scatter(devices, left=normed_in, right=d_kv_input),
             Scatter(devices, given=gains.astype(jnp.bfloat16).reshape(devices * lines, HEAD)),
         ],
         4,
     )
     gains = gains.reshape(-1)
     ends = [0]
-    for whole in (d_gain_in, d_gain_mid, d_gain_q, d_gain_kv):
-        ends.append(ends[-1] + whole.shape[0] // devices)
+    for whole in gain_grads:
+        ends.append(ends[-1] + whole.size // devices)
     own_gains = [gains[first:last] for first, last in zip(ends, ends[1:])]
     return (
         out,

time: 642 us -> 579 us (0.902)
  other arithmetic: 59.2 us -> 11.2 us
  Pallas kernels: 468 us -> 498 us
  local copies, waits for them, and re-layouts: 55.7 us -> 27.7 us
  matrix products: 20.6 us -> 2.2 us
    pallas_call x1 -> x3, Pallas kernels: 24.4 us -> 57 us  [the longest x1 30.5 us: head_layer(): pl.pallas_call(functools.partial(head_kernel, n), out_shape=(jax.ShapeDty...]
    unnamed x85 -> x29, local copies, waits for them, and re-layouts: 35.5 us -> 15.6 us
    transpose x4 -> x0, other arithmetic: 18.5 us -> none  [the longest x1 7.87 us: on_device(): gw_qa, gw_kva, gains = scatter_over_ctx(devices, [Scatter(devices, left=n...]
    dot_general x6 -> x1, matrix products: 20.6 us -> 2.2 us  [dot_nt(): lax.dot_general(left_op, right_op, (((1,), (1,)), ((), ())), preferred_el...]
    reduce_sum x6 -> x0, other arithmetic: 16 us -> none  [the longest x3 10.2 us: rms_scale(): jnp.mean(values * values, axis=-1, keepdims=True) + EPSILON]
    pallas_call x4, Pallas kernels: 218 us -> 228 us  [scatter_over_ctx(): pl.pallas_call(functools.partial(scatter_kernel, n, items), out_shape=tup...]
    pallas_call x1, Pallas kernels: 55.4 us -> 46.2 us  [attention_forward(): pl.pallas_call(functools.partial(forward_kernel, blocks, heads, seqs), ou...]
    convert_element_type x6 -> x0, other arithmetic: 8.76 us -> none  [the longest x1 2.68 us: on_device(): d_q_low = d_q_pre.astype(jnp.bfloat16)]
  transfers between devices with their start and end apart: 4 -> 4, of which waited for: 1 -> 1; matrix products, arithmetic and copies ran while one was open for 13% -> 3% of each run, Pallas kernels for 43% -> 53%
where the time goes in v5:
time: 579 us; the launch traced here: 574 us
  Pallas kernels  498 us (86%)
  local copies, waits for them, and re-layouts  27.7 us (5%)
  waiting for transfers between devices  20.3 us (4%)
  between operations  14.4 us (2%)
  other arithmetic  11.2 us (2%)
    pallas_call x4, Pallas kernels, scatter_over_ctx(): pl.pallas_call(functools.partial(scatter_kernel, n, items), out_shape=tup...  228 us
    pallas_call x1, Pallas kernels, middle_layer(): pl.pallas_call(functools.partial(middle_kernel, n), out_shape=(jax.ShapeD...  117 us
    pallas_call x1, Pallas kernels, attention_backward(): pl.pallas_call(functools.partial(backward_kernel, blocks, heads, seqs), o...  49.8 us
    pallas_call x1, Pallas kernels, attention_forward(): pl.pallas_call(functools.partial(forward_kernel, blocks, heads, seqs), ou...  46.2 us
    pallas_call x1, Pallas kernels, head_layer(): pl.pallas_call(functools.partial(head_kernel, n), out_shape=(jax.ShapeDty...  30.5 us
    psum x1, waiting for transfers between devices, on_device(): summed_tp = lax.psum(before_tp, 'tp')  20.2 us
    unnamed x29, local copies, waits for them, and re-layouts  15.6 us
    pallas_call x1, Pallas kernels, first_norm_back(): pl.pallas_call(first_norm_kernel, grid=(rows // block,), out_shape=(wide(...  14.8 us
  transfers between devices with their start and end apart: 4, of which 1 were waited for; matrix products, arithmetic and copies ran while one was open for 3% of the time, Pallas kernels for 53%

profile of v5, /device:TPU:0, one launch (start us, length us, event | category | flops | bytes accessed | tf_op | source)
XLA Modules:
  0.0 573.6 jit_solution(3695022402267411620)
XLA Ops:
  10.5 1.3 reshape.157.gain_q
  12.5 1.3 reshape.156.gain_in
  13.8 1.3 reshape.160.gain
  15.1 1.8 fusion.1
  16.9 30.5 %head_layer_0.1 = (bf16[8,512,288]{2,1,0:T(8,128)(2,1)}, bf16[512,768]{1,0:T(8,128)(2,1)}, f32[512,768]{1,0:T(8,128)}, f32[512,256]{1,0:T(8,128)}) custom-call(bf16[512,2560]{1,0:T(8,128)(2,1)} %tokens.7, f32[1,2560]{1,0:T(1,128)} %reshape.156.gain_in, f32[1,768]{1,0:T(1,128)} %reshape.157.gain_q, f32[1,256]{1,0:T(1,128)} %bitcast.23, ...), custom_call_target="tpu_custom_call" | custom-call | flops 2768240640 | bytes 25165824 | tf_op jit(solution)/shard_map/head_layer_0/pallas_call | solution.py:1174
  47.4 46.2 %attention_forward.1 = (bf16[2,10,256,256]{3,2,1,0:T(8,128)(2,1)}, f32[512,640]{1,0:T(8,128)}, bf16[512,640]{1,0:T(8,128)(2,1)}, f32[2,16,256]{2,1,0:T(8,128)}) custom-call(s32[22]{0:T(128)} %pad_add_fusion.meta, bf16[512,768]{1,0:T(8,128)(2,1)} %get-tuple-element.65.cq.refs_2_, bf16[960,768]{1,0:T(8,128)(2,1)} %bitcast.31, bf16[4096,288]{1,0:T(8,128)(2,1)} %bitcast.33, ...), custom_call_target="tpu_custom_call" | custom-call | flops 10737418240 | bytes 16777216 | tf_op jit(solution)/shard_map/attention_forward/pallas_call | solution.py:197
  93.6 116.5 %middle_layer_5.1 = (bf16[16,32,2560]{2,1,0:T(8,128)(2,1)}, bf16[512,2560]{1,0:T(8,128)(2,1)}, bf16[512,2560]{1,0:T(8,128)(2,1)}, bf16[512,1600]{1,0:T(8,128)(2,...) custom-call(bf16[512,640]{1,0:T(8,128)(2,1)} %get-tuple-element.70.o, ...), custom_call_target="tpu_custom_call" | custom-call | flops 26843545600 | bytes 67108864 | tf_op jit(solution)/shard_map/middle_layer_5/pallas_call | solution.py:881
  210.2 124.9 %scatter_over_ctx_1.1 = (f32[320,1600]{1,0:T(8,128)}, f32[320,1600]{1,0:T(8,128)}, f32[320,1600]{1,0:T(8,128)}) custom-call(bf16[512,2560]{1,0:T(8,128)(2,1)} %get-tuple-element.73.refs_0_, bf16[512,2560]{1,0:T(8,128)(2,1)} %get-tuple-element.74.refs_1_, bf16[512,1600]{1,0:T(8,128)(2,1)} %get-tuple-element.75.refs_2_, ...), custom_call_target="tpu_custom_call" | custom-call | flops 12582912000 | bytes 67108864 | tf_op jit(solution)/shard_map/scatter_over_ctx_1/pallas_call | solution.py:633
  335.2 11.6 %second_norm_back.1 = (f32[512,2560]{1,0:T(8,128)}, bf16[512,2560]{1,0:T(8,128)(2,1)}, bf16[512,640]{1,0:T(8,128)(2,1)}, f32[1,2560]{1,0:T(1,128)}) custom-call(bf16[512,2560]{1,0:T(8,128)(2,1)} %all-reduce.5.cloned.1.call-done.d_sum, bf16[512,2560]{1,0:T(8,128)(2,1)} %bitcast.17, bf16[512,2560]{1,0:T(8,128)(2,1)} %tokens.7, bf16[512,2560]{1,0:T(8,128)(2,1)} %cot.3, ...), custom_call_target="tpu_custom_call" | custom-call | flops 1677721600 | bytes 25165824 | tf_op jit(solution)/shard_map/second_norm_back/pallas_call | solution.py:976
  346.8 49.8 %attention_backward.1 = (bf16[512,960]{1,0:T(8,128)(2,1)}, bf16[4096,288]{1,0:T(8,128)(2,1)}, bf16[256,1280]{1,0:T(8,128)(2,1)}) custom-call(s32[22]{0:T(128)} %pad_add_fusion.meta, bf16[2,10,256,256]{3,2,1,0:T(8,128)(2,1)} %get-tuple-element.67.qx, f32[2,16,256]{2,1,0:T(8,128)} %get-tuple-element.68.u_in, f32[512,640]{1,0:T(8,128)} %get-tuple-element.69.o_in, ...), custom_call_target="tpu_custom_call" | custom-call | flops 21474836480 | bytes 25165824 | tf_op jit(solution)/shard_map/attention_backward/pallas_call | solution.py:380
  396.7 28.7 %scatter_over_ctx_2.1 = f32[512,288]{1,0:T(8,128)} custom-call(bf16[4096,288]{1,0:T(8,128)(2,1)} %get-tuple-element.85.refs_0_), custom_call_target="tpu_custom_call" | custom-call | bytes 67108864 | tf_op jit(solution)/shard_map/scatter_over_ctx_2/pallas_call | solution.py:633
  425.4 1.2 convert_element_type.40
  426.6 2.2 convolution_convert_fusion
  428.8 1.1 pad_maximum_fusion
  429.9 2.6 add_convert_fusion
  432.7 35.9 %scatter_over_ctx_3.1 = (f32[320,640]{1,0:T(8,128)}, f32[96,960]{1,0:T(8,128)}, f32[32,1280]{1,0:T(8,128)}) custom-call(bf16[256,1280]{1,0:T(8,128)(2,1)} %get-tuple-element.89.refs_0_, bf16[512,2560]{1,0:T(8,128)(2,1)} %get-tuple-element.90.refs_1_, bf16[512,768]{1,0:T(8,128)(2,1)} %get-tuple-element.65.cq.refs_2_, ...), custom_call_target="tpu_custom_call" | custom-call | flops 2432696320 | bytes 67108864 | tf_op jit(solution)/shard_map/scatter_over_ctx_3/pallas_call | solution.py:633
  468.6 20.2 %all-reduce.7.cloned.1.call-done = bf16[512,1056]{1,0:T(8,128)(2,1)} async-done(((bf16[512,1056]{1,0:T(8,128)(2,1)}), bf16[512,1056]{1,0:T(8,128)(2,1)}) %all-reduce.7.cloned.1.call-update) | async-done | bytes 1081360 | tf_op jit(solution)/shard_map/psum | solution.py:1298
  489.0 2.4 pad.9.d_tp
  491.4 14.8 %first_norm_back.1 = (bf16[512,2560]{1,0:T(8,128)(2,1)}, bf16[512,768]{1,0:T(8,128)(2,1)}, bf16[512,288]{1,0:T(8,128)(2,1)}, f32[512,2560]{1,0:T(8,128)}, f32[1,...) custom-call(bf16[512,1152]{1,0:T(8,128)(2,1)} %pad.9.d_tp, f32[512,768]{1,0:T(8,128)} %get-tuple-element.96.q_pre, ...), custom_call_target="tpu_custom_call" | custom-call | flops 2768240640 | bytes 33554432 | tf_op jit(solution)/shard_map/first_norm_back/pallas_call | solution.py:1047
  509.3 38.5 %scatter_over_ctx_4.1 = (f32[320,768]{1,0:T(8,128)}, f32[320,288]{1,0:T(8,128)}, f32[32,128]{1,0:T(8,128)}) custom-call(bf16[256,128]{1,0:T(8,128)(2,1)} %reshape.166.refs_0_, bf16[512,2560]{1,0:T(8,128)(2,1)} %get-tuple-element.104.refs_1_, bf16[512,768]{1,0:T(8,128)(2,1)} %get-tuple-element.105.refs_2_, bf16[512,288]{1,0:T(8,128)(2,1)} %get-tuple-element.106.refs_3_), custom_call_target="tpu_custom_call" | custom-call | flops 2768240640 | bytes 67108864 | tf_op jit(solution)/shard_map/scatter_over_ctx_4/pallas_call | solution.py:633
  547.9 1.3 slice.18
  549.1 1.2 slice.17
  550.3 2.0 copy.35
  552.3 1.4 fusion.12
  553.8 3.5 copy.47
  557.3 0.9 copy.48
  559.6 0.9 copy.51
  560.5 1.3 copy.52
  561.9 1.0 copy-done.1
  562.9 1.3 copy.53
  564.2 1.0 copy-done
  565.3 1.3 copy.54
  (52 shorter events, 8.9 us)
Async XLA Ops:
  7.2 327.9 %all-reduce.5.cloned.1.call-start = ((), (), s32[]{:S(2)}) async-start(), calls=%async_computation.1 | async-start | bytes 5242880 | tf_op jit(solution)/shard_map/psum | solution.py:1268
  210.2 219.8 %reduce-scatter.2.cloned.1.call-start = ((), (), s32[]{:S(2)}) async-start(), calls=%async_computation.2 | async-start | bytes 3276800 | tf_op jit(solution)/shard_map/reduce_scatter | solution.py:1281
  335.2 153.7 %all-reduce.7.cloned.1.call-start = ((), (), s32[]{:S(2)}) async-start(), calls=%async_computation.3 | async-start | bytes 2359296 | tf_op jit(solution)/shard_map/psum | solution.py:1298
  396.7 29.9 %copy-start.8 = (bf16[768,960]{0,1:T(8,128)(2,1)S(1)}, bf16[768,960]{0,1:T(8,128)(2,1)}, u32[]{:S(2)}) copy-start(bf16[768,960]{0,1:T(8,128)(2,1)} %param.19) | copy-start | bytes 4423684
  432.6 121.1 %all-gather.2.cloned.1.call-start = ((), (), s32[]{:S(2)}) async-start(), calls=%async_computation.4 | async-start | bytes 3276800 | tf_op jit(solution)/shard_map/all_gather | solution.py:1311
  432.7 56.2 %copy-start.7 = (f32[1,2560]{1,0:T(1,128)S(1)}, f32[1,2560]{1,0:T(1,128)}, u32[]{:S(2)}) copy-start(f32[1,2560]{1,0:T(1,128)} %get-tuple-element.101) | copy-start | bytes 30724
  553.7 3.5 copy-start.3
  553.7 4.5 copy-start.5
  553.7 5.2 copy-start.6
  557.3 2.4 copy-start.4
  557.3 3.3 copy-start.2
  560.5 2.4 copy-start.1
  562.9 2.4 copy-start
Sparse Core Ops, SparseCore 0:
  210.3 104.3 all-reduce.4
  335.3 52.6 reduce-scatter.1
  432.7 56.0 all-reduce.6
  490.8 54.3 all-gather.1
